TPU v7x, 32 devices: a whole 2x2x4 slice. The times are simulated.
32 devices in a mesh: parts: 2 (over y), clu: 4 (over z), sub: 2 (over x), rep: 2 (over core).
Axes of the slice: x: 2, y: 2, z: 4, core: 2. Of those that a mesh axis runs over, the one named last changes fastest.
Arguments:
- panel_field: bfloat16 [16, 512, 256], P(('parts', 'clu'), 'sub'), parts along dimension 0, may hold values from -6 to 6
- near_row: int32 [416], P(('parts', 'clu', 'rep')), parts along dimension 0, may hold values from 0 to 1
- near_col: int32 [416], P(('parts', 'clu', 'rep')), parts along dimension 0, may hold values from 0 to 7, as said below
- near_block: bfloat16 [416, 512, 512], P(('parts', 'clu', 'rep'), None, 'sub'), parts along dimension 0, may hold values from -0.0625 to 0.0625
- bases: bfloat16 [16, 512, 32], P(('parts', 'clu'), 'sub'), parts along dimension 0, may hold values from -0.25 to 0.25
- far_row: int32 [512], P(('parts', 'clu', 'rep')), parts along dimension 0, may hold values from 0 to 1
- far_col: int32 [512], P(('parts', 'clu', 'rep')), parts along dimension 0, may hold values from 0 to 7, as said below
- coupling: float32 [512, 32, 32], P(('parts', 'clu', 'rep')), parts along dimension 0, may hold values from -1 to 1
Outputs:
- product: float32 [16, 512, 256], P(('parts', 'clu'), 'sub'), parts along dimension 0
There are 2 independent parts, one for each index of `parts`. A program takes and returns all parts, laid end to end along the dimension named above; each array names one. Nothing has to cross between parts.
Inputs may be any that keep to these rules, and one draw needn't show every extreme that they name: Among the 26 near pairs of one device (aligned blocks of near_col) at most 13 have column clusters c with c // 2 equal to one index of clu, and in each such block some index of clu is named by exactly 13 of them. Among the 32 far pairs of one device (aligned blocks of far_col) at most 16 have column clusters c with c // 2 equal to one index of clu, and in each such block some index of clu is named by exactly 16 of them.
All inputs are finite; a program needn't handle non-finite values.
Results may differ from a plain program's by a relative error of at most 0.0015.
Values may be sent and summed in bfloat16 or wider, within the bound.
No kernel may reach another device: no remote copies, remote signals or barrier semaphores. Data moves between devices by JAX's collectives and lax.ppermute only.
A program may use at most 128 MiB of HBM per device.

v0:
```python
import jax
import jax.numpy as jnp
from jax import lax
from jax.sharding import PartitionSpec as P


def slot_plan(columns, owners, limit, local_count):
    target = columns // local_count
    local_ids = columns % local_count
    onehot = (target[:, None] == jnp.arange(owners, dtype=jnp.int32)[None, :]).astype(jnp.int32)
    earlier = jnp.cumsum(onehot, axis=0) - onehot
    slot_rank = jnp.sum(earlier * onehot, axis=1)
    position = target * limit + slot_rank
    placed = (position[:, None] == jnp.arange(owners * limit, dtype=jnp.int32)[None, :]).astype(
        jnp.int32
    )
    request_table = jnp.sum(placed * (local_ids + 1)[:, None], axis=0).reshape(owners, limit)
    return (position, request_table)


def shards(panel_field, near_row, near_col, near_block, bases, far_row, far_col, coupling):
    owners = lax.axis_size("clu")
    local_count = panel_field.shape[0]
    pair_count = near_col.shape[0]
    far_count = far_col.shape[0]
    near_limit = max(2, (2 * pair_count + owners - 1) // owners)
    far_limit = max(2, (2 * far_count + owners - 1) // owners)
    near_position, near_table = slot_plan(near_col, owners, near_limit, local_count)
    far_position, far_table = slot_plan(far_col, owners, far_limit, local_count)
    asked_near, asked_far = (
        lax.all_to_all(near_table, "clu", split_axis=0, concat_axis=0, tiled=True),
        lax.all_to_all(far_table, "clu", split_axis=0, concat_axis=0, tiled=True),
    )
    asked_near = asked_near.reshape(-1)
    asked_far = asked_far.reshape(-1)
    cluster_ids = jnp.arange(1, local_count + 1, dtype=jnp.int32)
    gathered = lax.all_gather(panel_field, "clu", axis=0, tiled=True)
    column_values = jnp.take(gathered, near_col, axis=0)
    own_full = lax.all_gather(panel_field, "sub", axis=1, tiled=True)
    row_values = jnp.take(own_full, near_row, axis=0)
    forward = jnp.einsum(
        "pab,pbk->pak", near_block, column_values, preferred_element_type=jnp.float32
    )
    row_hot = (near_row[:, None] == jnp.arange(local_count, dtype=jnp.int32)[None, :]).astype(
        jnp.float32
    )
    row_terms = jnp.einsum("pc,pak->cak", row_hot, forward, precision=lax.Precision.HIGHEST)
    transposed = jnp.einsum(
        "pab,pak->pbk", near_block, row_values, preferred_element_type=jnp.float32
    ).astype(jnp.bfloat16)
    send_back = (
        jnp.zeros((owners * near_limit,) + transposed.shape[1:], jnp.bfloat16)
        .at[near_position]
        .set(transposed)
    )
    returned = lax.all_to_all(send_back, "clu", split_axis=0, concat_axis=0, tiled=True)
    slot_hot = (asked_near[:, None] == cluster_ids[None, :]).astype(jnp.bfloat16)
    returned_sum = jnp.einsum("qc,qbk->cbk", slot_hot, returned, preferred_element_type=jnp.float32)
    rows_sum = lax.psum_scatter(row_terms, "sub", scatter_dimension=1, tiled=True)
    partial_projection = jnp.einsum(
        "cbr,cbk->crk", bases, panel_field, preferred_element_type=jnp.float32
    )
    projection = lax.psum_scatter(partial_projection, "sub", scatter_dimension=2, tiled=True)
    gathered_far = lax.all_gather(projection, "clu", axis=0, tiled=True)
    far_columns = jnp.take(gathered_far, far_col, axis=0)
    far_rows = jnp.take(projection, far_row, axis=0)
    coupled = jnp.einsum("pab,pbk->pak", coupling, far_columns, precision=lax.Precision.HIGHEST)
    far_hot = (far_row[:, None] == jnp.arange(local_count, dtype=jnp.int32)[None, :]).astype(
        jnp.float32
    )
    coupled_sum = jnp.einsum("pc,pak->cak", far_hot, coupled, precision=lax.Precision.HIGHEST)
    coupled_back = jnp.einsum("pab,pak->pbk", coupling, far_rows, precision=lax.Precision.HIGHEST)
    far_send = (
        jnp.zeros((owners * far_limit,) + coupled_back.shape[1:], jnp.float32)
        .at[far_position]
        .set(coupled_back)
    )
    far_returned = lax.all_to_all(far_send, "clu", split_axis=0, concat_axis=0, tiled=True)
    far_slot_hot = (asked_far[:, None] == cluster_ids[None, :]).astype(jnp.float32)
    far_back_sum = jnp.einsum(
        "qc,qak->cak", far_slot_hot, far_returned, precision=lax.Precision.HIGHEST
    )
    coefficient = lax.all_gather(coupled_sum + far_back_sum, "sub", axis=2, tiled=True)
    far_field = jnp.einsum(
        "cbr,crk->cbk", bases.astype(jnp.float32), coefficient, precision=lax.Precision.HIGHEST
    )
    combined = rows_sum + returned_sum + far_field
    return lax.psum(combined, "rep")


def solution(mesh):
    placed = (
        P(("parts", "clu"), "sub", None),
        P(("parts", "clu", "rep")),
        P(("parts", "clu", "rep")),
        P(("parts", "clu", "rep"), None, "sub"),
        P(("parts", "clu"), "sub", None),
        P(("parts", "clu", "rep")),
        P(("parts", "clu", "rep")),
        P(("parts", "clu", "rep"), None, None),
    )
    return jax.shard_map(
        shards,
        mesh=mesh,
        in_specs=placed,
        out_specs=P(("parts", "clu"), "sub", None),
        check_vma=False,
    )
```

profile of v0, /device:TPU:0, one launch (start us, length us, event | category | flops | bytes accessed | tf_op | source)
XLA Modules:
  0.0 301.6 jit_solution(15878902457074530720)
XLA Ops:
  7.4 1.8 fusion.53
  9.2 0.7 fusion.41
  10.3 0.7 all_to_all.18
  11.0 6.3 %all-to-all-start = ((s32[4,1,13]{2,1,0:T(1,128)}), s32[4,1,13]{2,1,0:T(1,128)S(1)}, u32[]{:S(2)}, u32[]{:S(2)}) async-start(s32[4,1,13]{2,1,0:T(1,128)} %bitcast.2), calls=%async_computation | async-start | bytes 4096 | tf_op jit(solution)/shard_map/all_to_all | solution.py:31
  19.7 0.7 all_to_all.21
  20.4 2.6 reduce-scatter.2.cloned.1.call-done
  23.0 1.3 gather_fusion.3
  24.4 4.6 %all-to-all-start.2 = ((s32[4,1,16]{2,1,0:T(1,128)}), s32[4,1,16]{2,1,0:T(1,128)S(1)}, u32[]{:S(2)}, u32[]{:S(2)}) async-start(s32[4,1,16]{2,1,0:T(1,128)} %bitcast.7), calls=%async_computation.3 | async-start | bytes 4096 | tf_op jit(solution)/shard_map/all_to_all | solution.py:32
  28.9 1.1 convolution_bitcast_fusion.1
  30.0 1.1 broadcast_in_dim.85
  31.1 4.3 %scatter_fusion.1 = f32[64,32,128]{2,1,0:T(8,128)} fusion(f32[64,32,128]{2,1,0:T(8,128)} %broadcast_in_dim.85, s32[32]{0:T(128)S(1)} %get-tuple-element.5, f32[32,32,128]{2,1,0:T(8,128)S(1)} %convolution_bitcast_fusion.1), kind=kCustom, calls=%fused_computation.5 | custom fusion | bytes 1572992 | tf_op jit(solution)/shard_map/scatter | solution.py:76
  35.5 5.1 %all-to-all-start.3 = ((f32[64,32,128]{2,1,0:T(8,128)}), f32[64,32,128]{2,1,0:T(8,128)S(1)}, u32[]{:S(2)}, u32[]{:S(2)}) async-start(f32[64,32,128]{2,1,0:T(8,128)} %scatter_fusion.1), calls=%async_computation.4 | async-start | bytes 2097152 | tf_op jit(solution)/shard_map/all_to_all | solution.py:78
  40.6 7.4 %all_gather.13 = bf16[2,512,256]{2,1,0:T(8,128)(2,1)S(1)} all-gather(bf16[2,256,256]{2,1,0:T(8,128)(2,1)S(1)} %copy-done.2), channel_id=1, replica_groups=mesh['parts'=2,'clu'=4,'sub'=2,'rep'=2] {'sub'}, dimensions={1}, use_global_device_ids=true | all-gather | bytes 786432 | tf_op jit(solution)/shard_map/all_gather | solution.py:39
  48.0 4.4 %gather_fusion.1 = bf16[26,512,256]{2,1,0:T(8,128)(2,1)} fusion(bf16[2,512,256]{2,1,0:T(8,128)(2,1)S(1)} %all_gather.13, s32[1024]{0:T(1024)S(1)} %pad_clamp_fusion.2), kind=kCustom, calls=%fused_computation.1 | custom fusion | bytes 13631592 | tf_op jit(solution)/shard_map/jit(_take)/gather | solution.py:40
  52.4 8.9 %convert_bitcast_fusion = bf16[26,256,256]{1,2,0:T(8,128)(2,1)} fusion(bf16[26,512,256]{2,1,0:T(8,128)(2,1)} %param.11, bf16[26,512,256]{2,1,0:T(8,128)(2,1)} %gather_fusion.1, pred[26]{0:T(512)(128)(4,1)S(1)} %compare_and_fusion.2), kind=kOutput, calls=%fused_computation.12 | convolution fusion | flops 1749942272 | bytes 17039386 | tf_op jit(solution)/shard_map/pab,pak->pbk/dot_general | solution.py:48
  61.3 5.5 %copy.34 = bf16[26,256,256]{2,1,0:T(8,128)(2,1)} copy(bf16[26,256,256]{1,2,0:T(8,128)(2,1)} %convert_bitcast_fusion) | data formatting | bytes 6815744 | tf_op jit(solution)/shard_map/convert_element_type | solution.py:50
  66.8 3.6 %broadcast_in_dim.77 = bf16[52,256,256]{2,1,0:T(8,128)(2,1)} broadcast(bf16[]{:T(256)} %constant.117.clone.1), dimensions={} | broadcast | bytes 6815746 | tf_op jit(solution)/shard_map/broadcast_in_dim | solution.py:52
  70.5 10.9 %scatter_fusion = bf16[52,256,256]{2,1,0:T(8,128)(2,1)} fusion(bf16[52,256,256]{2,1,0:T(8,128)(2,1)} %broadcast_in_dim.77, s32[26]{0:T(128)S(1)} %get-tuple-element.7, bf16[26,256,256]{2,1,0:T(8,128)(2,1)} %copy.34), kind=kCustom, calls=%fused_computation.4 | custom fusion | bytes 10223720 | tf_op jit(solution)/shard_map/scatter | solution.py:54
  81.4 5.5 %all-to-all-start.1 = ((bf16[52,256,256]{2,1,0:T(8,128)(2,1)}), bf16[52,256,256]{2,1,0:T(8,128)(2,1)}, u32[]{:S(2)}, u32[]{:S(2)}) async-start(bf16[52,256,256]{2,1,0:T(8,128)(2,1)} %scatter_fusion), calls=%async_computation.1 | async-start | bytes 13631488 | tf_op jit(solution)/shard_map/all_to_all | solution.py:56
  90.3 0.7 reduce.6
  91.0 60.4 %all-gather.2.cloned.1.call-done = bf16[8,256,256]{2,1,0:T(8,128)(2,1)} async-done(((bf16[2,256,256]{2,1,0:T(8,128)(2,1)}), bf16[8,256,256]{2,1,0:T(8,128)(2,1)}) %all-gather.2.cloned.1.call-update) | async-done | bytes 1048592 | tf_op jit(solution)/shard_map/all_gather | solution.py:37
  151.4 3.8 %gather_fusion = bf16[26,256,256]{2,1,0:T(8,128)(2,1)} fusion(bf16[8,256,256]{2,1,0:T(8,128)(2,1)} %all-gather.2.cloned.1.call-done, s32[1024]{0:T(1024)S(1)} %pad_clamp_fusion.3), kind=kCustom, calls=%fused_computation | custom fusion | bytes 6815848 | tf_op jit(solution)/shard_map/jit(_take)/gather | solution.py:38
  155.2 10.9 %convolution_bitcast_fusion = f32[26,512,256]{1,2,0:T(8,128)} fusion(bf16[26,512,256]{2,1,0:T(8,128)(2,1)} %param.11, bf16[26,256,256]{2,1,0:T(8,128)(2,1)} %gather_fusion, pred[26]{0:T(512)(128)(4,1)S(1)} %compare_and_fusion.3), kind=kOutput, calls=%fused_computation.6 | convolution fusion | flops 1746534400 | bytes 23855130 | tf_op jit(solution)/shard_map/pab,pbk->pak/dot_general | solution.py:41
  166.1 19.9 %copy.31 = f32[26,512,256]{2,0,1:T(8,128)} copy(f32[26,512,256]{1,2,0:T(8,128)} %convolution_bitcast_fusion) | data formatting | bytes 27262976 | tf_op jit(solution)/shard_map/pab,pbk->pak/dot_general | solution.py:41
  186.1 9.9 %fusion.33 = f32[2,512,256]{2,0,1:T(2,128)} fusion(f32[26,512,256]{2,0,1:T(8,128)} %copy.31, s32[26]{0:T(128)S(1)} %copy-done.4), kind=kOutput, calls=%fused_computation.54 | convolution fusion | flops 81788976 | bytes 14680168 | tf_op jit(solution)/shard_map/pc,pak->cak/dot_general | solution.py:47
  196.0 61.5 %all_gather.14 = f32[8,32,128]{2,1,0:T(8,128)S(1)} all-gather(f32[2,32,128]{2,1,0:T(8,128)S(1)} %copy-done.1), channel_id=1, replica_groups=mesh['parts'=2,'clu'=4,'sub'=2,'rep'=2] {'clu'}, dimensions={0}, use_global_device_ids=true | all-gather | bytes 163840 | tf_op jit(solution)/shard_map/all_gather | solution.py:64
  258.1 0.7 convolution_bitcast_fusion.2
  259.4 1.1 convolution_add_fusion
  260.5 4.8 %all_gather.15 = f32[2,32,256]{2,0,1:T(2,128)S(1)} all-gather(f32[2,32,128]{2,0,1:T(2,128)S(1)} %convolution_add_fusion), channel_id=1, replica_groups=mesh['parts'=2,'clu'=4,'sub'=2,'rep'=2] {'sub'}, dimensions={2}, use_global_device_ids=true | all-gather | bytes 98304 | tf_op jit(solution)/shard_map/all_gather | solution.py:83
  266.0 8.3 %fusion.14 = f32[2,256,256]{2,0,1:T(2,128)} fusion(bf16[52,256,256]{2,1,0:T(8,128)(2,1)} %all-to-all-done.1, f32[2,512,256]{2,0,1:T(2,128)} %all-reduce.6.cloned.1.call-done, u32[]{:T(128)S(6)} %multiply.1, f32[2,256,256]{1,0,2:T(2,128)S(1)} %copy.41, s32[52]{0:T(128)S(1)} %eq.121, s32[2]{0:T(128)S(1)} %iota_add_fusion), kind=kOutput, calls=%fused_computation.21 | convolution fusion | flops 13893736 | bytes 8388828 | tf_op jit(solution)/shard_map/qc,qbk->cbk/dot_general | solution.py:58
  274.3 18.3 %all-reduce.4.cloned.1.call-done = f32[2,256,256]{2,0,1:T(2,128)} async-done(((f32[2,256,256]{2,0,1:T(2,128)}), f32[2,256,256]{2,0,1:T(2,128)}) %all-reduce.4.cloned.1.call-update) | async-done | bytes 524304 | tf_op jit(solution)/shard_map/psum | solution.py:88
  292.6 1.9 copy.42
  (62 shorter events, 7.5 us)
Async XLA Ops:
  7.4 21.6 %copy-start = (f32[32,32,32]{2,1,0:T(8,128)S(1)}, f32[32,32,32]{2,1,0:T(8,128)}, u32[]{:S(2)}) copy-start(f32[32,32,32]{2,1,0:T(8,128)} %param.15) | copy-start | bytes 393220
  7.4 33.2 %copy-start.2 = (bf16[2,256,256]{2,1,0:T(8,128)(2,1)S(1)}, bf16[2,256,256]{2,1,0:T(8,128)(2,1)}, u32[]{:S(2)}) copy-start(bf16[2,256,256]{2,1,0:T(8,128)(2,1)} %param.8) | copy-start | bytes 786436
  7.4 33.2 %copy-start.4 = (s32[26]{0:T(128)S(1)}, s32[26]{0:T(128)}, u32[]{:S(2)}) copy-start(s32[26]{0:T(128)} %param.9) | copy-start | bytes 316
  7.4 15.6 %reduce-scatter.2.cloned.1.call-start = ((), (), s32[]{:S(2)}) async-start(), calls=%async_computation.6 | async-start | bytes 98304 | tf_op jit(solution)/shard_map/reduce_scatter | solution.py:63
  11.0 13.3 %all-to-all-start = ((s32[4,1,13]{2,1,0:T(1,128)}), s32[4,1,13]{2,1,0:T(1,128)S(1)}, u32[]{:S(2)}, u32[]{:S(2)}) async-start(s32[4,1,13]{2,1,0:T(1,128)} %bitcast.2), calls=%async_computation | async-start | bytes 4096 | tf_op jit(solution)/shard_map/all_to_all | solution.py:31
  24.4 11.1 %all-to-all-start.2 = ((s32[4,1,16]{2,1,0:T(1,128)}), s32[4,1,16]{2,1,0:T(1,128)S(1)}, u32[]{:S(2)}, u32[]{:S(2)}) async-start(s32[4,1,16]{2,1,0:T(1,128)} %bitcast.7), calls=%async_computation.3 | async-start | bytes 4096 | tf_op jit(solution)/shard_map/all_to_all | solution.py:32
  35.5 45.9 %all-to-all-start.3 = ((f32[64,32,128]{2,1,0:T(8,128)}), f32[64,32,128]{2,1,0:T(8,128)S(1)}, u32[]{:S(2)}, u32[]{:S(2)}) async-start(f32[64,32,128]{2,1,0:T(8,128)} %scatter_fusion.1), calls=%async_computation.4 | async-start | bytes 2097152 | tf_op jit(solution)/shard_map/all_to_all | solution.py:78
  81.4 6.3 %copy-start.8 = (u32[32]{0:T(128)S(1)}, u32[32]{0:T(128)}, u32[]{:S(2)}) copy-start(u32[32]{0:T(128)} %constant.130) | copy-start | bytes 388
  81.4 7.6 %copy-start.6 = (s32[26]{0:T(128)S(1)}, s32[26]{0:T(128)}, u32[]{:S(2)}) copy-start(s32[26]{0:T(128)} %param.10) | copy-start | bytes 316
  81.4 7.6 %copy-start.7 = (s32[32]{0:T(128)S(1)}, s32[32]{0:T(128)}, u32[]{:S(2)}) copy-start(s32[32]{0:T(128)} %param.14) | copy-start | bytes 388
  81.4 184.6 %all-to-all-start.1 = ((bf16[52,256,256]{2,1,0:T(8,128)(2,1)}), bf16[52,256,256]{2,1,0:T(8,128)(2,1)}, u32[]{:S(2)}, u32[]{:S(2)}) async-start(bf16[52,256,256]{2,1,0:T(8,128)(2,1)} %scatter_fusion), calls=%async_computation.1 | async-start | bytes 13631488 | tf_op jit(solution)/shard_map/all_to_all | solution.py:56
  86.9 64.6 %all-gather.2.cloned.1.call-start = ((), (), s32[]{:S(2)}) async-start(), calls=%async_computation.5 | async-start | bytes 1310720 | tf_op jit(solution)/shard_map/all_gather | solution.py:37
  87.4 178.6 %all-reduce.6.cloned.1.call-start = ((), (), s32[]{:S(2)}) async-start(), calls=%async_computation.8 | async-start | bytes 2097152
  186.1 9.9 %copy-start.1 = (f32[2,32,128]{2,1,0:T(8,128)S(1)}, f32[2,32,128]{2,1,0:T(8,128)}, u32[]{:S(2)}) copy-start(f32[2,32,128]{2,1,0:T(8,128)} %reduce-scatter.2.cloned.1.call-done) | copy-start | bytes 98308
  186.1 72.8 %copy-start.5 = (s32[32]{0:T(128)S(1)}, s32[32]{0:T(128)}, u32[]{:S(2)}) copy-start(s32[32]{0:T(128)} %param.13) | copy-start | bytes 388
  186.1 79.3 %copy-start.3 = (bf16[2,256,32]{1,2,0:T(8,128)(2,1)S(1)}, bf16[2,256,32]{1,2,0:T(8,128)(2,1)}, u32[]{:S(2)}) copy-start(bf16[2,256,32]{1,2,0:T(8,128)(2,1)} %param.12) | copy-start | bytes 98308
  196.0 96.6 %all-reduce.4.cloned.1.call-start = ((), (), s32[]{:S(2)}) async-start(), calls=%async_computation.7 | async-start | bytes 1048576 | tf_op jit(solution)/shard_map/psum | solution.py:88
Sparse Core Ops, SparseCore 0:
  10.4 12.5 reduce-scatter.1
  196.1 37.5 all-reduce.5
  274.4 18.1 all-reduce.3
Sparse Core Ops, SparseCore 1:
  88.9 62.5 all-gather.1
where the time goes:
time: 303 us; the launch traced here: 302 us
  waiting for transfers between devices  81.9 us (27%)
  blocking collectives  73.8 us (24%)
  local copies, waits for them, and re-layouts  60.3 us (20%)
  matrix products  43.6 us (14%)
  starting transfers between devices  21.8 us (7%)
  between operations  15.4 us (5%)
  other arithmetic  4.85 us (2%)
    all_gather x1, blocking collectives, shards(): gathered_far = lax.all_gather(projection, 'clu', axis=0, tiled=True)  61.5 us
    all_gather x1, waiting for transfers between devices, shards(): gathered = lax.all_gather(panel_field, 'clu', axis=0, tiled=True)  60.4 us
    dot_general x1, local copies, waits for them, and re-layouts, shards(): jnp.einsum('pab,pbk->pak', near_block, column_values, preferred_element_t...  19.9 us
    psum x1, waiting for transfers between devices, shards(): return lax.psum(combined, 'rep')  18.3 us
    dot_general x1, matrix products, shards(): jnp.einsum('pab,pbk->pak', near_block, column_values, preferred_element_t...  10.9 us
    scatter x1, local copies, waits for them, and re-layouts, shards(): send_back = jnp.zeros((owners * near_limit,) + transposed.shape[1:], jnp....  10.9 us
    dot_general x1, matrix products, shards(): jnp.einsum('pc,pak->cak', row_hot, forward, precision=lax.Precision.HIGHEST)  9.86 us
    dot_general x1, matrix products, shards(): jnp.einsum('pab,pak->pbk', near_block, row_values, preferred_element_type...  8.87 us
  transfers between devices with their start and end apart: 8, of which 3 were waited for; matrix products, arithmetic and copies ran while one was open for 32% of the time, Pallas kernels for 0%

commit v1 on v0

v1 whole, which is shorter than its diff:
```python
import functools

import jax
import jax.numpy as jnp
from jax import lax
from jax.experimental import pallas as pl
from jax.experimental.pallas import tpu as pltpu
from jax.sharding import PartitionSpec as P

HIGHEST = lax.Precision.HIGHEST
LAST = (((1,), (1,)), ((), ()))
FIRST = (((0,), (0,)), ((), ()))
VMEM = pl.BlockSpec(memory_space=pltpu.VMEM)
SMEM = pl.BlockSpec(memory_space=pltpu.SMEM)
ANY = pl.BlockSpec(memory_space=pl.ANY)
ROOM = pltpu.CompilerParams(vmem_limit_bytes=48 * 1024 * 1024)


def pack_kernel(where, panel, bases, packed, mine):
    clusters, _, width = panel.shape
    for c in range(clusters):
        packed[c, :width, :] = panel[c].T
        packed[c, width:, :] = bases[c].T
    mine[0] = packed[where[2]]


def pack(where, panel, bases):
    clusters, panels, width = panel.shape
    rows = width + bases.shape[2]
    return pl.pallas_call(
        pack_kernel,
        out_shape=(
            jax.ShapeDtypeStruct((clusters, rows, panels), panel.dtype),
            jax.ShapeDtypeStruct((1, rows, panels), panel.dtype),
        ),
        in_specs=[SMEM, VMEM, VMEM],
        out_specs=(VMEM, VMEM),
        compiler_params=ROOM,
    )(where, panel, bases)


def sum_couplings(far_row, far_slot, coupling, table):
    table[...] = jnp.zeros_like(table)
    for f in range(coupling.shape[0]):
        at = (far_row[f], far_slot[f])
        table[at] = table[at] + coupling[f]


def coupling_matrix(table):
    clusters, slots = table.shape[:2]
    return jnp.concatenate(
        [jnp.concatenate([table[c, t] for t in range(slots)], axis=1) for c in range(clusters)],
        axis=0,
    )


def load_blocks(block, held, sems, group):
    copies = []
    for n in range(block.shape[0] // group):
        span = pl.ds(n * group, group)
        copies.append(pltpu.make_async_copy(block.at[span], held.at[span], sems.at[n]))
        copies[-1].start()
    return copies


def back_kernel(plan, split, *refs):
    n = len(plan)
    place, near_row, near_slot, far_row, far_slot, coupling, block = refs[:7]
    pieces = refs[7 : 7 + n]
    outs = refs[7 + n : 7 + n + (2 if split else 1)]
    full, table, held, sems, piece_sems = refs[7 + n + len(outs) : 12 + n + len(outs)]
    total = refs[12 + n + len(outs)] if split else outs[0]
    group = 2 if block.shape[0] % 2 == 0 else 1
    panels = block.shape[2]
    clusters, rows = full.shape[:2]
    rank = table.shape[2]
    width = rows - rank
    moves = []
    for k, count in enumerate(plan):
        for c in range(count):
            moves.append(
                pltpu.make_async_copy(
                    pieces[k].at[c],
                    full.at[
                        place[2 * k] + c,
                        :,
                        pl.ds(pl.multiple_of(place[2 * k + 1] * panels, panels), panels),
                    ],
                    piece_sems.at[len(moves)],
                )
            )
            moves[-1].start()
    copies = load_blocks(block, held, sems, group)
    total[:, :width, :] = jnp.zeros((total.shape[0], width, panels), jnp.float32)
    sum_couplings(far_row, far_slot, coupling, table)
    for move in moves:
        move.wait()
    projection = jnp.concatenate(
        [
            lax.dot_general(
                full[c, width:, :], full[c, :width, :], LAST, preferred_element_type=jnp.float32
            )
            for c in range(clusters)
        ],
        axis=0,
    )
    weights = lax.dot_general(
        coupling_matrix(table),
        projection,
        FIRST,
        precision=HIGHEST,
        preferred_element_type=jnp.float32,
    )
    for t in range(total.shape[0]):
        for i in range(width // panels):
            total[t, width + i * rank : width + (i + 1) * rank, :] = weights[
                t * rank : (t + 1) * rank, i * panels : (i + 1) * panels
            ]
    for q in range(block.shape[0]):
        if q % group == 0:
            copies[q // group].wait()
        product = jnp.dot(
            full[near_row[q], :width, :], held[q], preferred_element_type=jnp.float32
        )
        slot = near_slot[q]
        total[slot, :width, :] += product.astype(jnp.bfloat16).astype(jnp.float32)
    if split:
        half = total.shape[0] // 2
        outs[0][...] = total[:half]
        outs[1][...] = total[half:]


def back_sums(slots, split, pieces, near_row, near_slot, far_row, far_slot, coupling, block):
    plan = tuple(piece.shape[0] for piece, _, _ in pieces)
    place = jnp.stack([jnp.asarray(v, jnp.int32) for _, c, s in pieces for v in (c, s)])
    rows = pieces[0][0].shape[1]
    pairs, full_panels, panels = block.shape
    rank = coupling.shape[1]
    width = rows - rank
    tall = width + rank * (width // panels)
    count = slots // 2 if split else slots
    shape = jax.ShapeDtypeStruct((count, tall, panels), jnp.float32)
    scratch = [
        pltpu.VMEM((2, rows, full_panels), jnp.bfloat16),
        pltpu.VMEM((2, slots, rank, rank), jnp.float32),
        pltpu.VMEM(block.shape, block.dtype),
        pltpu.SemaphoreType.DMA((pairs,)),
        pltpu.SemaphoreType.DMA((sum(plan),)),
    ]
    if split:
        scratch.append(pltpu.VMEM((slots, tall, panels), jnp.float32))
    return pl.pallas_call(
        functools.partial(back_kernel, plan, split),
        out_shape=(shape,) * (2 if split else 1),
        in_specs=[SMEM] * 5 + [VMEM, ANY] + [ANY] * len(pieces),
        out_specs=(VMEM,) * (2 if split else 1),
        scratch_shapes=scratch,
        compiler_params=ROOM,
    )(
        place, near_row, near_slot, far_row, far_slot, coupling, block, *[p for p, _, _ in pieces]
    )


def forward_kernel(plan, *refs):
    n = len(plan)
    place, near_row, near_col, far_row, far_col, coupling, block = refs[:7]
    pieces = refs[7 : 7 + n]
    keep, give = refs[7 + n : 9 + n]
    full, table, held, total, sems, piece_sems = refs[9 + n :]
    group = 2 if block.shape[0] % 2 == 0 else 1
    slots, rows, panels = full.shape
    rank = table.shape[2]
    width = rows - rank
    full_panels = block.shape[1]
    moves = []
    for k, count in enumerate(plan):
        moves.append(
            pltpu.make_async_copy(
                pieces[k], full.at[pl.ds(place[2 + k], count)], piece_sems.at[k]
            )
        )
        moves[-1].start()
    copies = load_blocks(block, held, sems, group)
    total[...] = jnp.zeros_like(total)
    sum_couplings(far_row, far_col, coupling, table)
    for move in moves:
        move.wait()
    projection = jnp.concatenate(
        [
            lax.dot_general(
                full[t, width:, :], full[t, :width, :], LAST, preferred_element_type=jnp.float32
            )
            for t in range(slots)
        ],
        axis=0,
    )
    weights = jnp.dot(
        coupling_matrix(table), projection, precision=HIGHEST, preferred_element_type=jnp.float32
    )
    for q in range(block.shape[0]):
        if q % group == 0:
            copies[q // group].wait()
        product = lax.dot_general(
            held[q], full[near_col[q], :width, :], LAST, preferred_element_type=jnp.float32
        )
        row = near_row[q]
        total[row] += product
    mine = place[0]
    core = place[1]
    subs = full_panels // panels
    for out, at in ((keep, core), (give, 1 - core)):
        for step in range(1, subs):
            other = lax.rem(mine + step, subs)
            out[0, (step - 1) * panels : step * panels, :] = total[
                at, pl.ds(pl.multiple_of(other * panels, panels), panels), :
            ]
        first = (subs - 1) * panels
        out[0, first + rank :, :] = total[at, pl.ds(pl.multiple_of(mine * panels, panels), panels), :]
        for c in range(2):

            @pl.when(at == c)
            def _():
                out[0, first : first + rank, :] = weights[c * rank : (c + 1) * rank]


def forward_sums(sub, core, slots, pieces, near_row, near_col, far_row, far_col, coupling, block):
    plan = tuple(piece.shape[0] for piece, _ in pieces)
    place = jnp.stack([jnp.asarray(v, jnp.int32) for v in (sub, core, *[c for _, c in pieces])])
    rows = pieces[0][0].shape[1]
    pairs, full_panels, panels = block.shape
    rank = coupling.shape[1]
    width = rows - rank
    shape = jax.ShapeDtypeStruct((1, full_panels + rank, width), jnp.float32)
    return pl.pallas_call(
        functools.partial(forward_kernel, plan),
        out_shape=(shape, shape),
        in_specs=[SMEM] * 5 + [VMEM, ANY] + [ANY] * len(pieces),
        out_specs=(VMEM, VMEM),
        scratch_shapes=[
            pltpu.VMEM((slots, rows, panels), jnp.bfloat16),
            pltpu.VMEM((2, slots, rank, rank), jnp.float32),
            pltpu.VMEM(block.shape, block.dtype),
            pltpu.VMEM((2, full_panels, width), jnp.float32),
            pltpu.SemaphoreType.DMA((pairs,)),
            pltpu.SemaphoreType.DMA((len(pieces),)),
        ],
        compiler_params=ROOM,
    )(place, near_row, near_col, far_row, far_col, coupling, block, *[p for p, _ in pieces])


def finish_kernel(where, packed, both, single, near, far, result, back, weight):
    core = where[2]
    clusters, rows, panels = packed.shape
    width = near.shape[1]
    rank = rows - width
    back[...] = both[...].astype(jnp.float32)
    back[core] = back[core] + single[0]
    for c in range(clusters):
        for i in range(width // panels):
            weight[c, :, i * panels : (i + 1) * panels] = back[
                c, width + i * rank : width + (i + 1) * rank, :
            ]
    weight[core] = weight[core] + far[...]
    for c in range(clusters):
        result[c] = back[c, :width, :].T + lax.dot_general(
            packed[c, width:, :].astype(jnp.float32),
            weight[c],
            FIRST,
            precision=HIGHEST,
            preferred_element_type=jnp.float32,
        )
    result[core] = result[core] + near[...]


def finish(where, packed, both, single, near, far):
    clusters, _, panels = packed.shape
    return pl.pallas_call(
        finish_kernel,
        out_shape=jax.ShapeDtypeStruct((clusters,) + near.shape, jnp.float32),
        in_specs=[SMEM] + [VMEM] * 5,
        out_specs=VMEM,
        scratch_shapes=[
            pltpu.VMEM(both.shape, jnp.float32),
            pltpu.VMEM((clusters,) + far.shape, jnp.float32),
        ],
        compiler_params=ROOM,
    )(where, packed, both, single, near, far)


def swap(value, axis):
    return lax.ppermute(value, axis, [(0, 1), (1, 0)])


def shards_small(panel_field, near_row, near_col, near_block, bases, far_row, far_col, coupling):
    owner, sub, core = lax.axis_index("clu"), lax.axis_index("sub"), lax.axis_index("rep")
    where = jnp.stack([owner, sub, core]).astype(jnp.int32)
    panels = panel_field.shape[1]
    rank = bases.shape[2]
    packed, mine = pack(where, panel_field, bases)

    axes = ("clu", "sub", "rep")
    numbered = [(o, s, r) for o in range(4) for s in range(2) for r in range(2)]
    by_core = [
        (i, ((o ^ (1 + r)) * 2 + s) * 2 + r) for i, (o, s, r) in enumerate(numbered)
    ]
    opposite = [(o, o ^ 3) for o in range(4)]

    def spread(two, one):
        return lax.ppermute(two, axes, by_core), lax.ppermute(one, "clu", opposite)

    across = swap(mine, "sub")
    across_other = swap(across, "rep")
    first, second = spread(packed, mine)

    def slot_of(cluster):
        turn = (cluster // 2) ^ owner
        local = cluster % 2
        paired = (turn == 1) | (turn == 2)
        kept = jnp.where(paired, turn == 1 + core, local == core)
        within = jnp.where(paired, local, jnp.where(turn == 3, 2, 3))
        return jnp.where(kept, within, 4 + within).astype(jnp.int32)

    keep, give = back_sums(
        8,
        True,
        [(packed, 0, sub), (across, core, 1 - sub), (across_other, 1 - core, 1 - sub)],
        near_row,
        slot_of(near_col),
        far_row,
        slot_of(far_col),
        coupling,
        near_block,
    )
    taken = swap(give, "rep")
    to_two = (keep[:2] + taken[:2]).astype(jnp.bfloat16)
    to_one = (keep[2:3] + taken[2:3]).astype(jnp.bfloat16)
    own = keep[3:] + taken[3:]
    back_two, back_one = spread(to_two, to_one)

    first_other, second_other = swap(first, "rep"), swap(second, "rep")
    ahead, behind = forward_sums(
        sub,
        core,
        8,
        [
            (packed, 2 * owner),
            (first, 2 * (owner ^ (1 + core))),
            (first_other, 2 * (owner ^ (2 - core))),
            (second, 2 * (owner ^ 3) + core),
            (second_other, 2 * (owner ^ 3) + 1 - core),
        ],
        near_row,
        near_col,
        far_row,
        far_col,
        coupling,
        near_block,
    )
    behind_other = swap(behind, "rep")
    split = panels + rank
    to_sub = ahead[0, :split] + behind_other[0, :split]
    stays = ahead[0, split:] + behind_other[0, split:]
    from_sub = swap(to_sub, "sub")
    near = stays + from_sub[:panels]
    far = to_sub[panels:] + from_sub[panels:]
    single = own + back_one.astype(jnp.float32)
    result = finish(where, packed, back_two, single, near, far)
    return result + swap(result, "rep")


def shards_any(panel_field, near_row, near_col, near_block, bases, far_row, far_col, coupling):
    owner, sub, core = lax.axis_index("clu"), lax.axis_index("sub"), lax.axis_index("rep")
    owners, subs = lax.axis_size("clu"), lax.axis_size("sub")
    where = jnp.stack([owner, sub, core]).astype(jnp.int32)
    clusters, panels, _ = panel_field.shape
    rank = bases.shape[2]
    packed, _ = pack(where, panel_field, bases)
    around = lax.all_gather(packed, "sub", axis=0)
    gathered = lax.all_gather(packed, "clu", axis=0, tiled=True)
    slots = owners * clusters
    (back,) = back_sums(
        slots,
        False,
        [(around[s], 0, s) for s in range(subs)],
        near_row,
        near_col,
        far_row,
        far_col,
        coupling,
        near_block,
    )
    back = lax.psum(lax.psum_scatter(back, "clu", scatter_dimension=0, tiled=True), "rep")
    ahead, behind = forward_sums(
        sub, core, slots, [(gathered, 0)], near_row, near_col, far_row, far_col, coupling, near_block
    )
    total = (ahead + swap(behind, "rep"))[0]
    first = (subs - 1) * panels
    far = lax.psum(total[first : first + rank], "sub")
    near = total[first + rank :]
    for step in range(1, subs):
        near = near + lax.ppermute(
            total[(step - 1) * panels : step * panels],
            "sub",
            [(s, (s + step) % subs) for s in range(subs)],
        )
    single = lax.dynamic_slice_in_dim(back, core, 1, axis=0)
    result = finish(where, packed, jnp.zeros_like(back), single, near, far)
    return result + swap(result, "rep")


def shards(*arrays):
    sizes = tuple(lax.axis_size(axis) for axis in ("clu", "sub", "rep"))
    if sizes == (4, 2, 2):
        return shards_small(*arrays)
    return shards_any(*arrays)


def solution(mesh):
    placed = (
        P(("parts", "clu"), "sub", None),
        P(("parts", "clu", "rep")),
        P(("parts", "clu", "rep")),
        P(("parts", "clu", "rep"), None, "sub"),
        P(("parts", "clu"), "sub", None),
        P(("parts", "clu", "rep")),
        P(("parts", "clu", "rep")),
        P(("parts", "clu", "rep"), None, None),
    )
    return jax.shard_map(
        shards,
        mesh=mesh,
        in_specs=placed,
        out_specs=P(("parts", "clu"), "sub", None),
        check_vma=False,
    )
```

time: 303 us -> 70.3 us (0.23)
  blocking collectives: 73.8 us -> 0 us
  local copies, waits for them, and re-layouts: 60.3 us -> 5.66 us
  waiting for transfers between devices: 81.9 us -> 27.7 us
  matrix products: 43.6 us -> 0 us
  Pallas kernels: 0 us -> 15.9 us
  between operations: 15.4 us -> 0.14 us
  starting transfers between devices: 21.8 us -> 18.7 us
    all_gather x3 -> x0, blocking collectives: 73.8 us -> none  [the longest x1 61.5 us: shards(): gathered_far = lax.all_gather(projection, 'clu', axis=0, tiled=True)]
    all_gather x1 -> x0, waiting for transfers between devices: 60.4 us -> none  [shards(): gathered = lax.all_gather(panel_field, 'clu', axis=0, tiled=True)]
    dot_general x10 -> x0, matrix products: 43.6 us -> none  [the longest x1 10.9 us: shards(): jnp.einsum('pab,pbk->pak', near_block, column_values, preferred_element_t...]
    ppermute x0 -> x12, waiting for transfers between devices: none -> 27.7 us  [the longest x8 12.8 us: swap(): return lax.ppermute(value, axis, [(0, 1), (1, 0)])]
    all_to_all x4 -> x0, starting transfers between devices: 21.5 us -> none  [the longest x1 6.32 us: shards(): lax.all_to_all(near_table, 'clu', split_axis=0, concat_axis=0, tiled=True)]
    dot_general x2 -> x0, local copies, waits for them, and re-layouts: 20.2 us -> none  [the longest x1 19.9 us: shards(): jnp.einsum('pab,pbk->pak', near_block, column_values, preferred_element_t...]
    ppermute x0 -> x12, starting transfers between devices: none -> 18.7 us  [the longest x8 9.5 us: swap(): return lax.ppermute(value, axis, [(0, 1), (1, 0)])]
    psum x1 -> x0, waiting for transfers between devices: 18.3 us -> none  [shards(): return lax.psum(combined, 'rep')]
  transfers between devices with their start and end apart: 8 -> 12, of which waited for: 3 -> 5; matrix products, arithmetic and copies ran while one was open for 32% -> 1% of each run, Pallas kernels for 0% -> 20%
where the time goes in v1:
time: 70.3 us; the launch traced here: 70 us
  waiting for transfers between devices  27.7 us (39%)
  starting transfers between devices  18.7 us (27%)
  Pallas kernels  15.9 us (23%)
  local copies, waits for them, and re-layouts  5.66 us (8%)
  other arithmetic  1.9 us (3%)
    ppermute x8, waiting for transfers between devices, swap(): return lax.ppermute(value, axis, [(0, 1), (1, 0)])  12.8 us
    ppermute x2, waiting for transfers between devices, spread(): lax.ppermute(one, 'clu', opposite)  9.95 us
    ppermute x8, starting transfers between devices, swap(): return lax.ppermute(value, axis, [(0, 1), (1, 0)])  9.5 us
    pallas_call x1, Pallas kernels, forward_sums(): pl.pallas_call(functools.partial(forward_kernel, plan), out_shape=(shape,...  7.55 us
    pallas_call x1, Pallas kernels, back_sums(): pl.pallas_call(functools.partial(back_kernel, plan, split), out_shape=(sh...  6.45 us
    unnamed x15, local copies, waits for them, and re-layouts  5.49 us
    ppermute x2, starting transfers between devices, spread(): lax.ppermute(one, 'clu', opposite)  5.08 us
    ppermute x2, waiting for transfers between devices, spread(): lax.ppermute(two, axes, by_core)  4.93 us
  transfers between devices with their start and end apart: 12, of which 5 were waited for; matrix products, arithmetic and copies ran while one was open for 1% of the time, Pallas kernels for 20%

profile of v1, /device:TPU:0, one launch (start us, length us, event | category | flops | bytes accessed | tf_op | source)
XLA Modules:
  0.0 70.0 jit_solution(11753914116585857154)
XLA Ops:
  0.0 0.9 %copy.9.bases = bf16[2,256,32]{2,1,0:T(8,128)(2,1)S(1)} copy(bf16[2,256,32]{1,2,0:T(8,128)(2,1)} %param.12) | data formatting | bytes 65536 | tf_op args[4]
  0.9 0.1 pad_add_fusion.where
  1.0 1.0 %copy-done.2 = bf16[2,256,256]{2,1,0:T(8,128)(2,1)S(1)} copy-done((bf16[2,256,256]{2,1,0:T(8,128)(2,1)S(1)}, bf16[2,256,256]{2,1,0:T(8,128)(2,1)}, u32[]{:S(2)}) %copy-start.2) | copy-done | bytes 262168
  1.9 0.7 shard_map.82
  2.6 3.1 %collective-permute-start.5 = (bf16[2,288,256]{2,1,0:T(8,128)(2,1)S(1)}, bf16[2,288,256]{2,1,0:T(8,128)(2,1)S(1)}, u32[]{:S(2)}, u32[]{:S(2)}) collective-permute-start(bf16[2,288,256]{2,1,0:T(8,128)(2,1)S(1)} %get-tuple-element.11.refs_7_.packed), channel_id=1, source_target_pairs={{0,4},{1,9},{2,6},{3,11},{4,0},{5,13},{6,2},{7,15},{8,12},{9,1},{1... | collective-permute-start | bytes 884744 | tf_op jit(solution)/shard_map/ppermute | solution.py:309
  5.7 2.5 %collective-permute-start.7 = (bf16[1,288,256]{2,1,0:T(8,128)(2,1)S(1)}, bf16[1,288,256]{2,1,0:T(8,128)(2,1)S(1)}, u32[]{:S(2)}, u32[]{:S(2)}) collective-permute-start(bf16[1,288,256]{2,1,0:T(8,128)(2,1)S(1)} %get-tuple-element.12), channel_id=1, source_target_pairs={{0,12},{4,8},{8,4},{12,0},{1,13},{5,9},{9,5},{13,1},{2,14},{6,10},... | collective-permute-start | bytes 442376 | tf_op jit(solution)/shard_map/ppermute | solution.py:309
  8.2 4.9 %collective-permute-done.5.refs_8_ = bf16[2,288,256]{2,1,0:T(8,128)(2,1)S(1)} collective-permute-done((bf16[2,288,256]{2,1,0:T(8,128)(2,1)S(1)}, bf16[2,288,256]{2,1,0:T(8,128)(2,1)S(1)}, u32[]{:S(2)}, u32[]{:S(2)}) %collective-permute-start.5) | collective-permute-done | bytes 294944 | tf_op jit(solution)/shard_map/ppermute | solution.py:309
  13.1 5.2 %collective-permute-start.6 = (bf16[2,288,256]{2,1,0:T(8,128)(2,1)S(1)}, bf16[2,288,256]{2,1,0:T(8,128)(2,1)S(1)}, u32[]{:S(2)}, u32[]{:S(2)}) collective-permute-start(bf16[2,288,256]{2,1,0:T(8,128)(2,1)S(1)} %collective-permute-done.5.refs_8_), channel_id=1, source_target_pairs={{0,1},{1,0},{2,3},{3,2},{4,5},{5,4},{6,7},{7,6},{8,9},{9,8},{10,11... | collective-permute-start | bytes 884744 | tf_op jit(solution)/shard_map/ppermute | solution.py:291
  18.3 1.5 %collective-permute-start = (bf16[1,288,256]{2,1,0:T(8,128)(2,1)S(1)}, bf16[1,288,256]{2,1,0:T(8,128)(2,1)S(1)}, u32[]{:S(2)}, u32[]{:S(2)}) collective-permute-start(bf16[1,288,256]{2,1,0:T(8,128)(2,1)S(1)} %get-tuple-element.12), channel_id=1, source_target_pairs={{0,2},{2,0},{1,3},{3,1},{4,6},{6,4},{5,7},{7,5},{8,10},{10,8},{9,1... | collective-permute-start | bytes 442376 | tf_op jit(solution)/shard_map/ppermute | solution.py:291
  19.8 0.1 stack.50.refs_0_
  19.9 0.1 stack.56.refs_0_
  20.1 0.7 select_select_fusion.1.refs_2_
  20.7 3.4 %collective-permute-done.refs_8_ = bf16[1,288,256]{2,1,0:T(8,128)(2,1)S(1)} collective-permute-done((bf16[1,288,256]{2,1,0:T(8,128)(2,1)S(1)}, bf16[1,288,256]{2,1,0:T(8,128)(2,1)S(1)}, u32[]{:S(2)}, u32[]{:S(2)}) %collective-permute-start) | collective-permute-done | bytes 147488 | tf_op jit(solution)/shard_map/ppermute | solution.py:291
  24.1 1.0 %copy-done = f32[32,32,32]{2,1,0:T(8,128)S(1)} copy-done((f32[32,32,32]{2,1,0:T(8,128)S(1)}, f32[32,32,32]{2,1,0:T(8,128)}, u32[]{:S(2)}) %copy-start) | copy-done | bytes 131096
  25.1 0.7 copy-done.3
  25.8 0.7 copy-done.4
  26.5 0.7 copy-done.5
  27.1 0.7 copy-done.6
  27.8 7.5 %shard_map.84 = (f32[1,544,256]{2,1,0:T(8,128)S(1)}, f32[1,544,256]{2,1,0:T(8,128)S(1)}) custom-call(s32[7]{0:T(128)S(1)} %stack.56.refs_0_, s32[26]{0:T(128)S(1)} %copy-done.3, s32[26]{0:T(128)S(1)} %copy-done.5, s32[32]{0:T(128)S(1)} %copy-done.4, s32[32]{0:T(128)S(1)} %copy-done.6, f32[32,32,32]{2,1,0:T(8,128)S(1)} %copy-done, ...), custom_call_target="tpu_custom_call" | custom-call | tf_op jit(solution)/shard_map/pallas_call | solution.py:234
  35.3 0.6 collective-permute-start.9
  35.9 6.4 %shard_map.83 = (f32[4,288,256]{2,1,0:T(8,128)S(1)}, f32[4,288,256]{2,1,0:T(8,128)S(1)}) custom-call(s32[6]{0:T(128)S(1)} %stack.50.refs_0_, s32[26]{0:T(128)S(1)} %copy-done.3, s32[26]{0:T(128)S(1)} %select_select_fusion.1.refs_2_, s32[32]{0:T(128)S(1)} %copy-done.4, s32[32]{0:T(128)S(1)} %select_select_fusion.refs_4_, f32[32,32,32]{2,1,0:T(8,128)S(1)} %copy-done.1, ...), custom_call_target="tpu_custom_call" | custom-call | tf_op jit(solution)/shard_map/pallas_call | solution.py:152
  42.4 0.1 collective-permute-start.2
  42.5 1.6 %collective-permute-start.10 = (f32[288,256]{1,0:T(8,128)S(1)}, f32[288,256]{1,0:T(8,128)S(1)}, u32[]{:S(2)}, u32[]{:S(2)}) collective-permute-start(f32[288,256]{1,0:T(8,128)S(1)} %bitcast.19), channel_id=1, source_target_pairs={{0,2},{2,0},{1,3},{3,1},{4,6},{6,4},{5,7},{7,5},{8,10},{10,8},{9,1... | collective-permute-start | bytes 884744 | tf_op jit(solution)/shard_map/ppermute | solution.py:291
  44.1 7.9 %collective-permute-done.10 = f32[288,256]{1,0:T(8,128)S(1)} collective-permute-done((f32[288,256]{1,0:T(8,128)S(1)}, f32[288,256]{1,0:T(8,128)S(1)}, u32[]{:S(2)}, u32[]{:S(2)}) %collective-permute-start.10) | collective-permute-done | bytes 294944 | tf_op jit(solution)/shard_map/ppermute | solution.py:291
  52.0 0.1 fusion
  52.1 1.0 %collective-permute-start.3 = (bf16[2,288,256]{2,1,0:T(8,128)(2,1)S(1)}, bf16[2,288,256]{2,1,0:T(8,128)(2,1)S(1)}, u32[]{:S(2)}, u32[]{:S(2)}) collective-permute-start(bf16[2,288,256]{2,1,0:T(8,128)(2,1)S(1)} %fusion), channel_id=1, source_target_pairs={{0,4},{1,9},{2,6},{3,11},{4,0},{5,13},{6,2},{7,15},{8,12},{9,1},{1... | collective-permute-start | bytes 884744 | tf_op jit(solution)/shard_map/ppermute | solution.py:309
  53.2 2.6 %collective-permute-start.4 = (bf16[1,288,256]{2,1,0:T(8,128)(2,1)S(1)}, bf16[1,288,256]{2,1,0:T(8,128)(2,1)S(1)}, u32[]{:S(2)}, u32[]{:S(2)}) collective-permute-start(bf16[1,288,256]{2,1,0:T(8,128)(2,1)S(1)} %fusion.1), channel_id=1, source_target_pairs={{0,12},{4,8},{8,4},{12,0},{1,13},{5,9},{9,5},{13,1},{2,14},{6,10},... | collective-permute-start | bytes 442376 | tf_op jit(solution)/shard_map/ppermute | solution.py:309
  55.8 9.9 %collective-permute-done.4 = bf16[1,288,256]{2,1,0:T(8,128)(2,1)S(1)} collective-permute-done((bf16[1,288,256]{2,1,0:T(8,128)(2,1)S(1)}, bf16[1,288,256]{2,1,0:T(8,128)(2,1)S(1)}, u32[]{:S(2)}, u32[]{:S(2)}) %collective-permute-start.4) | collective-permute-done | bytes 147488 | tf_op jit(solution)/shard_map/ppermute | solution.py:309
  65.8 1.2 %shard_map.85 = f32[2,256,256]{2,1,0:T(8,128)S(1)} custom-call(s32[3]{0:T(128)S(1)} %pad_add_fusion.where, bf16[2,288,256]{2,1,0:T(8,128)(2,1)S(1)} %get-tuple-element.11.refs_7_.packed, bf16[2,288,256]{2,1,0:T(8,128)(2,1)S(1)} %collective-permute-done.3.both, f32[1,288,256]{2,1,0:T(8,128)S(1)} %fusion.2.single, f32[256,256]{1,0:T(8,128)S(1)} %slice_add_fusion.4.near, ...), custom_call_target="tpu_custom_call" | custom-call | tf_op jit(solution)/shard_map/pallas_call | solution.py:277
  67.0 0.5 collective-permute-start.11
  67.6 1.5 %collective-permute-done.11 = f32[2,256,256]{2,1,0:T(8,128)S(1)} collective-permute-done((f32[2,256,256]{2,1,0:T(8,128)S(1)}, f32[2,256,256]{2,1,0:T(8,128)S(1)}, u32[]{:S(2)}, u32[]{:S(2)}) %collective-permute-start.11) | collective-permute-done | bytes 524320 | tf_op jit(solution)/shard_map/ppermute | solution.py:291
  69.1 0.9 %add.85 = f32[2,256,256]{2,1,0:T(8,128)} add(f32[2,256,256]{2,1,0:T(8,128)S(1)} %shard_map.85, f32[2,256,256]{2,1,0:T(8,128)S(1)} %collective-permute-done.11) | non-fusion elementwise | flops 131072 | bytes 1572864 | tf_op jit(solution)/shard_map/add | solution.py:368
  (23 shorter events, 0.3 us)
Async XLA Ops:
  1.0 1.0 %copy-start.2 = (bf16[2,256,256]{2,1,0:T(8,128)(2,1)S(1)}, bf16[2,256,256]{2,1,0:T(8,128)(2,1)}, u32[]{:S(2)}) copy-start(bf16[2,256,256]{2,1,0:T(8,128)(2,1)} %panel.1) | copy-start | bytes 786436
  2.6 10.5 %collective-permute-start.5 = (bf16[2,288,256]{2,1,0:T(8,128)(2,1)S(1)}, bf16[2,288,256]{2,1,0:T(8,128)(2,1)S(1)}, u32[]{:S(2)}, u32[]{:S(2)}) collective-permute-start(bf16[2,288,256]{2,1,0:T(8,128)(2,1)S(1)} %get-tuple-element.11.refs_7_.packed), channel_id=1, source_target_pairs={{0,4},{1,9},{2,6},{3,11},{4,0},{5,13},{6,2},{7,15},{8,12},{9,1},{1... | collective-permute-start | bytes 884744 | tf_op jit(solution)/shard_map/ppermute | solution.py:309
  5.7 14.3 %collective-permute-start.7 = (bf16[1,288,256]{2,1,0:T(8,128)(2,1)S(1)}, bf16[1,288,256]{2,1,0:T(8,128)(2,1)S(1)}, u32[]{:S(2)}, u32[]{:S(2)}) collective-permute-start(bf16[1,288,256]{2,1,0:T(8,128)(2,1)S(1)} %get-tuple-element.12), channel_id=1, source_target_pairs={{0,12},{4,8},{8,4},{12,0},{1,13},{5,9},{9,5},{13,1},{2,14},{6,10},... | collective-permute-start | bytes 442376 | tf_op jit(solution)/shard_map/ppermute | solution.py:309
  13.1 11.0 %collective-permute-start.6 = (bf16[2,288,256]{2,1,0:T(8,128)(2,1)S(1)}, bf16[2,288,256]{2,1,0:T(8,128)(2,1)S(1)}, u32[]{:S(2)}, u32[]{:S(2)}) collective-permute-start(bf16[2,288,256]{2,1,0:T(8,128)(2,1)S(1)} %collective-permute-done.5.refs_8_), channel_id=1, source_target_pairs={{0,1},{1,0},{2,3},{3,2},{4,5},{5,4},{6,7},{7,6},{8,9},{9,8},{10,11... | collective-permute-start | bytes 884744 | tf_op jit(solution)/shard_map/ppermute | solution.py:291
  18.3 5.8 %collective-permute-start = (bf16[1,288,256]{2,1,0:T(8,128)(2,1)S(1)}, bf16[1,288,256]{2,1,0:T(8,128)(2,1)S(1)}, u32[]{:S(2)}, u32[]{:S(2)}) collective-permute-start(bf16[1,288,256]{2,1,0:T(8,128)(2,1)S(1)} %get-tuple-element.12), channel_id=1, source_target_pairs={{0,2},{2,0},{1,3},{3,1},{4,6},{6,4},{5,7},{7,5},{8,10},{10,8},{9,1... | collective-permute-start | bytes 442376 | tf_op jit(solution)/shard_map/ppermute | solution.py:291
  20.0 4.1 %collective-permute-start.8 = (bf16[1,288,256]{2,1,0:T(8,128)(2,1)S(1)}, bf16[1,288,256]{2,1,0:T(8,128)(2,1)S(1)}, u32[]{:S(2)}, u32[]{:S(2)}) collective-permute-start(bf16[1,288,256]{2,1,0:T(8,128)(2,1)S(1)} %collective-permute-done.7.refs_10_), channel_id=1, source_target_pairs={{0,1},{1,0},{2,3},{3,2},{4,5},{5,4},{6,7},{7,6},{8,9},{9,8},{10,11... | collective-permute-start | bytes 442376 | tf_op jit(solution)/shard_map/ppermute | solution.py:291
  24.1 11.8 %collective-permute-start.1 = (bf16[1,288,256]{2,1,0:T(8,128)(2,1)S(1)}, bf16[1,288,256]{2,1,0:T(8,128)(2,1)S(1)}, u32[]{:S(2)}, u32[]{:S(2)}) collective-permute-start(bf16[1,288,256]{2,1,0:T(8,128)(2,1)S(1)} %collective-permute-done.refs_8_), channel_id=1, source_target_pairs={{0,1},{1,0},{2,3},{3,2},{4,5},{5,4},{6,7},{7,6},{8,9},{9,8},{10,11... | collective-permute-start | bytes 442376 | tf_op jit(solution)/shard_map/ppermute | solution.py:291
  24.1 1.0 %copy-start = (f32[32,32,32]{2,1,0:T(8,128)S(1)}, f32[32,32,32]{2,1,0:T(8,128)}, u32[]{:S(2)}) copy-start(f32[32,32,32]{2,1,0:T(8,128)} %refs_5_.3) | copy-start | bytes 393220
  25.1 0.7 copy-start.3
  25.8 0.7 copy-start.4
  26.5 0.7 copy-start.5
  27.1 0.7 copy-start.6
  27.8 8.2 %copy-start.1 = (f32[32,32,32]{2,1,0:T(8,128)S(1)}, f32[32,32,32]{2,1,0:T(8,128)}, u32[]{:S(2)}) copy-start(f32[32,32,32]{2,1,0:T(8,128)} %refs_5_.3) | copy-start | bytes 393220
  35.3 7.1 %collective-permute-start.9 = (f32[1,544,256]{2,1,0:T(8,128)S(1)}, f32[1,544,256]{2,1,0:T(8,128)S(1)}, u32[]{:S(2)}, u32[]{:S(2)}) collective-permute-start(f32[1,544,256]{2,1,0:T(8,128)S(1)} %get-tuple-element.16), channel_id=1, source_target_pairs={{0,1},{1,0},{2,3},{3,2},{4,5},{5,4},{6,7},{7,6},{8,9},{9,8},{10,11... | collective-permute-start | bytes 1671176 | tf_op jit(solution)/shard_map/ppermute | solution.py:291
  42.4 9.7 %collective-permute-start.2 = (f32[4,288,256]{2,1,0:T(8,128)S(1)}, f32[4,288,256]{2,1,0:T(8,128)S(1)}, u32[]{:S(2)}, u32[]{:S(2)}) collective-permute-start(f32[4,288,256]{2,1,0:T(8,128)S(1)} %get-tuple-element.14), channel_id=1, source_target_pairs={{0,1},{1,0},{2,3},{3,2},{4,5},{5,4},{6,7},{7,6},{8,9},{9,8},{10,11... | collective-permute-start | bytes 3538952 | tf_op jit(solution)/shard_map/ppermute | solution.py:291
  42.5 9.5 %collective-permute-start.10 = (f32[288,256]{1,0:T(8,128)S(1)}, f32[288,256]{1,0:T(8,128)S(1)}, u32[]{:S(2)}, u32[]{:S(2)}) collective-permute-start(f32[288,256]{1,0:T(8,128)S(1)} %bitcast.19), channel_id=1, source_target_pairs={{0,2},{2,0},{1,3},{3,1},{4,6},{6,4},{5,7},{7,5},{8,10},{10,8},{9,1... | collective-permute-start | bytes 884744 | tf_op jit(solution)/shard_map/ppermute | solution.py:291
  52.1 13.7 %collective-permute-start.3 = (bf16[2,288,256]{2,1,0:T(8,128)(2,1)S(1)}, bf16[2,288,256]{2,1,0:T(8,128)(2,1)S(1)}, u32[]{:S(2)}, u32[]{:S(2)}) collective-permute-start(bf16[2,288,256]{2,1,0:T(8,128)(2,1)S(1)} %fusion), channel_id=1, source_target_pairs={{0,4},{1,9},{2,6},{3,11},{4,0},{5,13},{6,2},{7,15},{8,12},{9,1},{1... | collective-permute-start | bytes 884744 | tf_op jit(solution)/shard_map/ppermute | solution.py:309
  53.2 12.6 %collective-permute-start.4 = (bf16[1,288,256]{2,1,0:T(8,128)(2,1)S(1)}, bf16[1,288,256]{2,1,0:T(8,128)(2,1)S(1)}, u32[]{:S(2)}, u32[]{:S(2)}) collective-permute-start(bf16[1,288,256]{2,1,0:T(8,128)(2,1)S(1)} %fusion.1), channel_id=1, source_target_pairs={{0,12},{4,8},{8,4},{12,0},{1,13},{5,9},{9,5},{13,1},{2,14},{6,10},... | collective-permute-start | bytes 442376 | tf_op jit(solution)/shard_map/ppermute | solution.py:309
  67.0 2.1 %collective-permute-start.11 = (f32[2,256,256]{2,1,0:T(8,128)S(1)}, f32[2,256,256]{2,1,0:T(8,128)S(1)}, u32[]{:S(2)}, u32[]{:S(2)}) collective-permute-start(f32[2,256,256]{2,1,0:T(8,128)S(1)} %shard_map.85), channel_id=1, source_target_pairs={{0,1},{1,0},{2,3},{3,2},{4,5},{5,4},{6,7},{7,6},{8,9},{9,8},{10,11... | collective-permute-start | bytes 1572872 | tf_op jit(solution)/shard_map/ppermute | solution.py:291

commit v2 on v0

v2 whole, which is shorter than its diff:
```python
import functools

import jax
import jax.numpy as jnp
from jax import lax
from jax.experimental import pallas as pl
from jax.experimental.pallas import tpu as pltpu
from jax.sharding import PartitionSpec as P

HIGHEST = lax.Precision.HIGHEST
LAST = (((1,), (1,)), ((), ()))
FIRST = (((0,), (0,)), ((), ()))
VMEM = pl.BlockSpec(memory_space=pltpu.VMEM)
SMEM = pl.BlockSpec(memory_space=pltpu.SMEM)
ANY = pl.BlockSpec(memory_space=pl.ANY)
ROOM = pltpu.CompilerParams(vmem_limit_bytes=32 * 1024 * 1024)


def cost(flops, moved):
    return pl.CostEstimate(flops=flops, bytes_accessed=moved, transcendentals=0)


COST1 = cost(0, 0)
COST2 = cost(0, 0)
COST3 = cost(1 << 30, 1 << 20)


def in_hbm(array):
    return pltpu.with_memory_space_constraint(array, pltpu.HBM)


PARTS = 3


def parts_of(block, held, sems):
    pairs = block.shape[0]
    cuts = [pairs * k // PARTS for k in range(PARTS + 1)]
    return [
        (
            range(a, b),
            pltpu.make_async_copy(block.at[pl.ds(a, b - a)], held.at[pl.ds(a, b - a)], sems.at[k]),
        )
        for k, (a, b) in enumerate(zip(cuts, cuts[1:]))
    ]


def load_kernel(block, held, sems):
    parts = parts_of(block, held, sems)
    for _, copy in parts:
        copy.start()
    for _, copy in parts:
        copy.wait()


def load(block):
    return pl.pallas_call(
        load_kernel,
        out_shape=jax.ShapeDtypeStruct(block.shape, block.dtype),
        in_specs=[ANY],
        out_specs=VMEM,
        scratch_shapes=[pltpu.SemaphoreType.DMA((PARTS,))],
        compiler_params=ROOM,
    )(in_hbm(block))


def pack_kernel(index, panel, bases, packed, mine, held, sems):
    clusters, _, width = panel.shape
    moves = []
    for c in range(clusters):
        moves.append(pltpu.make_async_copy(panel.at[c], held.at[c], sems.at[2 * c]))
        moves.append(
            pltpu.make_async_copy(bases.at[c], packed.at[c, pl.ds(width, bases.shape[1])], sems.at[2 * c + 1])
        )
    for move in moves:
        move.start()
    for c in range(clusters):
        moves[2 * c].wait()
        packed[c, :width, :] = held[c].T
    for c in range(clusters):
        moves[2 * c + 1].wait()
    mine[0] = packed[index[2]]


def pack(index, panel, bases):
    clusters, panels, width = panel.shape
    rows = width + bases.shape[1]
    return pl.pallas_call(
        pack_kernel,
        out_shape=(
            jax.ShapeDtypeStruct((clusters, rows, panels), panel.dtype),
            jax.ShapeDtypeStruct((1, rows, panels), panel.dtype),
        ),
        in_specs=[SMEM, ANY, ANY],
        out_specs=(VMEM, VMEM),
        scratch_shapes=[
            pltpu.VMEM(panel.shape, panel.dtype),
            pltpu.SemaphoreType.DMA((2 * clusters,)),
        ],
        compiler_params=ROOM,
    )(index, in_hbm(panel), in_hbm(bases))


def sum_couplings(row, slot, coupling, table):
    table[...] = jnp.zeros_like(table)
    for f in range(coupling.shape[0]):
        at = (row(f), slot(f))
        table[at] = table[at] + coupling[f]


def coupling_matrix(table):
    clusters, slots = table.shape[:2]
    return jnp.concatenate(
        [jnp.concatenate([table[c, t] for t in range(slots)], axis=1) for c in range(clusters)],
        axis=0,
    )


def each_pair(pairs, step):
    unroll = 13 if pairs % 13 == 0 else 1

    def several(n, carry):
        for k in range(unroll):
            step(n * unroll + k)
        return carry

    lax.fori_loop(0, pairs // unroll, several, 0)


def back_kernel(plan, slot_of, index, starts, coupling, block, *refs):
    n = len(plan)
    pieces = refs[:n]
    total, full, table, held, sems = refs[n:]
    near_row, near_col, far_row, far_col = starts
    parts = parts_of(block, held, sems)
    for _, copy in parts:
        copy.start()
    panels = block.shape[2]
    clusters, rows = full.shape[:2]
    rank = table.shape[2]
    width = rows - rank

    total[:, :width, :] = jnp.zeros((total.shape[0], width, panels), jnp.float32)
    sum_couplings(
        lambda f: index[far_row + f],
        lambda f: slot_of(index[far_col + f], index[0], index[2]),
        coupling,
        table,
    )
    for piece, where in zip(pieces, plan):
        first, sub = where(index[0], index[1], index[2])
        for c in range(piece.shape[0]):
            full[first + c, :, pl.ds(pl.multiple_of(sub * panels, panels), panels)] = piece[c]
    projection = jnp.concatenate(
        [
            lax.dot_general(
                full[c, width:, :], full[c, :width, :], LAST, preferred_element_type=jnp.float32
            )
            for c in range(clusters)
        ],
        axis=0,
    )
    weights = lax.dot_general(
        coupling_matrix(table),
        projection,
        FIRST,
        precision=HIGHEST,
        preferred_element_type=jnp.float32,
    )
    for t in range(total.shape[0]):
        for i in range(width // panels):
            total[t, width + i * rank : width + (i + 1) * rank, :] = weights[
                t * rank : (t + 1) * rank, i * panels : (i + 1) * panels
            ]

    def step(q):
        product = jnp.dot(
            full[index[near_row + q], :width, :], held[q], preferred_element_type=jnp.float32
        )
        slot = slot_of(index[near_col + q], index[0], index[2])
        total[slot, :width, :] += product.astype(jnp.bfloat16).astype(jnp.float32)

    for pairs, copy in parts:
        copy.wait()
        for q in pairs:
            step(q)


def back_sums(slots, slot_of, pieces, index, starts, coupling, block):
    rows = pieces[0][0].shape[1]
    pairs, full_panels, panels = block.shape
    rank = coupling.shape[1]
    width = rows - rank
    tall = width + rank * (width // panels)
    plan = tuple(where for _, where in pieces)

    def kernel(index, *refs):
        back_kernel(plan, slot_of, index, starts, *refs)

    return pl.pallas_call(
        kernel,
        out_shape=jax.ShapeDtypeStruct((slots, tall, panels), jnp.float32),
        in_specs=[SMEM, VMEM, ANY] + [VMEM] * len(pieces),
        out_specs=VMEM,
        scratch_shapes=[
            pltpu.VMEM((2, rows, full_panels), jnp.bfloat16),
            pltpu.VMEM((2, slots, rank, rank), jnp.float32),
            pltpu.VMEM(block.shape, block.dtype),
            pltpu.SemaphoreType.DMA((PARTS,)),
        ],
        compiler_params=ROOM,
        cost_estimate=COST1,
    )(index, coupling, in_hbm(block), *[p for p, _ in pieces])


def forward_rows(turns, index, starts, block, full, total):
    near_row, near_col, _, _ = starts
    rows, panels = total.shape[1] // len(turns), block.shape[2]
    subs = block.shape[1] // panels
    total[...] = jnp.zeros_like(total)

    def step(q):
        field = full[index[near_col + q], : total.shape[2], :]
        row = index[near_row + q]
        for k, turn in enumerate(turns):
            at = lax.rem(index[1] + turn, subs)
            product = lax.dot_general(
                block[q, pl.ds(pl.multiple_of(at * panels, panels), panels), :],
                field,
                LAST,
                preferred_element_type=jnp.float32,
            )
            total[row, k * rows : (k + 1) * rows, :] += product

    each_pair(block.shape[0], step)


def forward_kernel(plan, turns, index, starts, coupling, block, *refs):
    n = len(plan)
    pieces = refs[:n]
    keep, give, full, table, total = refs[n:]
    _, _, far_row, far_col = starts
    slots, rows, _ = full.shape
    rank = table.shape[2]
    width = rows - rank
    sum_couplings(lambda f: index[far_row + f], lambda f: index[far_col + f], coupling, table)
    for piece, where in zip(pieces, plan):
        first = where(index[0], index[1], index[2])
        for c in range(piece.shape[0]):
            full[first + c] = piece[c]
    projection = jnp.concatenate(
        [
            lax.dot_general(
                full[t, width:, :], full[t, :width, :], LAST, preferred_element_type=jnp.float32
            )
            for t in range(slots)
        ],
        axis=0,
    )
    weights = jnp.dot(
        coupling_matrix(table), projection, precision=HIGHEST, preferred_element_type=jnp.float32
    )
    forward_rows(turns, index, starts, block, full, total)
    core, tall = index[2], total.shape[1]
    keep[:tall, :] = total[core]
    keep[tall:, :] = weights
    give[:tall, :] = total[1 - core]
    give[tall:, :] = weights


def forward_far(slots, pieces, index, starts, coupling, block):
    rows = pieces[0][0].shape[1]
    pairs, full_panels, panels = block.shape
    rank = coupling.shape[1]
    width = rows - rank
    plan = tuple(where for _, where in pieces)
    turns = tuple(range(1, full_panels // panels))
    tall = panels * len(turns)
    shape = jax.ShapeDtypeStruct((tall + 2 * rank, width), jnp.float32)

    def kernel(index, *refs):
        forward_kernel(plan, turns, index, starts, *refs)

    return pl.pallas_call(
        kernel,
        out_shape=(shape, shape, jax.ShapeDtypeStruct((slots, rows, panels), jnp.bfloat16)),
        in_specs=[SMEM] + [VMEM] * (2 + len(pieces)),
        out_specs=(VMEM, VMEM, VMEM),
        scratch_shapes=[
            pltpu.VMEM((2, slots, rank, rank), jnp.float32),
            pltpu.VMEM((2, tall, width), jnp.float32),
        ],
        compiler_params=ROOM,
        cost_estimate=COST2,
    )(index, coupling, block, *[p for p, _ in pieces])


def merge_kernel(index, keep, taken, payload, far):
    rank = far.shape[1]
    panels = keep.shape[0] - 2 * rank
    core = index[2]
    for c in range(2):
        rows = slice(panels + c * rank, panels + (c + 1) * rank)
        far[c] = keep[rows, :] + taken[rows, :]
    weights = far[core]
    high = weights.astype(payload.dtype)
    payload[:panels, :] = (keep[:panels] + taken[:panels]).astype(payload.dtype)
    payload[panels : panels + rank, :] = high
    payload[panels + rank :, :] = (weights - high.astype(jnp.float32)).astype(payload.dtype)


def to_other_sub(index, keep, taken, panels):
    rows, width = keep.shape
    rank = (rows - panels) // 2
    return pl.pallas_call(
        merge_kernel,
        out_shape=(
            jax.ShapeDtypeStruct((rows, width), jnp.bfloat16),
            jax.ShapeDtypeStruct((2, rank, width), jnp.float32),
        ),
        in_specs=[SMEM, VMEM, VMEM],
        out_specs=(VMEM, VMEM),
        compiler_params=ROOM,
    )(index, keep, taken)


def own_kernel(starts, index, block, full, total):
    forward_rows((0,), index, starts, block, full, total)


def forward_own(index, starts, block, full, width):
    pairs, full_panels, panels = block.shape
    return pl.pallas_call(
        functools.partial(own_kernel, starts),
        out_shape=jax.ShapeDtypeStruct((2, panels, width), jnp.float32),
        in_specs=[SMEM, VMEM, VMEM],
        out_specs=VMEM,
        compiler_params=ROOM,
    )(index, block, full)


def finish_kernel(counts, index, packed, *refs):
    refs = list(refs)
    both, backs, nears, fars, subs = (
        [refs.pop(0) for _ in range(count)] for count in counts
    )
    result, back, weight = refs
    core = index[2]
    clusters, rows, panels = packed.shape
    width = result.shape[2]
    rank = rows - width
    for k, at in enumerate((core, 1 - core)):
        half = len(backs) // 2
        back[at] = sum(term[0].astype(jnp.float32) for term in backs[k * half : (k + 1) * half])
        result[at] = sum(term[at] for term in nears)
        weight[at] = sum(term[at] for term in fars)
        if subs:
            got = subs[k]
            result[at] += got[:panels].astype(jnp.float32)
            weight[at] += got[panels : panels + rank].astype(jnp.float32) + got[
                panels + rank :
            ].astype(jnp.float32)
    for term in both:
        back[...] += term[...].astype(jnp.float32)
    for c in range(clusters):
        for i in range(width // panels):
            weight[c, :, i * panels : (i + 1) * panels] += back[
                c, width + i * rank : width + (i + 1) * rank, :
            ]
        result[c] += back[c, :width, :].T + lax.dot_general(
            packed[c, width:, :].astype(jnp.float32),
            weight[c],
            FIRST,
            precision=HIGHEST,
            preferred_element_type=jnp.float32,
        )


def finish(index, packed, both, backs, nears, fars, subs):
    clusters = packed.shape[0]
    groups = (both, backs[0] + backs[1], nears, fars, subs)
    return pl.pallas_call(
        functools.partial(finish_kernel, tuple(len(group) for group in groups)),
        out_shape=jax.ShapeDtypeStruct(nears[0].shape, jnp.float32),
        in_specs=[SMEM] + [VMEM] * (1 + sum(len(group) for group in groups)),
        out_specs=VMEM,
        scratch_shapes=[
            pltpu.VMEM((clusters,) + backs[0][0].shape[1:], jnp.float32),
            pltpu.VMEM(fars[0].shape, jnp.float32),
        ],
        compiler_params=ROOM,
    )(index, packed, *[array for group in groups for array in group])


def swap(value, axis):
    return lax.ppermute(value, axis, [(0, 1), (1, 0)])


def stage(apart, run, *operands):
    shapes = jax.eval_shape(run, *operands)
    return lax.cond(
        apart,
        run,
        lambda *_: jax.tree.map(lambda v: jnp.zeros(v.shape, v.dtype), shapes),
        *operands,
    )


def index_table(where, *columns):
    starts, at = [], where.shape[0]
    for column in columns:
        starts.append(at)
        at += column.shape[0]
    return jnp.concatenate([where, *columns]), starts


def shards_small(panel_field, near_row, near_col, near_block, bases, far_row, far_col, coupling):
    owner, sub, core = lax.axis_index("clu"), lax.axis_index("sub"), lax.axis_index("rep")
    where = jnp.stack([owner, sub, core]).astype(jnp.int32)
    _, panels, width = panel_field.shape
    rank = bases.shape[2]
    packed, mine = pack(where, panel_field, jnp.swapaxes(bases, 1, 2))

    axes = ("clu", "sub", "rep")
    numbered = [(o, s, r) for o in range(4) for s in range(2) for r in range(2)]
    by_core = [(i, ((o ^ (1 + r)) * 2 + s) * 2 + r) for i, (o, s, r) in enumerate(numbered)]
    opposite = [(o, o ^ 3) for o in range(4)]

    def spread(two, one):
        return lax.ppermute(two, axes, by_core), lax.ppermute(one, "clu", opposite)

    across = swap(mine, "sub")
    first, second = spread(packed, mine)
    held = near_block

    def slot_of(cluster, owner, core):
        turn = lax.shift_right_logical(cluster, 1) ^ owner
        local = cluster & 1
        paired = (turn == 1) | (turn == 2)
        kept = jnp.where(paired, turn == 1 + core, local == core)
        within = jnp.where(paired, local, jnp.where(turn == 3, 2, 3))
        return jnp.where(kept, within, 4 + within)

    index, starts = index_table(where, near_row, near_col, far_row, far_col)
    apart = near_row[0] >= 0

    def back_half(packed, across, coupling, block):
        across_other = swap(across, "rep")
        total = back_sums(
            8,
            slot_of,
            [
                (packed, lambda o, s, r: (0, s)),
                (across, lambda o, s, r: (r, 1 - s)),
                (across_other, lambda o, s, r: (1 - r, 1 - s)),
            ],
            index,
            starts,
            coupling,
            block,
        )
        taken = swap(total[4:], "rep")
        to_two = (total[:2] + taken[:2]).astype(jnp.bfloat16)
        to_one = (total[2:3] + taken[2:3]).astype(jnp.bfloat16)
        return to_two, to_one, total[3:4] + taken[3:]

    to_two, to_one, own = stage(apart, back_half, packed, across, coupling, near_block)
    to_two, to_one, first, second = lax.optimization_barrier((to_two, to_one, first, second))
    back_two, back_one = spread(to_two, to_one)

    def forward_half(packed, first, second, coupling, block):
        first_other, second_other = swap(first, "rep"), swap(second, "rep")
        held = load(block)
        ahead, behind, full = forward_far(
            8,
            [
                (packed, lambda o, s, r: 2 * o),
                (first, lambda o, s, r: 2 * (o ^ (1 + r))),
                (first_other, lambda o, s, r: 2 * (o ^ (2 - r))),
                (second, lambda o, s, r: 2 * (o ^ 3) + r),
                (second_other, lambda o, s, r: 2 * (o ^ 3) + 1 - r),
            ],
            index,
            starts,
            coupling,
            held,
        )
        own_rows = forward_own(index, starts, held, full, width)
        payload, far = to_other_sub(index, ahead, swap(behind, "rep"), panels)
        return payload, far, own_rows

    payload, far, own_rows = stage(apart, forward_half, packed, first, second, coupling, near_block)

    def between_subs(payload, own_rows, own):
        from_sub = swap(payload, "sub")
        own_rows_other, own_other = swap(own_rows, "rep"), swap(own, "rep")
        return from_sub, swap(from_sub, "rep"), own_rows_other, own_other

    from_sub, from_sub_other, own_rows_other, own_other = stage(
        apart, between_subs, payload, own_rows, own
    )
    back_two, back_one, own_other = lax.optimization_barrier((back_two, back_one, own_other))
    back_two_other, back_one_other = swap(back_two, "rep"), swap(back_one, "rep")
    return finish(
        index,
        packed,
        (back_two, back_two_other),
        ((own, back_one), (own_other, back_one_other)),
        (own_rows, own_rows_other),
        (far,),
        (from_sub, from_sub_other),
    )


def shards_any(panel_field, near_row, near_col, near_block, bases, far_row, far_col, coupling):
    owner, sub, core = lax.axis_index("clu"), lax.axis_index("sub"), lax.axis_index("rep")
    owners, subs = lax.axis_size("clu"), lax.axis_size("sub")
    where = jnp.stack([owner, sub, core]).astype(jnp.int32)
    clusters, panels, width = panel_field.shape
    packed, _ = pack(where, panel_field, jnp.swapaxes(bases, 1, 2))
    around = lax.all_gather(packed, "sub", axis=0)
    gathered = lax.all_gather(packed, "clu", axis=0, tiled=True)
    slots = owners * clusters
    index, starts = index_table(where, near_row, near_col, far_row, far_col)
    held = load(near_block)
    back = back_sums(
        slots,
        lambda cluster, owner, core: cluster,
        [(around[k], lambda o, s, r, k=k: (0, k)) for k in range(subs)],
        index,
        starts,
        coupling,
        near_block,
    )
    back = lax.psum(lax.psum_scatter(back, "clu", scatter_dimension=0, tiled=True), "rep")
    ahead, behind, full = forward_far(
        slots, [(gathered, lambda o, s, r: 0)], index, starts, coupling, held
    )
    taken = swap(behind, "rep")
    near = forward_own(index, starts, held, full, width)
    near = near + swap(near, "rep")
    far = lax.psum((ahead + taken)[(subs - 1) * panels :], "sub").reshape(clusters, -1, width)
    ahead = (ahead + taken)[: (subs - 1) * panels]
    for turn in range(1, subs):
        got = lax.ppermute(
            ahead[(turn - 1) * panels : turn * panels],
            "sub",
            [(s, (s + turn) % subs) for s in range(subs)],
        )
        near = near + jnp.where(core == 0, jnp.stack([got, swap(got, "rep")]), jnp.stack([swap(got, "rep"), got]))
    single = lax.dynamic_slice_in_dim(back, core, 1, axis=0)
    other = lax.dynamic_slice_in_dim(back, 1 - core, 1, axis=0)
    return finish(
        index,
        packed,
        (),
        ((single,), (other,)),
        (near,),
        (far,),
        (),
    )


def shards(*arrays):
    sizes = tuple(lax.axis_size(axis) for axis in ("clu", "sub", "rep"))
    if sizes == (4, 2, 2):
        return shards_small(*arrays)
    return shards_any(*arrays)


def solution(mesh):
    placed = (
        P(("parts", "clu"), "sub", None),
        P(("parts", "clu", "rep")),
        P(("parts", "clu", "rep")),
        P(("parts", "clu", "rep"), None, "sub"),
        P(("parts", "clu"), "sub", None),
        P(("parts", "clu", "rep")),
        P(("parts", "clu", "rep")),
        P(("parts", "clu", "rep"), None, None),
    )
    return jax.shard_map(
        shards,
        mesh=mesh,
        in_specs=placed,
        out_specs=P(("parts", "clu"), "sub", None),
        check_vma=False,
    )
```

time: 303 us -> 47.5 us (0.16)
  blocking collectives: 73.8 us -> 0 us
  waiting for transfers between devices: 81.9 us -> 12.8 us
  local copies, waits for them, and re-layouts: 60.3 us -> 0.87 us
  matrix products: 43.6 us -> 0 us
  Pallas kernels: 0 us -> 19.1 us
  between operations: 15.4 us -> 0.71 us
  starting transfers between devices: 21.8 us -> 13.4 us
  other arithmetic: 4.85 us -> 0.24 us
    all_gather x3 -> x0, blocking collectives: 73.8 us -> none  [the longest x1 61.5 us: shards(): gathered_far = lax.all_gather(projection, 'clu', axis=0, tiled=True)]
    all_gather x1 -> x0, waiting for transfers between devices: 60.4 us -> none  [shards(): gathered = lax.all_gather(panel_field, 'clu', axis=0, tiled=True)]
    dot_general x10 -> x0, matrix products: 43.6 us -> none  [the longest x1 10.9 us: shards(): jnp.einsum('pab,pbk->pak', near_block, column_values, preferred_element_t...]
    all_to_all x4 -> x0, starting transfers between devices: 21.5 us -> none  [the longest x1 6.32 us: shards(): lax.all_to_all(near_table, 'clu', split_axis=0, concat_axis=0, tiled=True)]
    dot_general x2 -> x0, local copies, waits for them, and re-layouts: 20.2 us -> none  [the longest x1 19.9 us: shards(): jnp.einsum('pab,pbk->pak', near_block, column_values, preferred_element_t...]
    pallas_call x0 -> x7, Pallas kernels: none -> 19.1 us  [the longest x1 6.22 us: back_sums(): pl.pallas_call(kernel, out_shape=jax.ShapeDtypeStruct((slots, tall, panel...]
    psum x1 -> x0, waiting for transfers between devices: 18.3 us -> none  [shards(): return lax.psum(combined, 'rep')]
    scatter x2 -> x0, local copies, waits for them, and re-layouts: 15.2 us -> none  [the longest x1 10.9 us: shards(): send_back = jnp.zeros((owners * near_limit,) + transposed.shape[1:], jnp....]
  transfers between devices with their start and end apart: 8 -> 16, of which waited for: 3 -> 6; matrix products, arithmetic and copies ran while one was open for 32% -> 2% of each run, Pallas kernels for 0% -> 31%
where the time goes in v2:
time: 47.5 us; the launch traced here: 47.2 us
  Pallas kernels  19.1 us (40%)
  starting transfers between devices  13.4 us (28%)
  waiting for transfers between devices  12.8 us (27%)
  local copies, waits for them, and re-layouts  0.87 us (2%)
  between operations  0.71 us (1%)
    ppermute x12, waiting for transfers between devices, swap(): return lax.ppermute(value, axis, [(0, 1), (1, 0)])  12.8 us
    pallas_call x1, Pallas kernels, back_sums(): pl.pallas_call(kernel, out_shape=jax.ShapeDtypeStruct((slots, tall, panel...  6.22 us
    ppermute x2, starting transfers between devices, spread(): lax.ppermute(one, 'clu', opposite)  5.12 us
    ppermute x12, starting transfers between devices, swap(): return lax.ppermute(value, axis, [(0, 1), (1, 0)])  4.93 us
    ppermute x2, starting transfers between devices, spread(): lax.ppermute(two, axes, by_core)  3.38 us
    pallas_call x1, Pallas kernels, load(): pl.pallas_call(load_kernel, out_shape=jax.ShapeDtypeStruct(block.shape, b...  3.09 us
    pallas_call x1, Pallas kernels, forward_far(): pl.pallas_call(kernel, out_shape=(shape, shape, jax.ShapeDtypeStruct((slo...  2.85 us
    pallas_call x1, Pallas kernels, finish(): pl.pallas_call(functools.partial(finish_kernel, tuple((len(group) for gro...  2.68 us
  transfers between devices with their start and end apart: 16, of which 6 were waited for; matrix products, arithmetic and copies ran while one was open for 2% of the time, Pallas kernels for 31%

profile of v2, /device:TPU:0, one launch (start us, length us, event | category | flops | bytes accessed | tf_op | source)
XLA Modules:
  0.0 47.2 jit_solution(16960986345312689400)
XLA Ops:
  0.0 0.1 pad_add_fusion.index
  0.1 1.7 %shard_map.82 = (bf16[2,288,256]{2,1,0:T(8,128)(2,1)S(1)}, bf16[1,288,256]{2,1,0:T(8,128)(2,1)S(1)}) custom-call(s32[3]{0:T(128)S(1)} %pad_add_fusion.index, bf16[2,256,256]{2,1,0:T(8,128)(2,1)} %panel.1, bf16[2,32,256]{2,1,0:T(8,128)(2,1)} %bitcast.6), custom_call_target="tpu_custom_call" | custom-call | tf_op jit(solution)/shard_map/pallas_call | solution.py:87
  1.8 3.1 %collective-permute-start.10 = (bf16[2,288,256]{2,1,0:T(8,128)(2,1)S(1)}, bf16[2,288,256]{2,1,0:T(8,128)(2,1)S(1)}, u32[]{:S(2)}, u32[]{:S(2)}) collective-permute-start(bf16[2,288,256]{2,1,0:T(8,128)(2,1)S(1)} %get-tuple-element.71.packed), channel_id=1, source_target_pairs={{0,4},{1,9},{2,6},{3,11},{4,0},{5,13},{6,2},{7,15},{8,12},{9,1},{1... | collective-permute-start | bytes 884744 | tf_op jit(solution)/shard_map/ppermute | solution.py:429
  4.8 1.5 %collective-permute-start.9 = (bf16[1,288,256]{2,1,0:T(8,128)(2,1)S(1)}, bf16[1,288,256]{2,1,0:T(8,128)(2,1)S(1)}, u32[]{:S(2)}, u32[]{:S(2)}) collective-permute-start(bf16[1,288,256]{2,1,0:T(8,128)(2,1)S(1)} %get-tuple-element.72), channel_id=1, source_target_pairs={{0,2},{2,0},{1,3},{3,1},{4,6},{6,4},{5,7},{7,5},{8,10},{10,8},{9,1... | collective-permute-start | bytes 442376 | tf_op jit(solution)/shard_map/ppermute | solution.py:395
  6.3 2.5 %collective-permute-start.11 = (bf16[1,288,256]{2,1,0:T(8,128)(2,1)S(1)}, bf16[1,288,256]{2,1,0:T(8,128)(2,1)S(1)}, u32[]{:S(2)}, u32[]{:S(2)}) collective-permute-start(bf16[1,288,256]{2,1,0:T(8,128)(2,1)S(1)} %get-tuple-element.72), channel_id=1, source_target_pairs={{0,12},{4,8},{8,4},{12,0},{1,13},{5,9},{9,5},{13,1},{2,14},{6,10},... | collective-permute-start | bytes 442376 | tf_op jit(solution)/shard_map/ppermute | solution.py:429
  9.5 0.8 %concatenate.4.index = s32[119]{0:T(128)S(1)} concatenate(s32[1]{0:T(128)} %bitcast, s32[1]{0:T(128)} %bitcast.1, s32[1]{0:T(128)} %bitcast.2, s32[26]{0:T(128)} %param.15, s32[26]{0:T(128)} %param.16, s32[32]{0:T(128)} %param.19, s32[32]{0:T(128)} %param.20), dimensions={0} | concatenate | bytes 952 | tf_op jit(solution)/shard_map/concatenate | solution.py:413
  10.3 0.9 %collective-permute-done.9 = bf16[1,288,256]{2,1,0:T(8,128)(2,1)S(1)} collective-permute-done((bf16[1,288,256]{2,1,0:T(8,128)(2,1)S(1)}, bf16[1,288,256]{2,1,0:T(8,128)(2,1)S(1)}, u32[]{:S(2)}, u32[]{:S(2)}) %collective-permute-start.9) | collective-permute-done | bytes 147488 | tf_op jit(solution)/shard_map/ppermute | solution.py:395
  11.2 10.8 %conditional.3 = (bf16[2,288,256]{2,1,0:T(8,128)(2,1)S(1)}, bf16[1,288,256]{2,1,0:T(8,128)(2,1)S(1)}, f32[1,288,256]{2,1,0:T(8,128)S(1)}) conditional(s32[]{:T(128)} %bitcast.4, () %tuple.31, (bf16[1,288,256]{2,1,0:T(8,128)(2,1)S(1)}, s32[119]{0:T(128)S(1)}, f32[32,32,32]{2,1,0:T(8,128)}, bf16[26,512,256]{2,1,0:T(8,128)(2,1)}, ...), branch_computations={%region_0.0_spmd, %region_1.0_spmd} | conditional | flops 516096 | bytes 10764392 | solution.py:400
  11.2 1.4 %collective-permute-done.7.refs_4_ = bf16[1,288,256]{2,1,0:T(8,128)(2,1)S(1)} collective-permute-done((bf16[1,288,256]{2,1,0:T(8,128)(2,1)S(1)}, bf16[1,288,256]{2,1,0:T(8,128)(2,1)S(1)}, u32[]{:S(2)}, u32[]{:S(2)}) %collective-permute-start.7) | collective-permute-done | bytes 147488 | tf_op jit(solution)/shard_map/cond/branch_1_fun/ppermute | solution.py:395
  12.5 6.2 %branch_1_fun.5 = f32[8,288,256]{2,1,0:T(8,128)S(1)} custom-call(s32[119]{0:T(128)S(1)} %get-tuple-element.33.index, f32[32,32,32]{2,1,0:T(8,128)} %get-tuple-element.34.refs_0_, bf16[26,512,256]{2,1,0:T(8,128)(2,1)} %get-tuple-element.35.refs_1_, bf16[2,288,256]{2,1,0:T(8,128)(2,1)S(1)} %get-tuple-element.36.refs_2_, ...), custom_call_target="tpu_custom_call" | custom-call | tf_op jit(solution)/shard_map/cond/branch_1_fun/pallas_call | solution.py:199
  18.8 0.1 slice.26
  18.8 0.2 collective-permute-start.8
  19.1 2.7 %collective-permute-done.8 = f32[4,288,256]{2,1,0:T(8,128)S(1)} collective-permute-done((f32[4,288,256]{2,1,0:T(8,128)S(1)}, f32[4,288,256]{2,1,0:T(8,128)S(1)}, u32[]{:S(2)}, u32[]{:S(2)}) %collective-permute-start.8) | collective-permute-done | bytes 1179680 | tf_op jit(solution)/shard_map/cond/branch_1_fun/ppermute | solution.py:395
  21.8 0.1 fusion
  21.9 0.1 slice_add_fusion.1
  22.0 0.3 collective-permute-start.12
  22.3 2.6 %collective-permute-start.13 = (bf16[1,288,256]{2,1,0:T(8,128)(2,1)S(1)}, bf16[1,288,256]{2,1,0:T(8,128)(2,1)S(1)}, u32[]{:S(2)}, u32[]{:S(2)}) collective-permute-start(bf16[1,288,256]{2,1,0:T(8,128)(2,1)S(1)} %get-tuple-element.76), channel_id=1, source_target_pairs={{0,12},{4,8},{8,4},{12,0},{1,13},{5,9},{9,5},{13,1},{2,14},{6,10},... | collective-permute-start | bytes 442376 | tf_op jit(solution)/shard_map/ppermute | solution.py:429
  24.9 9.2 %conditional.4 = (bf16[320,256]{1,0:T(8,128)(2,1)S(1)}, f32[2,32,256]{2,1,0:T(8,128)S(1)}, f32[2,256,256]{2,1,0:T(8,128)S(1)}) conditional(s32[]{:T(128)} %bitcast.4, () %tuple.35, (bf16[26,512,256]{2,1,0:T(8,128)(2,1)}, bf16[2,288,256]{2,1,0:T(8,128)(2,1)S(1)}, bf16[1,288,256]{2,1,0:T(8,128)(2,1)S(1)}, s32[119]{0:T(128)S(1)}, ...), branch_computations={%region_2.0_spmd, %region_3.0_spmd} | conditional | bytes 3604652 | solution.py:400
  24.9 0.5 %collective-permute-start.1 = (bf16[1,288,256]{2,1,0:T(8,128)(2,1)S(1)}, bf16[1,288,256]{2,1,0:T(8,128)(2,1)S(1)}, u32[]{:S(2)}, u32[]{:S(2)}) collective-permute-start(bf16[1,288,256]{2,1,0:T(8,128)(2,1)S(1)} %get-tuple-element.43.refs_5_), channel_id=1, source_target_pairs={{0,1},{1,0},{2,3},{3,2},{4,5},{5,4},{6,7},{7,6},{8,9},{9,8},{10,11... | collective-permute-start | bytes 442376 | tf_op jit(solution)/shard_map/cond/branch_1_fun/ppermute | solution.py:395
  25.4 3.1 %branch_1_fun.6.refs_1_.block = bf16[26,512,256]{2,1,0:T(8,128)(2,1)S(1)} custom-call(bf16[26,512,256]{2,1,0:T(8,128)(2,1)} %get-tuple-element.40.block), custom_call_target="tpu_custom_call" | custom-call | tf_op jit(solution)/shard_map/cond/branch_1_fun/pallas_call | solution.py:56
  28.5 2.9 %branch_1_fun.7 = (f32[320,256]{1,0:T(8,128)S(1)}, f32[320,256]{1,0:T(8,128)S(1)}, bf16[8,288,256]{2,1,0:T(8,128)(2,1)S(1)}) custom-call(s32[119]{0:T(128)S(1)} %get-tuple-element.38.index, f32[32,32,32]{2,1,0:T(8,128)S(1)} %copy-done, bf16[26,512,256]{2,1,0:T(8,128)(2,1)S(1)} %branch_1_fun.6.refs_1_.block, ...), custom_call_target="tpu_custom_call" | custom-call | tf_op jit(solution)/shard_map/cond/branch_1_fun/pallas_call | solution.py:283
  31.5 2.0 %branch_1_fun.9 = f32[2,256,256]{2,1,0:T(8,128)S(1)} custom-call(s32[119]{0:T(128)S(1)} %get-tuple-element.38.index, bf16[26,512,256]{2,1,0:T(8,128)(2,1)S(1)} %branch_1_fun.6.refs_1_.block, bf16[8,288,256]{2,1,0:T(8,128)(2,1)S(1)} %get-tuple-element.48.full), custom_call_target="tpu_custom_call" | custom-call | tf_op jit(solution)/shard_map/cond/branch_1_fun/pallas_call | solution.py:332
  33.5 0.6 %branch_1_fun.8 = (bf16[320,256]{1,0:T(8,128)(2,1)S(1)}, f32[2,32,256]{2,1,0:T(8,128)S(1)}) custom-call(s32[119]{0:T(128)S(1)} %get-tuple-element.38.index, f32[320,256]{1,0:T(8,128)S(1)} %get-tuple-element.44.keep, f32[320,256]{1,0:T(8,128)S(1)} %collective-permute-done.2.taken), custom_call_target="tpu_custom_call" | custom-call | tf_op jit(solution)/shard_map/cond/branch_1_fun/pallas_call | solution.py:314
  34.1 8.6 %conditional.5 = (bf16[320,256]{1,0:T(8,128)(2,1)}, bf16[320,256]{1,0:T(8,128)(2,1)}, f32[2,256,256]{2,1,0:T(8,128)}, f32[1,288,256]{2,1,0:T(8,128)}) conditional(s32[]{:T(128)} %bitcast.4, () %tuple.34, (bf16[320,256]{1,0:T(8,128)(2,1)S(1)}, f32[2,256,256]{2,1,0:T(8,128)S(1)}, f32[1,288,256]{2,1,0:T(8,128)S(1)}) %tuple.37), branch_computations={%region_4.0_spmd, %region_5.0_spmd} | conditional | bytes 4587712 | solution.py:400
  34.1 0.6 %collective-permute-start.5 = (f32[2,256,256]{2,1,0:T(8,128)S(1)}, f32[2,256,256]{2,1,0:T(8,128)}, u32[]{:S(2)}, u32[]{:S(2)}) collective-permute-start(f32[2,256,256]{2,1,0:T(8,128)S(1)} %get-tuple-element.50), channel_id=1, source_target_pairs={{0,1},{1,0},{2,3},{3,2},{4,5},{5,4},{6,7},{7,6},{8,9},{9,8},{10,11... | collective-permute-start | bytes 1572872 | tf_op jit(solution)/shard_map/cond/branch_1_fun/ppermute | solution.py:395
  34.7 1.5 %collective-permute-start.3 = (bf16[320,256]{1,0:T(8,128)(2,1)S(1)}, bf16[320,256]{1,0:T(8,128)(2,1)}, u32[]{:S(2)}, u32[]{:S(2)}) collective-permute-start(bf16[320,256]{1,0:T(8,128)(2,1)S(1)} %get-tuple-element.49), channel_id=1, source_target_pairs={{0,2},{2,0},{1,3},{3,1},{4,6},{6,4},{5,7},{7,5},{8,10},{10,8},{9,1... | collective-permute-start | bytes 491528 | tf_op jit(solution)/shard_map/cond/branch_1_fun/ppermute | solution.py:395
  36.1 4.8 %collective-permute-done.3 = bf16[320,256]{1,0:T(8,128)(2,1)} collective-permute-done((bf16[320,256]{1,0:T(8,128)(2,1)S(1)}, bf16[320,256]{1,0:T(8,128)(2,1)}, u32[]{:S(2)}, u32[]{:S(2)}) %collective-permute-start.3) | collective-permute-done | bytes 163872 | tf_op jit(solution)/shard_map/cond/branch_1_fun/ppermute | solution.py:395
  40.9 1.7 %collective-permute-done.4 = bf16[320,256]{1,0:T(8,128)(2,1)} collective-permute-done((bf16[320,256]{1,0:T(8,128)(2,1)}, bf16[320,256]{1,0:T(8,128)(2,1)}, u32[]{:S(2)}, u32[]{:S(2)}) %collective-permute-start.4) | collective-permute-done | bytes 163872 | tf_op jit(solution)/shard_map/cond/branch_1_fun/ppermute | solution.py:395
  42.7 0.2 collective-permute-start.14
  42.9 0.4 collective-permute-start.15
  43.3 1.3 %collective-permute-done.15.refs_5_ = bf16[1,288,256]{2,1,0:T(8,128)(2,1)S(1)} collective-permute-done((bf16[1,288,256]{2,1,0:T(8,128)(2,1)S(1)}, bf16[1,288,256]{2,1,0:T(8,128)(2,1)S(1)}, u32[]{:S(2)}, u32[]{:S(2)}) %collective-permute-start.15) | collective-permute-done | bytes 147488 | tf_op jit(solution)/shard_map/ppermute | solution.py:395
  44.6 2.7 %shard_map.83 = f32[2,256,256]{2,1,0:T(8,128)} custom-call(s32[119]{0:T(128)S(1)} %concatenate.4.index, bf16[2,288,256]{2,1,0:T(8,128)(2,1)S(1)} %get-tuple-element.71.packed, bf16[2,288,256]{2,1,0:T(8,128)(2,1)S(1)} %collective-permute-done.12.refs_0_, bf16[2,288,256]{2,1,0:T(8,128)(2,1)S(1)} %collective-permute-done.14.refs_1_, ...), custom_call_target="tpu_custom_call" | custom-call | tf_op jit(solution)/shard_map/pallas_call | solution.py:381
  (17 shorter events, 0.1 us)
Async XLA Ops:
  1.8 20.2 %collective-permute-start.10 = (bf16[2,288,256]{2,1,0:T(8,128)(2,1)S(1)}, bf16[2,288,256]{2,1,0:T(8,128)(2,1)S(1)}, u32[]{:S(2)}, u32[]{:S(2)}) collective-permute-start(bf16[2,288,256]{2,1,0:T(8,128)(2,1)S(1)} %get-tuple-element.71.packed), channel_id=1, source_target_pairs={{0,4},{1,9},{2,6},{3,11},{4,0},{5,13},{6,2},{7,15},{8,12},{9,1},{1... | collective-permute-start | bytes 884744 | tf_op jit(solution)/shard_map/ppermute | solution.py:429
  4.8 6.3 %collective-permute-start.9 = (bf16[1,288,256]{2,1,0:T(8,128)(2,1)S(1)}, bf16[1,288,256]{2,1,0:T(8,128)(2,1)S(1)}, u32[]{:S(2)}, u32[]{:S(2)}) collective-permute-start(bf16[1,288,256]{2,1,0:T(8,128)(2,1)S(1)} %get-tuple-element.72), channel_id=1, source_target_pairs={{0,2},{2,0},{1,3},{3,1},{4,6},{6,4},{5,7},{7,5},{8,10},{10,8},{9,1... | collective-permute-start | bytes 442376 | tf_op jit(solution)/shard_map/ppermute | solution.py:395
  6.3 15.6 %collective-permute-start.11 = (bf16[1,288,256]{2,1,0:T(8,128)(2,1)S(1)}, bf16[1,288,256]{2,1,0:T(8,128)(2,1)S(1)}, u32[]{:S(2)}, u32[]{:S(2)}) collective-permute-start(bf16[1,288,256]{2,1,0:T(8,128)(2,1)S(1)} %get-tuple-element.72), channel_id=1, source_target_pairs={{0,12},{4,8},{8,4},{12,0},{1,13},{5,9},{9,5},{13,1},{2,14},{6,10},... | collective-permute-start | bytes 442376 | tf_op jit(solution)/shard_map/ppermute | solution.py:429
  11.2 1.4 %collective-permute-start.7 = (bf16[1,288,256]{2,1,0:T(8,128)(2,1)S(1)}, bf16[1,288,256]{2,1,0:T(8,128)(2,1)S(1)}, u32[]{:S(2)}, u32[]{:S(2)}) collective-permute-start(bf16[1,288,256]{2,1,0:T(8,128)(2,1)S(1)} %get-tuple-element.37.refs_3_), channel_id=1, source_target_pairs={{0,1},{1,0},{2,3},{3,2},{4,5},{5,4},{6,7},{7,6},{8,9},{9,8},{10,11... | collective-permute-start | bytes 442376 | tf_op jit(solution)/shard_map/cond/branch_1_fun/ppermute | solution.py:395
  18.8 2.9 %collective-permute-start.8 = (f32[4,288,256]{2,1,0:T(8,128)S(1)}, f32[4,288,256]{2,1,0:T(8,128)S(1)}, u32[]{:S(2)}, u32[]{:S(2)}) collective-permute-start(f32[4,288,256]{2,1,0:T(8,128)S(1)} %slice.26), channel_id=1, source_target_pairs={{0,1},{1,0},{2,3},{3,2},{4,5},{5,4},{6,7},{7,6},{8,9},{9,8},{10,11... | collective-permute-start | bytes 3538952 | tf_op jit(solution)/shard_map/cond/branch_1_fun/ppermute | solution.py:395
  22.0 20.7 %collective-permute-start.12 = (bf16[2,288,256]{2,1,0:T(8,128)(2,1)S(1)}, bf16[2,288,256]{2,1,0:T(8,128)(2,1)S(1)}, u32[]{:S(2)}, u32[]{:S(2)}) collective-permute-start(bf16[2,288,256]{2,1,0:T(8,128)(2,1)S(1)} %get-tuple-element.75), channel_id=1, source_target_pairs={{0,4},{1,9},{2,6},{3,11},{4,0},{5,13},{6,2},{7,15},{8,12},{9,1},{1... | collective-permute-start | bytes 884744 | tf_op jit(solution)/shard_map/ppermute | solution.py:429
  22.3 20.4 %collective-permute-start.13 = (bf16[1,288,256]{2,1,0:T(8,128)(2,1)S(1)}, bf16[1,288,256]{2,1,0:T(8,128)(2,1)S(1)}, u32[]{:S(2)}, u32[]{:S(2)}) collective-permute-start(bf16[1,288,256]{2,1,0:T(8,128)(2,1)S(1)} %get-tuple-element.76), channel_id=1, source_target_pairs={{0,12},{4,8},{8,4},{12,0},{1,13},{5,9},{9,5},{13,1},{2,14},{6,10},... | collective-permute-start | bytes 442376 | tf_op jit(solution)/shard_map/ppermute | solution.py:429
  24.9 3.6 %collective-permute-start = (bf16[2,288,256]{2,1,0:T(8,128)(2,1)S(1)}, bf16[2,288,256]{2,1,0:T(8,128)(2,1)S(1)}, u32[]{:S(2)}, u32[]{:S(2)}) collective-permute-start(bf16[2,288,256]{2,1,0:T(8,128)(2,1)S(1)} %get-tuple-element.42.refs_3_), channel_id=1, source_target_pairs={{0,1},{1,0},{2,3},{3,2},{4,5},{5,4},{6,7},{7,6},{8,9},{9,8},{10,11... | collective-permute-start | bytes 884744 | tf_op jit(solution)/shard_map/cond/branch_1_fun/ppermute | solution.py:395
  24.9 3.6 %collective-permute-start.1 = (bf16[1,288,256]{2,1,0:T(8,128)(2,1)S(1)}, bf16[1,288,256]{2,1,0:T(8,128)(2,1)S(1)}, u32[]{:S(2)}, u32[]{:S(2)}) collective-permute-start(bf16[1,288,256]{2,1,0:T(8,128)(2,1)S(1)} %get-tuple-element.43.refs_5_), channel_id=1, source_target_pairs={{0,1},{1,0},{2,3},{3,2},{4,5},{5,4},{6,7},{7,6},{8,9},{9,8},{10,11... | collective-permute-start | bytes 442376 | tf_op jit(solution)/shard_map/cond/branch_1_fun/ppermute | solution.py:395
  25.4 3.1 %copy-start = (f32[32,32,32]{2,1,0:T(8,128)S(1)}, f32[32,32,32]{2,1,0:T(8,128)}, u32[]{:S(2)}) copy-start(f32[32,32,32]{2,1,0:T(8,128)} %get-tuple-element.39.refs_0_) | copy-start | bytes 393220 | tf_op jit(solution)/shard_map/cond
  31.4 2.1 %collective-permute-start.2 = (f32[320,256]{1,0:T(8,128)S(1)}, f32[320,256]{1,0:T(8,128)S(1)}, u32[]{:S(2)}, u32[]{:S(2)}) collective-permute-start(f32[320,256]{1,0:T(8,128)S(1)} %get-tuple-element.45), channel_id=1, source_target_pairs={{0,1},{1,0},{2,3},{3,2},{4,5},{5,4},{6,7},{7,6},{8,9},{9,8},{10,11... | collective-permute-start | bytes 983048 | tf_op jit(solution)/shard_map/cond/branch_1_fun/ppermute | solution.py:395
  34.1 8.6 %collective-permute-start.5 = (f32[2,256,256]{2,1,0:T(8,128)S(1)}, f32[2,256,256]{2,1,0:T(8,128)}, u32[]{:S(2)}, u32[]{:S(2)}) collective-permute-start(f32[2,256,256]{2,1,0:T(8,128)S(1)} %get-tuple-element.50), channel_id=1, source_target_pairs={{0,1},{1,0},{2,3},{3,2},{4,5},{5,4},{6,7},{7,6},{8,9},{9,8},{10,11... | collective-permute-start | bytes 1572872 | tf_op jit(solution)/shard_map/cond/branch_1_fun/ppermute | solution.py:395
  34.7 6.3 %collective-permute-start.3 = (bf16[320,256]{1,0:T(8,128)(2,1)S(1)}, bf16[320,256]{1,0:T(8,128)(2,1)}, u32[]{:S(2)}, u32[]{:S(2)}) collective-permute-start(bf16[320,256]{1,0:T(8,128)(2,1)S(1)} %get-tuple-element.49), channel_id=1, source_target_pairs={{0,2},{2,0},{1,3},{3,1},{4,6},{6,4},{5,7},{7,5},{8,10},{10,8},{9,1... | collective-permute-start | bytes 491528 | tf_op jit(solution)/shard_map/cond/branch_1_fun/ppermute | solution.py:395
  36.1 4.8 %collective-permute-start.6 = (f32[1,288,256]{2,1,0:T(8,128)S(1)}, f32[1,288,256]{2,1,0:T(8,128)}, u32[]{:S(2)}, u32[]{:S(2)}) collective-permute-start(f32[1,288,256]{2,1,0:T(8,128)S(1)} %get-tuple-element.51), channel_id=1, source_target_pairs={{0,1},{1,0},{2,3},{3,2},{4,5},{5,4},{6,7},{7,6},{8,9},{9,8},{10,11... | collective-permute-start | bytes 884744 | tf_op jit(solution)/shard_map/cond/branch_1_fun/ppermute | solution.py:395
  40.9 1.7 %collective-permute-start.4 = (bf16[320,256]{1,0:T(8,128)(2,1)}, bf16[320,256]{1,0:T(8,128)(2,1)}, u32[]{:S(2)}, u32[]{:S(2)}) collective-permute-start(bf16[320,256]{1,0:T(8,128)(2,1)} %collective-permute-done.3), channel_id=1, source_target_pairs={{0,1},{1,0},{2,3},{3,2},{4,5},{5,4},{6,7},{7,6},{8,9},{9,8},{10,11... | collective-permute-start | bytes 491528 | tf_op jit(solution)/shard_map/cond/branch_1_fun/ppermute | solution.py:395
  42.7 1.9 %collective-permute-start.14 = (bf16[2,288,256]{2,1,0:T(8,128)(2,1)S(1)}, bf16[2,288,256]{2,1,0:T(8,128)(2,1)S(1)}, u32[]{:S(2)}, u32[]{:S(2)}) collective-permute-start(bf16[2,288,256]{2,1,0:T(8,128)(2,1)S(1)} %collective-permute-done.12.refs_0_), channel_id=1, source_target_pairs={{0,1},{1,0},{2,3},{3,2},{4,5},{5,4},{6,7},{7,6},{8,9},{9,8},{10,11... | collective-permute-start | bytes 884744 | tf_op jit(solution)/shard_map/ppermute | solution.py:395
  42.9 1.6 %collective-permute-start.15 = (bf16[1,288,256]{2,1,0:T(8,128)(2,1)S(1)}, bf16[1,288,256]{2,1,0:T(8,128)(2,1)S(1)}, u32[]{:S(2)}, u32[]{:S(2)}) collective-permute-start(bf16[1,288,256]{2,1,0:T(8,128)(2,1)S(1)} %collective-permute-done.13.refs_3_), channel_id=1, source_target_pairs={{0,1},{1,0},{2,3},{3,2},{4,5},{5,4},{6,7},{7,6},{8,9},{9,8},{10,11... | collective-permute-start | bytes 442376 | tf_op jit(solution)/shard_map/ppermute | solution.py:395

commit v3 on v2

--- a/solution.py
+++ b/solution.py
@@ -16,15 +16,6 @@
 ROOM = pltpu.CompilerParams(vmem_limit_bytes=32 * 1024 * 1024)
 
 
-def cost(flops, moved):
-    return pl.CostEstimate(flops=flops, bytes_accessed=moved, transcendentals=0)
-
-
-COST1 = cost(0, 0)
-COST2 = cost(0, 0)
-COST3 = cost(1 << 30, 1 << 20)
-
-
 def in_hbm(array):
     return pltpu.with_memory_space_constraint(array, pltpu.HBM)
 
@@ -44,23 +35,66 @@
     ]
 
 
-def load_kernel(block, held, sems):
+def load_kernel(slot_of, starts, index, coupling, block, held, matrix, couplings, table, sems, sem):
     parts = parts_of(block, held, sems)
+    first = pltpu.make_async_copy(coupling, couplings, sem)
+    first.start()
     for _, copy in parts:
         copy.start()
+    table[...] = jnp.zeros_like(table)
+    first.wait()
+    sum_couplings(slot_of, starts, index, couplings, matrix, table)
     for _, copy in parts:
         copy.wait()
 
 
-def load(block):
-    return pl.pallas_call(
-        load_kernel,
-        out_shape=jax.ShapeDtypeStruct(block.shape, block.dtype),
-        in_specs=[ANY],
+def sum_couplings(slot_of, starts, index, coupling, matrix, table):
+    _, _, far_row, far_col = starts
+    rank = coupling.shape[1]
+    for f in range(coupling.shape[0]):
+        at = (index[far_row + f], slot_of(index[far_col + f], index[0], index[2]))
+        table[at] = table[at] + coupling[f]
+    for c in range(table.shape[0]):
+        matrix[c * rank : (c + 1) * rank, :] = jnp.concatenate(
+            [table[c, t] for t in range(table.shape[1])], axis=1
+        )
+
+
+def load(slots, slot_of, index, starts, coupling, block):
+    rank = coupling.shape[1]
+    return pl.pallas_call(
+        functools.partial(load_kernel, slot_of, starts),
+        out_shape=(
+            jax.ShapeDtypeStruct(block.shape, block.dtype),
+            jax.ShapeDtypeStruct((2 * rank, slots * rank), jnp.float32),
+        ),
+        in_specs=[SMEM, ANY, ANY],
+        out_specs=(VMEM, VMEM),
+        scratch_shapes=[
+            pltpu.VMEM(coupling.shape, coupling.dtype),
+            pltpu.VMEM((2, slots, rank, rank), jnp.float32),
+            pltpu.SemaphoreType.DMA((PARTS,)),
+            pltpu.SemaphoreType.DMA,
+        ],
+        compiler_params=ROOM,
+    )(index, in_hbm(coupling), in_hbm(block))
+
+
+def matrix_kernel(slot_of, starts, index, coupling, matrix, table):
+    table[...] = jnp.zeros_like(table)
+    sum_couplings(slot_of, starts, index, coupling, matrix, table)
+
+
+def couplings_by(slots, slot_of, index, starts, coupling):
+    rank = coupling.shape[1]
+    return pl.pallas_call(
+        functools.partial(matrix_kernel, slot_of, starts),
+        out_shape=jax.ShapeDtypeStruct((2 * rank, slots * rank), jnp.float32),
+        in_specs=[SMEM, VMEM],
         out_specs=VMEM,
-        scratch_shapes=[pltpu.SemaphoreType.DMA((PARTS,))],
-        compiler_params=ROOM,
-    )(in_hbm(block))
+        scratch_shapes=[pltpu.VMEM((2, slots, rank, rank), jnp.float32)],
+        compiler_params=ROOM,
+    )(index, coupling)
 
 
 def pack_kernel(index, panel, bases, packed, mine, held, sems):
@@ -100,21 +134,6 @@
     )(index, in_hbm(panel), in_hbm(bases))
 
 
-def sum_couplings(row, slot, coupling, table):
-    table[...] = jnp.zeros_like(table)
-    for f in range(coupling.shape[0]):
-        at = (row(f), slot(f))
-        table[at] = table[at] + coupling[f]
-
-
-def coupling_matrix(table):
-    clusters, slots = table.shape[:2]
-    return jnp.concatenate(
-        [jnp.concatenate([table[c, t] for t in range(slots)], axis=1) for c in range(clusters)],
-        axis=0,
-    )
-
-
 def each_pair(pairs, step):
     unroll = 13 if pairs % 13 == 0 else 1
 
@@ -126,26 +145,16 @@
     lax.fori_loop(0, pairs // unroll, several, 0)
 
 
-def back_kernel(plan, slot_of, index, starts, coupling, block, *refs):
+def back_kernel(plan, slot_of, starts, index, matrix, block, *refs):
     n = len(plan)
     pieces = refs[:n]
-    total, full, table, held, sems = refs[n:]
-    near_row, near_col, far_row, far_col = starts
-    parts = parts_of(block, held, sems)
-    for _, copy in parts:
-        copy.start()
+    total, full = refs[n:]
+    near_row, near_col, _, _ = starts
     panels = block.shape[2]
     clusters, rows = full.shape[:2]
-    rank = table.shape[2]
+    rank = matrix.shape[0] // clusters
     width = rows - rank
-
     total[:, :width, :] = jnp.zeros((total.shape[0], width, panels), jnp.float32)
-    sum_couplings(
-        lambda f: index[far_row + f],
-        lambda f: slot_of(index[far_col + f], index[0], index[2]),
-        coupling,
-        table,
-    )
     for piece, where in zip(pieces, plan):
         first, sub = where(index[0], index[1], index[2])
         for c in range(piece.shape[0]):
@@ -160,7 +169,7 @@
         axis=0,
     )
     weights = lax.dot_general(
-        coupling_matrix(table),
+        matrix[...],
         projection,
         FIRST,
         precision=HIGHEST,
@@ -174,49 +183,35 @@
 
     def step(q):
         product = jnp.dot(
-            full[index[near_row + q], :width, :], held[q], preferred_element_type=jnp.float32
+            full[index[near_row + q], :width, :], block[q], preferred_element_type=jnp.float32
         )
         slot = slot_of(index[near_col + q], index[0], index[2])
         total[slot, :width, :] += product.astype(jnp.bfloat16).astype(jnp.float32)
 
-    for pairs, copy in parts:
-        copy.wait()
-        for q in pairs:
-            step(q)
-
-
-def back_sums(slots, slot_of, pieces, index, starts, coupling, block):
+    each_pair(block.shape[0], step)
+
+
+def back_sums(slots, slot_of, pieces, index, starts, matrix, block):
     rows = pieces[0][0].shape[1]
-    pairs, full_panels, panels = block.shape
-    rank = coupling.shape[1]
+    _, full_panels, panels = block.shape
+    rank = matrix.shape[1] // slots
     width = rows - rank
     tall = width + rank * (width // panels)
     plan = tuple(where for _, where in pieces)
-
-    def kernel(index, *refs):
-        back_kernel(plan, slot_of, index, starts, *refs)
-
-    return pl.pallas_call(
-        kernel,
+    return pl.pallas_call(
+        functools.partial(back_kernel, plan, slot_of, starts),
         out_shape=jax.ShapeDtypeStruct((slots, tall, panels), jnp.float32),
-        in_specs=[SMEM, VMEM, ANY] + [VMEM] * len(pieces),
+        in_specs=[SMEM] + [VMEM] * (2 + len(pieces)),
         out_specs=VMEM,
-        scratch_shapes=[
-            pltpu.VMEM((2, rows, full_panels), jnp.bfloat16),
-            pltpu.VMEM((2, slots, rank, rank), jnp.float32),
-            pltpu.VMEM(block.shape, block.dtype),
-            pltpu.SemaphoreType.DMA((PARTS,)),
-        ],
-        compiler_params=ROOM,
-        cost_estimate=COST1,
-    )(index, coupling, in_hbm(block), *[p for p, _ in pieces])
-
-
-def forward_rows(turns, index, starts, block, full, total):
+        scratch_shapes=[pltpu.VMEM((2, rows, full_panels), jnp.bfloat16)],
+        compiler_params=ROOM,
+    )(index, matrix, block, *[p for p, _ in pieces])
+
+
+def forward_step(turns, index, starts, block, full, total):
     near_row, near_col, _, _ = starts
     rows, panels = total.shape[1] // len(turns), block.shape[2]
     subs = block.shape[1] // panels
-    total[...] = jnp.zeros_like(total)
 
     def step(q):
         field = full[index[near_col + q], : total.shape[2], :]
@@ -231,21 +226,22 @@
             )
             total[row, k * rows : (k + 1) * rows, :] += product
 
-    each_pair(block.shape[0], step)
-
-
-def forward_kernel(plan, turns, index, starts, coupling, block, *refs):
+    return step
+
+
+def forward_kernel(plan, turns, starts, index, matrix, block, *refs):
     n = len(plan)
     pieces = refs[:n]
-    keep, give, full, table, total = refs[n:]
-    _, _, far_row, far_col = starts
+    keep, give, full, held, total, sems = refs[n:]
+    parts = parts_of(block, held, sems)
+    for _, copy in parts:
+        copy.start()
     slots, rows, _ = full.shape
-    rank = table.shape[2]
+    rank = matrix.shape[1] // slots
     width = rows - rank
-    sum_couplings(lambda f: index[far_row + f], lambda f: index[far_col + f], coupling, table)
     for piece, where in zip(pieces, plan):
-        first = where(index[0], index[1], index[2])
-        for c in range(piece.shape[0]):
+        firsts = where(index[0], index[1], index[2])
+        for c, first in enumerate(firsts):
             full[first + c] = piece[c]
     projection = jnp.concatenate(
         [
@@ -257,9 +253,14 @@
         axis=0,
     )
     weights = jnp.dot(
-        coupling_matrix(table), projection, precision=HIGHEST, preferred_element_type=jnp.float32
-    )
-    forward_rows(turns, index, starts, block, full, total)
+        matrix[...], projection, precision=HIGHEST, preferred_element_type=jnp.float32
+    )
+    total[...] = jnp.zeros_like(total)
+    step = forward_step(turns, index, starts, held, full, total)
+    for pairs, copy in parts:
+        copy.wait()
+        for q in pairs:
+            step(q)
     core, tall = index[2], total.shape[1]
     keep[:tall, :] = total[core]
     keep[tall:, :] = weights
@@ -267,31 +268,31 @@
     give[tall:, :] = weights
 
 
-def forward_far(slots, pieces, index, starts, coupling, block):
+def forward_far(slots, pieces, index, starts, matrix, block):
     rows = pieces[0][0].shape[1]
-    pairs, full_panels, panels = block.shape
-    rank = coupling.shape[1]
+    _, full_panels, panels = block.shape
+    rank = matrix.shape[1] // slots
     width = rows - rank
     plan = tuple(where for _, where in pieces)
     turns = tuple(range(1, full_panels // panels))
     tall = panels * len(turns)
     shape = jax.ShapeDtypeStruct((tall + 2 * rank, width), jnp.float32)
-
-    def kernel(index, *refs):
-        forward_kernel(plan, turns, index, starts, *refs)
-
-    return pl.pallas_call(
-        kernel,
-        out_shape=(shape, shape, jax.ShapeDtypeStruct((slots, rows, panels), jnp.bfloat16)),
-        in_specs=[SMEM] + [VMEM] * (2 + len(pieces)),
-        out_specs=(VMEM, VMEM, VMEM),
+    return pl.pallas_call(
+        functools.partial(forward_kernel, plan, turns, starts),
+        out_shape=(
+            shape,
+            shape,
+            jax.ShapeDtypeStruct((slots, rows, panels), jnp.bfloat16),
+            jax.ShapeDtypeStruct(block.shape, block.dtype),
+        ),
+        in_specs=[SMEM, VMEM, ANY] + [VMEM] * len(pieces),
+        out_specs=(VMEM,) * 4,
         scratch_shapes=[
-            pltpu.VMEM((2, slots, rank, rank), jnp.float32),
             pltpu.VMEM((2, tall, width), jnp.float32),
+            pltpu.SemaphoreType.DMA((PARTS,)),
         ],
         compiler_params=ROOM,
-        cost_estimate=COST2,
-    )(index, coupling, block, *[p for p, _ in pieces])
+    )(index, matrix, in_hbm(block), *[p for p, _ in pieces])
 
 
 def merge_kernel(index, keep, taken, payload, far):
@@ -324,14 +325,14 @@
 
 
 def own_kernel(starts, index, block, full, total):
-    forward_rows((0,), index, starts, block, full, total)
+    total[...] = jnp.zeros_like(total)
+    each_pair(block.shape[0], forward_step((0,), index, starts, block, full, total))
 
 
 def forward_own(index, starts, block, full, width):
-    pairs, full_panels, panels = block.shape
     return pl.pallas_call(
         functools.partial(own_kernel, starts),
-        out_shape=jax.ShapeDtypeStruct((2, panels, width), jnp.float32),
+        out_shape=jax.ShapeDtypeStruct((2, block.shape[2], width), jnp.float32),
         in_specs=[SMEM, VMEM, VMEM],
         out_specs=VMEM,
         compiler_params=ROOM,
@@ -340,25 +341,26 @@
 
 def finish_kernel(counts, index, packed, *refs):
     refs = list(refs)
-    both, backs, nears, fars, subs = (
-        [refs.pop(0) for _ in range(count)] for count in counts
-    )
+    both, backs, nears, fars, subs = ([refs.pop(0) for _ in range(count)] for count in counts)
     result, back, weight = refs
     core = index[2]
     clusters, rows, panels = packed.shape
     width = result.shape[2]
     rank = rows - width
+    half = len(backs) // 2
     for k, at in enumerate((core, 1 - core)):
-        half = len(backs) // 2
-        back[at] = sum(term[0].astype(jnp.float32) for term in backs[k * half : (k + 1) * half])
-        result[at] = sum(term[at] for term in nears)
-        weight[at] = sum(term[at] for term in fars)
+        back[at] = sum(
+            term[0].astype(jnp.float32) for term in backs[k * half : (k + 1) * half]
+        )
+        near = sum(term[at] for term in nears)
+        far = sum(term[at] for term in fars)
         if subs:
             got = subs[k]
-            result[at] += got[:panels].astype(jnp.float32)
-            weight[at] += got[panels : panels + rank].astype(jnp.float32) + got[
-                panels + rank :
-            ].astype(jnp.float32)
+            near += got[:panels].astype(jnp.float32)
+            far += got[panels : panels + rank].astype(jnp.float32)
+            far += got[panels + rank :].astype(jnp.float32)
+        result[at] = near
+        weight[at] = far
     for term in both:
         back[...] += term[...].astype(jnp.float32)
     for c in range(clusters):
@@ -376,7 +378,6 @@
 
 
 def finish(index, packed, both, backs, nears, fars, subs):
-    clusters = packed.shape[0]
     groups = (both, backs[0] + backs[1], nears, fars, subs)
     return pl.pallas_call(
         functools.partial(finish_kernel, tuple(len(group) for group in groups)),
@@ -384,7 +385,7 @@
         in_specs=[SMEM] + [VMEM] * (1 + sum(len(group) for group in groups)),
         out_specs=VMEM,
         scratch_shapes=[
-            pltpu.VMEM((clusters,) + backs[0][0].shape[1:], jnp.float32),
+            pltpu.VMEM((packed.shape[0],) + backs[0][0].shape[1:], jnp.float32),
             pltpu.VMEM(fars[0].shape, jnp.float32),
         ],
         compiler_params=ROOM,
@@ -425,11 +426,9 @@
     by_core = [(i, ((o ^ (1 + r)) * 2 + s) * 2 + r) for i, (o, s, r) in enumerate(numbered)]
     opposite = [(o, o ^ 3) for o in range(4)]
 
-    def spread(two, one):
-        return lax.ppermute(two, axes, by_core), lax.ppermute(one, "clu", opposite)
-
     across = swap(mine, "sub")
-    first, second = spread(packed, mine)
+    incoming = [lax.ppermute(packed[c : c + 1], axes, by_core) for c in range(2)]
+    incoming.append(lax.ppermute(mine, "clu", opposite))
     held = near_block
 
     def slot_of(cluster, owner, core):
@@ -443,8 +442,12 @@
     index, starts = index_table(where, near_row, near_col, far_row, far_col)
     apart = near_row[0] >= 0
 
+    def cluster_of(cluster, owner, core):
+        return cluster
+
     def back_half(packed, across, coupling, block):
         across_other = swap(across, "rep")
+        held, by_slot = load(8, slot_of, index, starts, coupling, block)
         total = back_sums(
             8,
             slot_of,
@@ -455,57 +458,65 @@
             ],
             index,
             starts,
-            coupling,
-            block,
+            by_slot,
+            held,
         )
         taken = swap(total[4:], "rep")
         to_two = (total[:2] + taken[:2]).astype(jnp.bfloat16)
         to_one = (total[2:3] + taken[2:3]).astype(jnp.bfloat16)
-        return to_two, to_one, total[3:4] + taken[3:]
-
-    to_two, to_one, own = stage(apart, back_half, packed, across, coupling, near_block)
-    to_two, to_one, first, second = lax.optimization_barrier((to_two, to_one, first, second))
-    back_two, back_one = spread(to_two, to_one)
-
-    def forward_half(packed, first, second, coupling, block):
-        first_other, second_other = swap(first, "rep"), swap(second, "rep")
-        held = load(block)
-        ahead, behind, full = forward_far(
+        by_cluster = couplings_by(8, cluster_of, index, starts, coupling)
+        return to_two, to_one, total[3:4] + taken[3:], by_cluster
+
+    to_two, to_one, own, by_cluster = stage(
+        apart, back_half, packed, across, coupling, near_block
+    )
+    to_two, to_one, *incoming = lax.optimization_barrier((to_two, to_one, *incoming))
+    back_two = lax.ppermute(to_two, axes, by_core)
+    back_one = lax.ppermute(to_one, "clu", opposite)
+    incoming = jnp.concatenate(incoming, axis=0)
+    incoming_other = swap(incoming, "rep")
+
+    def forward_half(packed, incoming, incoming_other, matrix, block):
+        ahead, behind, full, held = forward_far(
             8,
             [
-                (packed, lambda o, s, r: 2 * o),
-                (first, lambda o, s, r: 2 * (o ^ (1 + r))),
-                (first_other, lambda o, s, r: 2 * (o ^ (2 - r))),
-                (second, lambda o, s, r: 2 * (o ^ 3) + r),
-                (second_other, lambda o, s, r: 2 * (o ^ 3) + 1 - r),
+                (packed, lambda o, s, r: (2 * o,) * 2),
+                (incoming, lambda o, s, r: (2 * (o ^ (1 + r)),) * 2 + (2 * (o ^ 3) + r - 2,)),
+                (
+                    incoming_other,
+                    lambda o, s, r: (2 * (o ^ (2 - r)),) * 2 + (2 * (o ^ 3) + 1 - r - 2,),
+                ),
             ],
             index,
             starts,
-            coupling,
-            held,
+            matrix,
+            block,
         )
         own_rows = forward_own(index, starts, held, full, width)
         payload, far = to_other_sub(index, ahead, swap(behind, "rep"), panels)
         return payload, far, own_rows
 
-    payload, far, own_rows = stage(apart, forward_half, packed, first, second, coupling, near_block)
+    payload, far, own_rows = stage(
+        apart, forward_half, packed, incoming, incoming_other, by_cluster, near_block
+    )
 
     def between_subs(payload, own_rows, own):
-        from_sub = swap(payload, "sub")
-        own_rows_other, own_other = swap(own_rows, "rep"), swap(own, "rep")
-        return from_sub, swap(from_sub, "rep"), own_rows_other, own_other
-
-    from_sub, from_sub_other, own_rows_other, own_other = stage(
-        apart, between_subs, payload, own_rows, own
-    )
-    back_two, back_one, own_other = lax.optimization_barrier((back_two, back_one, own_other))
-    back_two_other, back_one_other = swap(back_two, "rep"), swap(back_one, "rep")
+        own = jnp.where(
+            jnp.arange(2)[:, None, None] == core, own, swap(own, "rep")
+        )
+        return swap(payload, "sub"), own_rows + swap(own_rows, "rep"), own
+
+    from_sub, near, own = stage(apart, between_subs, payload, own_rows, own)
+    back_two, back_one, near = lax.optimization_barrier((back_two, back_one, near))
+    from_sub_other = swap(from_sub, "rep")
+    backs = jnp.concatenate([back_two, back_one], axis=0)
+    backs_other = swap(backs, "rep")
     return finish(
         index,
         packed,
-        (back_two, back_two_other),
-        ((own, back_one), (own_other, back_one_other)),
-        (own_rows, own_rows_other),
+        (own, backs[:2], backs_other[:2]),
+        ((backs[2:],), (backs_other[2:],)),
+        (near,),
         (far,),
         (from_sub, from_sub_other),
     )
@@ -521,19 +532,22 @@
     gathered = lax.all_gather(packed, "clu", axis=0, tiled=True)
     slots = owners * clusters
     index, starts = index_table(where, near_row, near_col, far_row, far_col)
-    held = load(near_block)
+    def slot_of(cluster, owner, core):
+        return cluster
+
+    held, matrix = load(slots, slot_of, index, starts, coupling, near_block)
     back = back_sums(
         slots,
-        lambda cluster, owner, core: cluster,
+        slot_of,
         [(around[k], lambda o, s, r, k=k: (0, k)) for k in range(subs)],
         index,
         starts,
-        coupling,
-        near_block,
+        matrix,
+        held,
     )
     back = lax.psum(lax.psum_scatter(back, "clu", scatter_dimension=0, tiled=True), "rep")
-    ahead, behind, full = forward_far(
-        slots, [(gathered, lambda o, s, r: 0)], index, starts, coupling, held
+    ahead, behind, full, held = forward_far(
+        slots, [(gathered, lambda o, s, r: (0,) * slots)], index, starts, matrix, near_block
     )
     taken = swap(behind, "rep")
     near = forward_own(index, starts, held, full, width)
@@ -549,15 +563,7 @@
         near = near + jnp.where(core == 0, jnp.stack([got, swap(got, "rep")]), jnp.stack([swap(got, "rep"), got]))
     single = lax.dynamic_slice_in_dim(back, core, 1, axis=0)
     other = lax.dynamic_slice_in_dim(back, 1 - core, 1, axis=0)
-    return finish(
-        index,
-        packed,
-        (),
-        ((single,), (other,)),
-        (near,),
-        (far,),
-        (),
-    )
+    return finish(index, packed, (), ((single,), (other,)), (near,), (far,), ())
 
 
 def shards(*arrays):

time: 47.5 us -> 44.2 us (0.931)
  waiting for transfers between devices: 12.8 us -> 8.48 us
    ppermute x12 -> x10, waiting for transfers between devices: 12.8 us -> 8.47 us  [swap(): return lax.ppermute(value, axis, [(0, 1), (1, 0)])]
    ppermute x12 -> x10, starting transfers between devices: 4.93 us -> 5.61 us  [swap(): return lax.ppermute(value, axis, [(0, 1), (1, 0)])]
    pallas_call x3 -> x4, Pallas kernels: 12.2 us -> 12.6 us  [the longest x1 4.25 us: forward_far(): pl.pallas_call(functools.partial(forward_kernel, plan, turns, starts), ou...]
    ppermute x4 -> x5, starting transfers between devices: 8.5 us -> 8.07 us  [the longest x1 5.11 us: shards_small(): incoming.append(lax.ppermute(mine, 'clu', opposite))]
  transfers between devices with their start and end apart: 16 -> 15, of which waited for: 6 -> 7; matrix products, arithmetic and copies ran while one was open for 2% -> 3% of each run, Pallas kernels for 31% -> 35%
where the time goes in v3:
time: 44.2 us; the launch traced here: 44 us
  Pallas kernels  19.2 us (43%)
  starting transfers between devices  13.7 us (31%)
  waiting for transfers between devices  8.48 us (19%)
  local copies, waits for them, and re-layouts  1.31 us (3%)
  between operations  0.77 us (2%)
  other arithmetic  0.46 us (1%)
    ppermute x10, waiting for transfers between devices, swap(): return lax.ppermute(value, axis, [(0, 1), (1, 0)])  8.47 us
    ppermute x10, starting transfers between devices, swap(): return lax.ppermute(value, axis, [(0, 1), (1, 0)])  5.61 us
    ppermute x1, starting transfers between devices, shards_small(): incoming.append(lax.ppermute(mine, 'clu', opposite))  5.11 us
    pallas_call x1, Pallas kernels, forward_far(): pl.pallas_call(functools.partial(forward_kernel, plan, turns, starts), ou...  4.25 us
    pallas_call x1, Pallas kernels, back_sums(): pl.pallas_call(functools.partial(back_kernel, plan, slot_of, starts), out...  3.85 us
    pallas_call x1, Pallas kernels, load(): pl.pallas_call(functools.partial(load_kernel, slot_of, starts), out_shape...  3.75 us
    pallas_call x1, Pallas kernels, finish(): pl.pallas_call(functools.partial(finish_kernel, tuple((len(group) for gro...  2.35 us
    ppermute x2, starting transfers between devices, shards_small(): incoming = [lax.ppermute(packed[c:c + 1], axes, by_core) for c in range(2)]  2.08 us
  transfers between devices with their start and end apart: 15, of which 7 were waited for; matrix products, arithmetic and copies ran while one was open for 3% of the time, Pallas kernels for 35%

profile of v3, /device:TPU:0, one launch (start us, length us, event | category | flops | bytes accessed | tf_op | source)
XLA Modules:
  0.0 44.0 jit_solution(17073987094379747427)
XLA Ops:
  0.1 1.7 %shard_map.83 = (bf16[2,288,256]{2,1,0:T(8,128)(2,1)S(1)}, bf16[1,288,256]{2,1,0:T(8,128)(2,1)S(1)}) custom-call(s32[3]{0:T(128)S(1)} %pad_add_fusion.index, bf16[2,256,256]{2,1,0:T(8,128)(2,1)} %panel.1, bf16[2,32,256]{2,1,0:T(8,128)(2,1)} %bitcast.10), custom_call_target="tpu_custom_call" | custom-call | tf_op jit(solution)/shard_map/pallas_call | solution.py:121
  1.8 5.1 %collective-permute-start.9 = (bf16[1,288,256]{2,1,0:T(8,128)(2,1)S(1)}, bf16[1,288,256]{2,1,0:T(8,128)(2,1)S(1)}, u32[]{:S(2)}, u32[]{:S(2)}) collective-permute-start(bf16[1,288,256]{2,1,0:T(8,128)(2,1)S(1)} %get-tuple-element.79), channel_id=1, source_target_pairs={{0,12},{4,8},{8,4},{12,0},{1,13},{5,9},{9,5},{13,1},{2,14},{6,10},... | collective-permute-start | bytes 442376 | tf_op jit(solution)/shard_map/ppermute | solution.py:431
  6.9 1.5 %collective-permute-start.6 = (bf16[1,288,256]{2,1,0:T(8,128)(2,1)S(1)}, bf16[1,288,256]{2,1,0:T(8,128)(2,1)S(1)}, u32[]{:S(2)}, u32[]{:S(2)}) collective-permute-start(bf16[1,288,256]{2,1,0:T(8,128)(2,1)S(1)} %get-tuple-element.79), channel_id=1, source_target_pairs={{0,2},{2,0},{1,3},{3,1},{4,6},{6,4},{5,7},{7,5},{8,10},{10,8},{9,1... | collective-permute-start | bytes 442376 | tf_op jit(solution)/shard_map/ppermute | solution.py:396
  8.5 2.0 %collective-permute-start.7 = (bf16[1,288,256]{2,1,0:T(8,128)(2,1)S(1)}, bf16[1,288,256]{2,1,0:T(8,128)(2,1)S(1)}, u32[]{:S(2)}, u32[]{:S(2)}) collective-permute-start(bf16[1,288,256]{2,1,0:T(8,128)(2,1)S(1)} %get-tuple-element.103), channel_id=1, source_target_pairs={{0,4},{1,9},{2,6},{3,11},{4,0},{5,13},{6,2},{7,15},{8,12},{9,1},{1... | collective-permute-start | bytes 442376 | tf_op jit(solution)/shard_map/ppermute | solution.py:430
  11.1 0.8 %concatenate.10.index = s32[119]{0:T(128)S(1)} concatenate(s32[1]{0:T(128)} %bitcast.2, s32[1]{0:T(128)} %bitcast.3, s32[1]{0:T(128)} %bitcast.4, s32[26]{0:T(128)} %param.15, s32[26]{0:T(128)} %param.16, s32[32]{0:T(128)} %param.19, s32[32]{0:T(128)} %param.20), dimensions={0} | concatenate | bytes 952 | tf_op jit(solution)/shard_map/concatenate | solution.py:414
  11.9 0.3 collective-permute-done.6
  12.2 11.0 %conditional.3 = (bf16[2,288,256]{2,1,0:T(8,128)(2,1)S(1)}, bf16[1,288,256]{2,1,0:T(8,128)(2,1)S(1)}, f32[1,288,256]{2,1,0:T(8,128)S(1)}, f32[64,256]{1,0:T(8,128)S(1)}) conditional(s32[]{:T(128)} %bitcast.6, () %tuple.33, (s32[119]{0:T(128)S(1)}, f32[32,32,32]{2,1,0:T(8,128)}, bf16[26,512,256]{2,1,0:T(8,128)(2,1)}, ...), branch_computations={%region_0.0_spmd, %region_1.0_spmd} | conditional | flops 516096 | bytes 11288716 | solution.py:401
  12.2 3.7 %branch_1_fun.6 = (bf16[26,512,256]{2,1,0:T(8,128)(2,1)S(1)}, f32[64,256]{1,0:T(8,128)S(1)}) custom-call(s32[119]{0:T(128)S(1)} %get-tuple-element.35.index, f32[32,32,32]{2,1,0:T(8,128)} %get-tuple-element.99.coupling, bf16[26,512,256]{2,1,0:T(8,128)(2,1)} %get-tuple-element.37.block), custom_call_target="tpu_custom_call" | custom-call | tf_op jit(solution)/shard_map/cond/branch_1_fun/pallas_call | solution.py:65
  15.9 3.8 %branch_1_fun.7 = f32[8,288,256]{2,1,0:T(8,128)S(1)} custom-call(s32[119]{0:T(128)S(1)} %get-tuple-element.35.index, f32[64,256]{1,0:T(8,128)S(1)} %get-tuple-element.38.matrix, bf16[26,512,256]{2,1,0:T(8,128)(2,1)S(1)} %get-tuple-element.39.block, bf16[2,288,256]{2,1,0:T(8,128)(2,1)S(1)} %get-tuple-element.40.refs_0_, ...), custom_call_target="tpu_custom_call" | custom-call | tf_op jit(solution)/shard_map/cond/branch_1_fun/pallas_call | solution.py:201
  19.9 0.6 %collective-permute-start.2 = (f32[4,288,256]{2,1,0:T(8,128)S(1)}, f32[4,288,256]{2,1,0:T(8,128)S(1)}, u32[]{:S(2)}, u32[]{:S(2)}) collective-permute-start(f32[4,288,256]{2,1,0:T(8,128)S(1)} %slice.42), channel_id=1, source_target_pairs={{0,1},{1,0},{2,3},{3,2},{4,5},{5,4},{6,7},{7,6},{8,9},{9,8},{10,11... | collective-permute-start | bytes 3538952 | tf_op jit(solution)/shard_map/cond/branch_1_fun/ppermute | solution.py:396
  20.5 0.3 copy-done
  20.8 0.8 %branch_1_fun.8 = f32[64,256]{1,0:T(8,128)S(1)} custom-call(s32[119]{0:T(128)S(1)} %get-tuple-element.35.index, f32[32,32,32]{2,1,0:T(8,128)S(1)} %copy-done), custom_call_target="tpu_custom_call" | custom-call | tf_op jit(solution)/shard_map/cond/branch_1_fun/pallas_call | solution.py:90
  21.7 1.3 %collective-permute-done.2 = f32[4,288,256]{2,1,0:T(8,128)S(1)} collective-permute-done((f32[4,288,256]{2,1,0:T(8,128)S(1)}, f32[4,288,256]{2,1,0:T(8,128)S(1)}, u32[]{:S(2)}, u32[]{:S(2)}) %collective-permute-start.2) | collective-permute-done | bytes 1179680 | tf_op jit(solution)/shard_map/cond/branch_1_fun/ppermute | solution.py:396
  23.2 0.4 collective-permute-start.10
  23.7 0.9 %collective-permute-start.12 = (bf16[1,288,256]{2,1,0:T(8,128)(2,1)S(1)}, bf16[1,288,256]{2,1,0:T(8,128)(2,1)S(1)}, u32[]{:S(2)}, u32[]{:S(2)}) collective-permute-start(bf16[1,288,256]{2,1,0:T(8,128)(2,1)S(1)} %get-tuple-element.91), channel_id=1, source_target_pairs={{0,12},{4,8},{8,4},{12,0},{1,13},{5,9},{9,5},{13,1},{2,14},{6,10},... | collective-permute-start | bytes 442376 | tf_op jit(solution)/shard_map/ppermute | solution.py:475
  24.6 0.5 %collective-permute-done.10 = bf16[3,288,256]{2,1,0:T(8,128)(2,1)S(1)} collective-permute-done((bf16[3,288,256]{2,1,0:T(8,128)(2,1)S(1)}, bf16[3,288,256]{2,1,0:T(8,128)(2,1)S(1)}, u32[]{:S(2)}, u32[]{:S(2)}) %collective-permute-start.10) | collective-permute-done | bytes 442400 | tf_op jit(solution)/shard_map/ppermute | solution.py:396
  25.1 7.3 %conditional.4 = (bf16[320,256]{1,0:T(8,128)(2,1)S(1)}, f32[2,32,256]{2,1,0:T(8,128)S(1)}, f32[2,256,256]{2,1,0:T(8,128)S(1)}) conditional(s32[]{:T(128)} %bitcast.6, () %tuple.32, (s32[119]{0:T(128)S(1)}, f32[64,256]{1,0:T(8,128)S(1)}, bf16[26,512,256]{2,1,0:T(8,128)(2,1)}, bf16[2,288,256]{2,1,0:T(8,128)(2,1)S(1)}, ...), branch_computations={%region_2.0_spmd, %region_3.0_spmd} | conditional | bytes 1310784 | solution.py:401
  25.1 4.2 %branch_1_fun.9 = (f32[320,256]{1,0:T(8,128)S(1)}, f32[320,256]{1,0:T(8,128)S(1)}, bf16[8,288,256]{2,1,0:T(8,128)(2,1)S(1)}, bf16[26,512,256]{2,1,0:T(8,128)(2,1)S(1)}) custom-call(s32[119]{0:T(128)S(1)} %get-tuple-element.42.index, f32[64,256]{1,0:T(8,128)S(1)} %get-tuple-element.43.matrix, bf16[26,512,256]{2,1,0:T(8,128)(2,1)} %get-tuple-element.44.block, ...), custom_call_target="tpu_custom_call" | custom-call | tf_op jit(solution)/shard_map/cond/branch_1_fun/pallas_call | solution.py:280
  29.4 0.4 collective-permute-start
  29.8 2.0 %branch_1_fun.11 = f32[2,256,256]{2,1,0:T(8,128)S(1)} custom-call(s32[119]{0:T(128)S(1)} %get-tuple-element.42.index, bf16[26,512,256]{2,1,0:T(8,128)(2,1)S(1)} %get-tuple-element.52.block, bf16[8,288,256]{2,1,0:T(8,128)(2,1)S(1)} %get-tuple-element.53.full), custom_call_target="tpu_custom_call" | custom-call | tf_op jit(solution)/shard_map/cond/branch_1_fun/pallas_call | solution.py:333
  31.8 0.6 %branch_1_fun.10 = (bf16[320,256]{1,0:T(8,128)(2,1)S(1)}, f32[2,32,256]{2,1,0:T(8,128)S(1)}) custom-call(s32[119]{0:T(128)S(1)} %get-tuple-element.42.index, f32[320,256]{1,0:T(8,128)S(1)} %get-tuple-element.48.keep, f32[320,256]{1,0:T(8,128)S(1)} %collective-permute-done.taken), custom_call_target="tpu_custom_call" | custom-call | tf_op jit(solution)/shard_map/cond/branch_1_fun/pallas_call | solution.py:315
  32.4 6.9 %conditional.5 = (bf16[320,256]{1,0:T(8,128)(2,1)}, f32[2,256,256]{2,1,0:T(8,128)S(1)}, f32[2,288,256]{2,1,0:T(8,128)S(1)}) conditional(s32[]{:T(128)} %bitcast.6, () %tuple.31, (bf16[320,256]{1,0:T(8,128)(2,1)S(1)}, f32[2,256,256]{2,1,0:T(8,128)S(1)}, s32[]{:T(128)}, f32[1,288,256]{2,1,0:T(8,128)S(1)}) %tuple.37), branch_computations={%region_4.0_spmd, %region_5.6_spmd} | conditional | flops 278530 | bytes 6684824 | solution.py:401
  32.4 0.2 collective-permute-start.5
  32.6 0.4 collective-permute-start.4
  33.0 1.5 %collective-permute-start.3 = (bf16[320,256]{1,0:T(8,128)(2,1)S(1)}, bf16[320,256]{1,0:T(8,128)(2,1)}, u32[]{:S(2)}, u32[]{:S(2)}) collective-permute-start(bf16[320,256]{1,0:T(8,128)(2,1)S(1)} %get-tuple-element.54), channel_id=1, source_target_pairs={{0,2},{2,0},{1,3},{3,1},{4,6},{6,4},{5,7},{7,5},{8,10},{10,8},{9,1... | collective-permute-start | bytes 491528 | tf_op jit(solution)/shard_map/cond/branch_1_fun/ppermute | solution.py:396
  34.5 0.1 broadcast_select_fusion
  34.6 0.2 collective-permute-done.4
  34.9 4.5 %collective-permute-done.3 = bf16[320,256]{1,0:T(8,128)(2,1)} collective-permute-done((bf16[320,256]{1,0:T(8,128)(2,1)S(1)}, bf16[320,256]{1,0:T(8,128)(2,1)}, u32[]{:S(2)}, u32[]{:S(2)}) %collective-permute-start.3) | collective-permute-done | bytes 163872 | tf_op jit(solution)/shard_map/cond/branch_1_fun/ppermute | solution.py:396
  39.5 0.5 %collective-permute-start.14 = (bf16[320,256]{1,0:T(8,128)(2,1)}, bf16[320,256]{1,0:T(8,128)(2,1)S(1)}, u32[]{:S(2)}, u32[]{:S(2)}) collective-permute-start(bf16[320,256]{1,0:T(8,128)(2,1)} %get-tuple-element.97.refs_7_), channel_id=1, source_target_pairs={{0,1},{1,0},{2,3},{3,2},{4,5},{5,4},{6,7},{7,6},{8,9},{9,8},{10,11... | collective-permute-start | bytes 491528 | tf_op jit(solution)/shard_map/ppermute | solution.py:396
  40.0 1.3 %collective-permute-done.13 = bf16[3,288,256]{2,1,0:T(8,128)(2,1)S(1)} collective-permute-done((bf16[3,288,256]{2,1,0:T(8,128)(2,1)S(1)}, bf16[3,288,256]{2,1,0:T(8,128)(2,1)S(1)}, u32[]{:S(2)}, u32[]{:S(2)}) %collective-permute-start.13) | collective-permute-done | bytes 442400 | tf_op jit(solution)/shard_map/ppermute | solution.py:396
  41.3 0.4 collective-permute-done.14.refs_8_
  41.7 2.4 %shard_map.84 = f32[2,256,256]{2,1,0:T(8,128)} custom-call(s32[119]{0:T(128)S(1)} %concatenate.10.index, bf16[2,288,256]{2,1,0:T(8,128)(2,1)S(1)} %get-tuple-element.78.packed, f32[2,288,256]{2,1,0:T(8,128)S(1)} %get-tuple-element.89.refs_0_, bf16[2,288,256]{2,1,0:T(8,128)(2,1)S(1)} %collective-permute-done.11.refs_1_, ...), custom_call_target="tpu_custom_call" | custom-call | tf_op jit(solution)/shard_map/pallas_call | solution.py:382
  (26 shorter events, 0.7 us)
Async XLA Ops:
  1.8 21.4 %collective-permute-start.9 = (bf16[1,288,256]{2,1,0:T(8,128)(2,1)S(1)}, bf16[1,288,256]{2,1,0:T(8,128)(2,1)S(1)}, u32[]{:S(2)}, u32[]{:S(2)}) collective-permute-start(bf16[1,288,256]{2,1,0:T(8,128)(2,1)S(1)} %get-tuple-element.79), channel_id=1, source_target_pairs={{0,12},{4,8},{8,4},{12,0},{1,13},{5,9},{9,5},{13,1},{2,14},{6,10},... | collective-permute-start | bytes 442376 | tf_op jit(solution)/shard_map/ppermute | solution.py:431
  6.9 5.3 %collective-permute-start.6 = (bf16[1,288,256]{2,1,0:T(8,128)(2,1)S(1)}, bf16[1,288,256]{2,1,0:T(8,128)(2,1)S(1)}, u32[]{:S(2)}, u32[]{:S(2)}) collective-permute-start(bf16[1,288,256]{2,1,0:T(8,128)(2,1)S(1)} %get-tuple-element.79), channel_id=1, source_target_pairs={{0,2},{2,0},{1,3},{3,1},{4,6},{6,4},{5,7},{7,5},{8,10},{10,8},{9,1... | collective-permute-start | bytes 442376 | tf_op jit(solution)/shard_map/ppermute | solution.py:396
  8.4 14.8 %collective-permute-start.8 = (bf16[1,288,256]{2,1,0:T(8,128)(2,1)S(1)}, bf16[1,288,256]{2,1,0:T(8,128)(2,1)S(1)}, u32[]{:S(2)}, u32[]{:S(2)}) collective-permute-start(bf16[1,288,256]{2,1,0:T(8,128)(2,1)S(1)} %get-tuple-element.102), channel_id=1, source_target_pairs={{0,4},{1,9},{2,6},{3,11},{4,0},{5,13},{6,2},{7,15},{8,12},{9,1},{1... | collective-permute-start | bytes 442376 | tf_op jit(solution)/shard_map/ppermute | solution.py:430
  8.5 14.7 %collective-permute-start.7 = (bf16[1,288,256]{2,1,0:T(8,128)(2,1)S(1)}, bf16[1,288,256]{2,1,0:T(8,128)(2,1)S(1)}, u32[]{:S(2)}, u32[]{:S(2)}) collective-permute-start(bf16[1,288,256]{2,1,0:T(8,128)(2,1)S(1)} %get-tuple-element.103), channel_id=1, source_target_pairs={{0,4},{1,9},{2,6},{3,11},{4,0},{5,13},{6,2},{7,15},{8,12},{9,1},{1... | collective-permute-start | bytes 442376 | tf_op jit(solution)/shard_map/ppermute | solution.py:430
  12.2 3.8 %collective-permute-start.1 = (bf16[1,288,256]{2,1,0:T(8,128)(2,1)S(1)}, bf16[1,288,256]{2,1,0:T(8,128)(2,1)S(1)}, u32[]{:S(2)}, u32[]{:S(2)}) collective-permute-start(bf16[1,288,256]{2,1,0:T(8,128)(2,1)S(1)} %get-tuple-element.41.refs_1_), channel_id=1, source_target_pairs={{0,1},{1,0},{2,3},{3,2},{4,5},{5,4},{6,7},{7,6},{8,9},{9,8},{10,11... | collective-permute-start | bytes 442376 | tf_op jit(solution)/shard_map/cond/branch_1_fun/ppermute | solution.py:396
  19.8 1.0 %copy-start = (f32[32,32,32]{2,1,0:T(8,128)S(1)}, f32[32,32,32]{2,1,0:T(8,128)}, u32[]{:S(2)}) copy-start(f32[32,32,32]{2,1,0:T(8,128)} %get-tuple-element.99.coupling) | copy-start | bytes 393220 | tf_op jit(solution)/shard_map/cond
  19.9 3.1 %collective-permute-start.2 = (f32[4,288,256]{2,1,0:T(8,128)S(1)}, f32[4,288,256]{2,1,0:T(8,128)S(1)}, u32[]{:S(2)}, u32[]{:S(2)}) collective-permute-start(f32[4,288,256]{2,1,0:T(8,128)S(1)} %slice.42), channel_id=1, source_target_pairs={{0,1},{1,0},{2,3},{3,2},{4,5},{5,4},{6,7},{7,6},{8,9},{9,8},{10,11... | collective-permute-start | bytes 3538952 | tf_op jit(solution)/shard_map/cond/branch_1_fun/ppermute | solution.py:396
  23.2 1.9 %collective-permute-start.10 = (bf16[3,288,256]{2,1,0:T(8,128)(2,1)S(1)}, bf16[3,288,256]{2,1,0:T(8,128)(2,1)S(1)}, u32[]{:S(2)}, u32[]{:S(2)}) collective-permute-start(bf16[3,288,256]{2,1,0:T(8,128)(2,1)S(1)} %constant_dynamic-update-slice_fusion), channel_id=1, source_target_pairs={{0,1},{1,0},{2,3},{3,2},{4,5},{5,4},{6,7},{7,6},{8,9},{9,8},{10,11... | collective-permute-start | bytes 1327112 | tf_op jit(solution)/shard_map/ppermute | solution.py:396
  23.7 15.7 %collective-permute-start.11 = (bf16[2,288,256]{2,1,0:T(8,128)(2,1)S(1)}, bf16[2,288,256]{2,1,0:T(8,128)(2,1)S(1)}, u32[]{:S(2)}, u32[]{:S(2)}) collective-permute-start(bf16[2,288,256]{2,1,0:T(8,128)(2,1)S(1)} %get-tuple-element.90), channel_id=1, source_target_pairs={{0,4},{1,9},{2,6},{3,11},{4,0},{5,13},{6,2},{7,15},{8,12},{9,1},{1... | collective-permute-start | bytes 884744 | tf_op jit(solution)/shard_map/ppermute | solution.py:474
  23.7 15.7 %collective-permute-start.12 = (bf16[1,288,256]{2,1,0:T(8,128)(2,1)S(1)}, bf16[1,288,256]{2,1,0:T(8,128)(2,1)S(1)}, u32[]{:S(2)}, u32[]{:S(2)}) collective-permute-start(bf16[1,288,256]{2,1,0:T(8,128)(2,1)S(1)} %get-tuple-element.91), channel_id=1, source_target_pairs={{0,12},{4,8},{8,4},{12,0},{1,13},{5,9},{9,5},{13,1},{2,14},{6,10},... | collective-permute-start | bytes 442376 | tf_op jit(solution)/shard_map/ppermute | solution.py:475
  29.4 2.4 %collective-permute-start = (f32[320,256]{1,0:T(8,128)S(1)}, f32[320,256]{1,0:T(8,128)S(1)}, u32[]{:S(2)}, u32[]{:S(2)}) collective-permute-start(f32[320,256]{1,0:T(8,128)S(1)} %get-tuple-element.49), channel_id=1, source_target_pairs={{0,1},{1,0},{2,3},{3,2},{4,5},{5,4},{6,7},{7,6},{8,9},{9,8},{10,11... | collective-permute-start | bytes 983048 | tf_op jit(solution)/shard_map/cond/branch_1_fun/ppermute | solution.py:396
  32.4 2.1 %collective-permute-start.5 = (f32[1,288,256]{2,1,0:T(8,128)S(1)}, f32[1,288,256]{2,1,0:T(8,128)S(1)}, u32[]{:S(2)}, u32[]{:S(2)}) collective-permute-start(f32[1,288,256]{2,1,0:T(8,128)S(1)} %get-tuple-element.57), channel_id=1, source_target_pairs={{0,1},{1,0},{2,3},{3,2},{4,5},{5,4},{6,7},{7,6},{8,9},{9,8},{10,11... | collective-permute-start | bytes 884744 | tf_op jit(solution)/shard_map/cond/branch_1_fun/ppermute | solution.py:396
  32.6 2.2 %collective-permute-start.4 = (f32[2,256,256]{2,1,0:T(8,128)S(1)}, f32[2,256,256]{2,1,0:T(8,128)S(1)}, u32[]{:S(2)}, u32[]{:S(2)}) collective-permute-start(f32[2,256,256]{2,1,0:T(8,128)S(1)} %get-tuple-element.55), channel_id=1, source_target_pairs={{0,1},{1,0},{2,3},{3,2},{4,5},{5,4},{6,7},{7,6},{8,9},{9,8},{10,11... | collective-permute-start | bytes 1572872 | tf_op jit(solution)/shard_map/cond/branch_1_fun/ppermute | solution.py:396
  33.0 6.3 %collective-permute-start.3 = (bf16[320,256]{1,0:T(8,128)(2,1)S(1)}, bf16[320,256]{1,0:T(8,128)(2,1)}, u32[]{:S(2)}, u32[]{:S(2)}) collective-permute-start(bf16[320,256]{1,0:T(8,128)(2,1)S(1)} %get-tuple-element.54), channel_id=1, source_target_pairs={{0,2},{2,0},{1,3},{3,1},{4,6},{6,4},{5,7},{7,5},{8,10},{10,8},{9,1... | collective-permute-start | bytes 491528 | tf_op jit(solution)/shard_map/cond/branch_1_fun/ppermute | solution.py:396
  39.4 1.9 %collective-permute-start.13 = (bf16[3,288,256]{2,1,0:T(8,128)(2,1)S(1)}, bf16[3,288,256]{2,1,0:T(8,128)(2,1)S(1)}, u32[]{:S(2)}, u32[]{:S(2)}) collective-permute-start(bf16[3,288,256]{2,1,0:T(8,128)(2,1)S(1)} %pad_maximum_fusion), channel_id=1, source_target_pairs={{0,1},{1,0},{2,3},{3,2},{4,5},{5,4},{6,7},{7,6},{8,9},{9,8},{10,11... | collective-permute-start | bytes 1327112 | tf_op jit(solution)/shard_map/ppermute | solution.py:396
  39.5 2.2 %collective-permute-start.14 = (bf16[320,256]{1,0:T(8,128)(2,1)}, bf16[320,256]{1,0:T(8,128)(2,1)S(1)}, u32[]{:S(2)}, u32[]{:S(2)}) collective-permute-start(bf16[320,256]{1,0:T(8,128)(2,1)} %get-tuple-element.97.refs_7_), channel_id=1, source_target_pairs={{0,1},{1,0},{2,3},{3,2},{4,5},{5,4},{6,7},{7,6},{8,9},{9,8},{10,11... | collective-permute-start | bytes 491528 | tf_op jit(solution)/shard_map/ppermute | solution.py:396

commit v4 on v3

--- a/solution.py
+++ b/solution.py
@@ -440,7 +440,7 @@
         return jnp.where(kept, within, 4 + within)
 
     index, starts = index_table(where, near_row, near_col, far_row, far_col)
-    apart = near_row[0] >= 0
+    apart = where[0] >= 0
 
     def cluster_of(cluster, owner, core):
         return cluster
@@ -470,7 +470,8 @@
     to_two, to_one, own, by_cluster = stage(
         apart, back_half, packed, across, coupling, near_block
     )
-    to_two, to_one, *incoming = lax.optimization_barrier((to_two, to_one, *incoming))
+    to_two, *pair = lax.optimization_barrier((to_two, *incoming[:2]))
+    to_one, *incoming = lax.optimization_barrier((to_one, *pair, incoming[2]))
     back_two = lax.ppermute(to_two, axes, by_core)
     back_one = lax.ppermute(to_one, "clu", opposite)
     incoming = jnp.concatenate(incoming, axis=0)
@@ -500,23 +501,17 @@
         apart, forward_half, packed, incoming, incoming_other, by_cluster, near_block
     )
 
-    def between_subs(payload, own_rows, own):
-        own = jnp.where(
-            jnp.arange(2)[:, None, None] == core, own, swap(own, "rep")
-        )
-        return swap(payload, "sub"), own_rows + swap(own_rows, "rep"), own
-
-    from_sub, near, own = stage(apart, between_subs, payload, own_rows, own)
-    back_two, back_one, near = lax.optimization_barrier((back_two, back_one, near))
-    from_sub_other = swap(from_sub, "rep")
+    from_sub = swap(payload, "sub")
     backs = jnp.concatenate([back_two, back_one], axis=0)
     backs_other = swap(backs, "rep")
+    own_other, own_rows_other = swap(own, "rep"), swap(own_rows, "rep")
+    from_sub_other = swap(from_sub.astype(jnp.float32), "rep")
     return finish(
         index,
         packed,
-        (own, backs[:2], backs_other[:2]),
-        ((backs[2:],), (backs_other[2:],)),
-        (near,),
+        (backs[:2], backs_other[:2]),
+        ((own, backs[2:]), (own_other, backs_other[2:])),
+        (own_rows, own_rows_other),
         (far,),
         (from_sub, from_sub_other),
     )

time: 44.2 us -> 42.5 us (0.962)
  waiting for transfers between devices: 8.48 us -> 6.35 us
  starting transfers between devices: 13.7 us -> 15.3 us
  between operations: 0.77 us -> 0.12 us
    ppermute x10, waiting for transfers between devices: 8.47 us -> 4.41 us  [swap(): return lax.ppermute(value, axis, [(0, 1), (1, 0)])]
    ppermute x10, starting transfers between devices: 5.61 us -> 7.94 us  [swap(): return lax.ppermute(value, axis, [(0, 1), (1, 0)])]
    ppermute x1, waiting for transfers between devices: 0.01 us -> 1.93 us  [shards_small(): back_one = lax.ppermute(to_one, 'clu', opposite)]
    ppermute x1, starting transfers between devices: 5.11 us -> 3.6 us  [shards_small(): incoming.append(lax.ppermute(mine, 'clu', opposite))]
    ppermute x1, starting transfers between devices: 0.87 us -> 1.71 us  [shards_small(): back_one = lax.ppermute(to_one, 'clu', opposite)]
  transfers between devices with their start and end apart: 15 -> 15, of which waited for: 7 -> 4; matrix products, arithmetic and copies ran while one was open for 3% -> 3% of each run, Pallas kernels for 35% -> 36%
where the time goes in v4:
time: 42.5 us; the launch traced here: 42.3 us
  Pallas kernels  18.8 us (44%)
  starting transfers between devices  15.3 us (36%)
  waiting for transfers between devices  6.35 us (15%)
  local copies, waits for them, and re-layouts  1.26 us (3%)
    ppermute x10, starting transfers between devices, swap(): return lax.ppermute(value, axis, [(0, 1), (1, 0)])  7.94 us
    ppermute x10, waiting for transfers between devices, swap(): return lax.ppermute(value, axis, [(0, 1), (1, 0)])  4.41 us
    pallas_call x1, Pallas kernels, forward_far(): pl.pallas_call(functools.partial(forward_kernel, plan, turns, starts), ou...  4.25 us
    pallas_call x1, Pallas kernels, back_sums(): pl.pallas_call(functools.partial(back_kernel, plan, slot_of, starts), out...  3.8 us
    pallas_call x1, Pallas kernels, load(): pl.pallas_call(functools.partial(load_kernel, slot_of, starts), out_shape...  3.75 us
    ppermute x1, starting transfers between devices, shards_small(): incoming.append(lax.ppermute(mine, 'clu', opposite))  3.6 us
    ppermute x2, starting transfers between devices, shards_small(): incoming = [lax.ppermute(packed[c:c + 1], axes, by_core) for c in range(2)]  2.09 us
    pallas_call x1, Pallas kernels, finish(): pl.pallas_call(functools.partial(finish_kernel, tuple((len(group) for gro...  2.01 us
  transfers between devices with their start and end apart: 15, of which 4 were waited for; matrix products, arithmetic and copies ran while one was open for 3% of the time, Pallas kernels for 36%

profile of v4, /device:TPU:0, one launch (start us, length us, event | category | flops | bytes accessed | tf_op | source)
XLA Modules:
  0.0 42.3 jit_solution(1238106542507148103)
XLA Ops:
  0.0 0.1 pad_add_fusion.index
  0.1 1.7 %shard_map.83 = (bf16[2,288,256]{2,1,0:T(8,128)(2,1)S(1)}, bf16[1,288,256]{2,1,0:T(8,128)(2,1)S(1)}) custom-call(s32[3]{0:T(128)S(1)} %pad_add_fusion.index, bf16[2,256,256]{2,1,0:T(8,128)(2,1)} %panel.1, bf16[2,32,256]{2,1,0:T(8,128)(2,1)} %bitcast.4), custom_call_target="tpu_custom_call" | custom-call | tf_op jit(solution)/shard_map/pallas_call | solution.py:121
  1.8 3.0 %collective-permute-start.3 = (bf16[1,288,256]{2,1,0:T(8,128)(2,1)S(1)}, bf16[1,288,256]{2,1,0:T(8,128)(2,1)S(1)}, u32[]{:S(2)}, u32[]{:S(2)}) collective-permute-start(bf16[1,288,256]{2,1,0:T(8,128)(2,1)S(1)} %get-tuple-element.63), channel_id=1, source_target_pairs={{0,2},{2,0},{1,3},{3,1},{4,6},{6,4},{5,7},{7,5},{8,10},{10,8},{9,1... | collective-permute-start | bytes 442376 | tf_op jit(solution)/shard_map/ppermute | solution.py:396
  4.8 1.6 %collective-permute-start.4 = (bf16[1,288,256]{2,1,0:T(8,128)(2,1)S(1)}, bf16[1,288,256]{2,1,0:T(8,128)(2,1)S(1)}, u32[]{:S(2)}, u32[]{:S(2)}) collective-permute-start(bf16[1,288,256]{2,1,0:T(8,128)(2,1)S(1)} %get-tuple-element.83), channel_id=1, source_target_pairs={{0,4},{1,9},{2,6},{3,11},{4,0},{5,13},{6,2},{7,15},{8,12},{9,1},{1... | collective-permute-start | bytes 442376 | tf_op jit(solution)/shard_map/ppermute | solution.py:430
  6.4 0.4 %collective-permute-start.5 = (bf16[1,288,256]{2,1,0:T(8,128)(2,1)S(1)}, bf16[1,288,256]{2,1,0:T(8,128)(2,1)S(1)}, u32[]{:S(2)}, u32[]{:S(2)}) collective-permute-start(bf16[1,288,256]{2,1,0:T(8,128)(2,1)S(1)} %get-tuple-element.82), channel_id=1, source_target_pairs={{0,4},{1,9},{2,6},{3,11},{4,0},{5,13},{6,2},{7,15},{8,12},{9,1},{1... | collective-permute-start | bytes 442376 | tf_op jit(solution)/shard_map/ppermute | solution.py:430
  6.9 3.6 %collective-permute-start.7 = (bf16[1,288,256]{2,1,0:T(8,128)(2,1)S(1)}, bf16[1,288,256]{2,1,0:T(8,128)(2,1)S(1)}, u32[]{:S(2)}, u32[]{:S(2)}) collective-permute-start(bf16[1,288,256]{2,1,0:T(8,128)(2,1)S(1)} %get-tuple-element.63), channel_id=1, source_target_pairs={{0,12},{4,8},{8,4},{12,0},{1,13},{5,9},{9,5},{13,1},{2,14},{6,10},... | collective-permute-start | bytes 442376 | tf_op jit(solution)/shard_map/ppermute | solution.py:431
  10.5 0.8 %concatenate.10.index = s32[119]{0:T(128)S(1)} concatenate(s32[1]{0:T(128)} %bitcast, s32[1]{0:T(128)} %bitcast.1, s32[1]{0:T(128)} %bitcast.2, s32[26]{0:T(128)} %param.13, s32[26]{0:T(128)} %param.14, s32[32]{0:T(128)} %param.17, s32[32]{0:T(128)} %param.18), dimensions={0} | concatenate | bytes 952 | tf_op jit(solution)/shard_map/concatenate | solution.py:414
  11.3 11.0 %conditional.2 = (bf16[2,288,256]{2,1,0:T(8,128)(2,1)S(1)}, bf16[1,288,256]{2,1,0:T(8,128)(2,1)S(1)}, f32[1,288,256]{2,1,0:T(8,128)S(1)}, f32[64,256]{1,0:T(8,128)S(1)}) conditional(s32[]{:T(128)} %convert_element_type.13, () %tuple.23, (s32[119]{0:T(128)S(1)}, f32[32,32,32]{2,1,0:T(8,128)}, bf16[26,512,256]{2,1,0:T(8,128)(2,1)}, ...), branch_computations={%region_0.0_spmd, %region_1.0_spmd} | conditional | flops 516096 | bytes 11288716 | solution.py:401
  11.3 3.7 %branch_1_fun.6 = (bf16[26,512,256]{2,1,0:T(8,128)(2,1)S(1)}, f32[64,256]{1,0:T(8,128)S(1)}) custom-call(s32[119]{0:T(128)S(1)} %get-tuple-element.27.index, f32[32,32,32]{2,1,0:T(8,128)} %get-tuple-element.79.coupling, bf16[26,512,256]{2,1,0:T(8,128)(2,1)} %get-tuple-element.29.block), custom_call_target="tpu_custom_call" | custom-call | tf_op jit(solution)/shard_map/cond/branch_1_fun/pallas_call | solution.py:65
  15.1 3.8 %branch_1_fun.7 = f32[8,288,256]{2,1,0:T(8,128)S(1)} custom-call(s32[119]{0:T(128)S(1)} %get-tuple-element.27.index, f32[64,256]{1,0:T(8,128)S(1)} %get-tuple-element.30.matrix, bf16[26,512,256]{2,1,0:T(8,128)(2,1)S(1)} %get-tuple-element.31.block, bf16[2,288,256]{2,1,0:T(8,128)(2,1)S(1)} %get-tuple-element.32.refs_0_, ...), custom_call_target="tpu_custom_call" | custom-call | tf_op jit(solution)/shard_map/cond/branch_1_fun/pallas_call | solution.py:201
  18.9 0.1 slice.38
  19.0 0.6 %collective-permute-start.2 = (f32[4,288,256]{2,1,0:T(8,128)S(1)}, f32[4,288,256]{2,1,0:T(8,128)S(1)}, u32[]{:S(2)}, u32[]{:S(2)}) collective-permute-start(f32[4,288,256]{2,1,0:T(8,128)S(1)} %slice.38), channel_id=1, source_target_pairs={{0,1},{1,0},{2,3},{3,2},{4,5},{5,4},{6,7},{7,6},{8,9},{9,8},{10,11... | collective-permute-start | bytes 3538952 | tf_op jit(solution)/shard_map/cond/branch_1_fun/ppermute | solution.py:396
  19.6 0.3 copy-done
  20.0 0.8 %branch_1_fun.8 = f32[64,256]{1,0:T(8,128)S(1)} custom-call(s32[119]{0:T(128)S(1)} %get-tuple-element.27.index, f32[32,32,32]{2,1,0:T(8,128)S(1)} %copy-done), custom_call_target="tpu_custom_call" | custom-call | tf_op jit(solution)/shard_map/cond/branch_1_fun/pallas_call | solution.py:90
  20.8 1.4 %collective-permute-done.2 = f32[4,288,256]{2,1,0:T(8,128)S(1)} collective-permute-done((f32[4,288,256]{2,1,0:T(8,128)S(1)}, f32[4,288,256]{2,1,0:T(8,128)S(1)}, u32[]{:S(2)}, u32[]{:S(2)}) %collective-permute-start.2) | collective-permute-done | bytes 1179680 | tf_op jit(solution)/shard_map/cond/branch_1_fun/ppermute | solution.py:396
  22.1 0.1 slice_add_fusion.1
  22.2 0.1 fusion
  22.4 0.4 %collective-permute-start.11 = (bf16[3,288,256]{2,1,0:T(8,128)(2,1)S(1)}, bf16[3,288,256]{2,1,0:T(8,128)(2,1)S(1)}, u32[]{:S(2)}, u32[]{:S(2)}) collective-permute-start(bf16[3,288,256]{2,1,0:T(8,128)(2,1)S(1)} %constant_dynamic-update-slice_fusion), channel_id=1, source_target_pairs={{0,1},{1,0},{2,3},{3,2},{4,5},{5,4},{6,7},{7,6},{8,9},{9,8},{10,11... | collective-permute-start | bytes 1327112 | tf_op jit(solution)/shard_map/ppermute | solution.py:396
  22.8 1.7 %collective-permute-start.8 = (bf16[1,288,256]{2,1,0:T(8,128)(2,1)S(1)}, bf16[1,288,256]{2,1,0:T(8,128)(2,1)S(1)}, u32[]{:S(2)}, u32[]{:S(2)}) collective-permute-start(bf16[1,288,256]{2,1,0:T(8,128)(2,1)S(1)} %get-tuple-element.69), channel_id=1, source_target_pairs={{0,12},{4,8},{8,4},{12,0},{1,13},{5,9},{9,5},{13,1},{2,14},{6,10},... | collective-permute-start | bytes 442376 | tf_op jit(solution)/shard_map/ppermute | solution.py:476
  24.5 7.0 %conditional.3 = (bf16[320,256]{1,0:T(8,128)(2,1)S(1)}, f32[2,32,256]{2,1,0:T(8,128)S(1)}, f32[2,256,256]{2,1,0:T(8,128)S(1)}) conditional(s32[]{:T(128)} %convert_element_type.13, () %tuple.27, (s32[119]{0:T(128)S(1)}, f32[64,256]{1,0:T(8,128)S(1)}, bf16[26,512,256]{2,1,0:T(8,128)(2,1)}, bf16[2,288,256]{2,1,0:T(8,128)(2,1)S(1)}, ...), branch_computations={%region_2.0_spmd, %region_3.0_spmd} | conditional | bytes 1310784 | solution.py:401
  24.5 4.3 %branch_1_fun.9 = (f32[320,256]{1,0:T(8,128)S(1)}, f32[320,256]{1,0:T(8,128)S(1)}, bf16[8,288,256]{2,1,0:T(8,128)(2,1)S(1)}, bf16[26,512,256]{2,1,0:T(8,128)(2,1)S(1)}) custom-call(s32[119]{0:T(128)S(1)} %get-tuple-element.34.index, f32[64,256]{1,0:T(8,128)S(1)} %get-tuple-element.35.matrix, bf16[26,512,256]{2,1,0:T(8,128)(2,1)} %get-tuple-element.36.block, ...), custom_call_target="tpu_custom_call" | custom-call | tf_op jit(solution)/shard_map/cond/branch_1_fun/pallas_call | solution.py:280
  28.8 0.1 collective-permute-start
  28.9 2.0 %branch_1_fun.11 = f32[2,256,256]{2,1,0:T(8,128)S(1)} custom-call(s32[119]{0:T(128)S(1)} %get-tuple-element.34.index, bf16[26,512,256]{2,1,0:T(8,128)(2,1)S(1)} %get-tuple-element.44.block, bf16[8,288,256]{2,1,0:T(8,128)(2,1)S(1)} %get-tuple-element.45.full), custom_call_target="tpu_custom_call" | custom-call | tf_op jit(solution)/shard_map/cond/branch_1_fun/pallas_call | solution.py:333
  30.9 0.6 %branch_1_fun.10 = (bf16[320,256]{1,0:T(8,128)(2,1)S(1)}, f32[2,32,256]{2,1,0:T(8,128)S(1)}) custom-call(s32[119]{0:T(128)S(1)} %get-tuple-element.34.index, f32[320,256]{1,0:T(8,128)S(1)} %get-tuple-element.40.keep, f32[320,256]{1,0:T(8,128)S(1)} %collective-permute-done.taken), custom_call_target="tpu_custom_call" | custom-call | tf_op jit(solution)/shard_map/cond/branch_1_fun/pallas_call | solution.py:315
  31.5 1.3 %collective-permute-start.13 = (bf16[320,256]{1,0:T(8,128)(2,1)S(1)}, bf16[320,256]{1,0:T(8,128)(2,1)S(1)}, u32[]{:S(2)}, u32[]{:S(2)}) collective-permute-start(bf16[320,256]{1,0:T(8,128)(2,1)S(1)} %get-tuple-element.77), channel_id=1, source_target_pairs={{0,2},{2,0},{1,3},{3,1},{4,6},{6,4},{5,7},{7,5},{8,10},{10,8},{9,1... | collective-permute-start | bytes 491528 | tf_op jit(solution)/shard_map/ppermute | solution.py:396
  32.8 0.2 collective-permute-start.12
  33.0 1.9 %collective-permute-done.8.refs_3_ = bf16[1,288,256]{2,1,0:T(8,128)(2,1)S(1)} collective-permute-done((bf16[1,288,256]{2,1,0:T(8,128)(2,1)S(1)}, bf16[1,288,256]{2,1,0:T(8,128)(2,1)S(1)}, u32[]{:S(2)}, u32[]{:S(2)}) %collective-permute-start.8) | collective-permute-done | bytes 147488 | tf_op jit(solution)/shard_map/ppermute | solution.py:476
  35.0 1.6 %collective-permute-start.9 = (bf16[3,288,256]{2,1,0:T(8,128)(2,1)S(1)}, bf16[3,288,256]{2,1,0:T(8,128)(2,1)S(1)}, u32[]{:S(2)}, u32[]{:S(2)}) collective-permute-start(bf16[3,288,256]{2,1,0:T(8,128)(2,1)S(1)} %pad_maximum_fusion), channel_id=1, source_target_pairs={{0,1},{1,0},{2,3},{3,2},{4,5},{5,4},{6,7},{7,6},{8,9},{9,8},{10,11... | collective-permute-start | bytes 1327112 | tf_op jit(solution)/shard_map/ppermute | solution.py:396
  36.6 1.5 %collective-permute-done.13.refs_9_ = bf16[320,256]{1,0:T(8,128)(2,1)S(1)} collective-permute-done((bf16[320,256]{1,0:T(8,128)(2,1)S(1)}, bf16[320,256]{1,0:T(8,128)(2,1)S(1)}, u32[]{:S(2)}, u32[]{:S(2)}) %collective-permute-start.13) | collective-permute-done | bytes 163872 | tf_op jit(solution)/shard_map/ppermute | solution.py:396
  38.2 0.5 %collective-permute-start.10 = (f32[1,288,256]{2,1,0:T(8,128)S(1)}, f32[1,288,256]{2,1,0:T(8,128)S(1)}, u32[]{:S(2)}, u32[]{:S(2)}) collective-permute-start(f32[1,288,256]{2,1,0:T(8,128)S(1)} %get-tuple-element.70.refs_2_), channel_id=1, source_target_pairs={{0,1},{1,0},{2,3},{3,2},{4,5},{5,4},{6,7},{7,6},{8,9},{9,8},{10,11... | collective-permute-start | bytes 884744 | tf_op jit(solution)/shard_map/ppermute | solution.py:396
  38.8 1.5 %collective-permute-done.10.refs_4_ = f32[1,288,256]{2,1,0:T(8,128)S(1)} collective-permute-done((f32[1,288,256]{2,1,0:T(8,128)S(1)}, f32[1,288,256]{2,1,0:T(8,128)S(1)}, u32[]{:S(2)}, u32[]{:S(2)}) %collective-permute-start.10) | collective-permute-done | bytes 294944 | tf_op jit(solution)/shard_map/ppermute | solution.py:396
  40.3 2.0 %shard_map.84 = f32[2,256,256]{2,1,0:T(8,128)} custom-call(s32[119]{0:T(128)S(1)} %concatenate.10.index, bf16[2,288,256]{2,1,0:T(8,128)(2,1)S(1)} %get-tuple-element.62.packed, bf16[2,288,256]{2,1,0:T(8,128)(2,1)S(1)} %collective-permute-done.6.refs_0_, bf16[2,288,256]{2,1,0:T(8,128)(2,1)S(1)} %slice.44.refs_1_, ...), custom_call_target="tpu_custom_call" | custom-call | tf_op jit(solution)/shard_map/pallas_call | solution.py:382
  (23 shorter events, 0.3 us)
Async XLA Ops:
  1.8 9.5 %collective-permute-start.3 = (bf16[1,288,256]{2,1,0:T(8,128)(2,1)S(1)}, bf16[1,288,256]{2,1,0:T(8,128)(2,1)S(1)}, u32[]{:S(2)}, u32[]{:S(2)}) collective-permute-start(bf16[1,288,256]{2,1,0:T(8,128)(2,1)S(1)} %get-tuple-element.63), channel_id=1, source_target_pairs={{0,2},{2,0},{1,3},{3,1},{4,6},{6,4},{5,7},{7,5},{8,10},{10,8},{9,1... | collective-permute-start | bytes 442376 | tf_op jit(solution)/shard_map/ppermute | solution.py:396
  4.8 17.5 %collective-permute-start.4 = (bf16[1,288,256]{2,1,0:T(8,128)(2,1)S(1)}, bf16[1,288,256]{2,1,0:T(8,128)(2,1)S(1)}, u32[]{:S(2)}, u32[]{:S(2)}) collective-permute-start(bf16[1,288,256]{2,1,0:T(8,128)(2,1)S(1)} %get-tuple-element.83), channel_id=1, source_target_pairs={{0,4},{1,9},{2,6},{3,11},{4,0},{5,13},{6,2},{7,15},{8,12},{9,1},{1... | collective-permute-start | bytes 442376 | tf_op jit(solution)/shard_map/ppermute | solution.py:430
  6.4 15.9 %collective-permute-start.5 = (bf16[1,288,256]{2,1,0:T(8,128)(2,1)S(1)}, bf16[1,288,256]{2,1,0:T(8,128)(2,1)S(1)}, u32[]{:S(2)}, u32[]{:S(2)}) collective-permute-start(bf16[1,288,256]{2,1,0:T(8,128)(2,1)S(1)} %get-tuple-element.82), channel_id=1, source_target_pairs={{0,4},{1,9},{2,6},{3,11},{4,0},{5,13},{6,2},{7,15},{8,12},{9,1},{1... | collective-permute-start | bytes 442376 | tf_op jit(solution)/shard_map/ppermute | solution.py:430
  6.9 15.4 %collective-permute-start.7 = (bf16[1,288,256]{2,1,0:T(8,128)(2,1)S(1)}, bf16[1,288,256]{2,1,0:T(8,128)(2,1)S(1)}, u32[]{:S(2)}, u32[]{:S(2)}) collective-permute-start(bf16[1,288,256]{2,1,0:T(8,128)(2,1)S(1)} %get-tuple-element.63), channel_id=1, source_target_pairs={{0,12},{4,8},{8,4},{12,0},{1,13},{5,9},{9,5},{13,1},{2,14},{6,10},... | collective-permute-start | bytes 442376 | tf_op jit(solution)/shard_map/ppermute | solution.py:431
  11.3 3.8 %collective-permute-start.1 = (bf16[1,288,256]{2,1,0:T(8,128)(2,1)S(1)}, bf16[1,288,256]{2,1,0:T(8,128)(2,1)S(1)}, u32[]{:S(2)}, u32[]{:S(2)}) collective-permute-start(bf16[1,288,256]{2,1,0:T(8,128)(2,1)S(1)} %get-tuple-element.33.refs_1_), channel_id=1, source_target_pairs={{0,1},{1,0},{2,3},{3,2},{4,5},{5,4},{6,7},{7,6},{8,9},{9,8},{10,11... | collective-permute-start | bytes 442376 | tf_op jit(solution)/shard_map/cond/branch_1_fun/ppermute | solution.py:396
  18.9 1.0 %copy-start = (f32[32,32,32]{2,1,0:T(8,128)S(1)}, f32[32,32,32]{2,1,0:T(8,128)}, u32[]{:S(2)}) copy-start(f32[32,32,32]{2,1,0:T(8,128)} %get-tuple-element.79.coupling) | copy-start | bytes 393220 | tf_op jit(solution)/shard_map/cond
  19.0 3.1 %collective-permute-start.2 = (f32[4,288,256]{2,1,0:T(8,128)S(1)}, f32[4,288,256]{2,1,0:T(8,128)S(1)}, u32[]{:S(2)}, u32[]{:S(2)}) collective-permute-start(f32[4,288,256]{2,1,0:T(8,128)S(1)} %slice.38), channel_id=1, source_target_pairs={{0,1},{1,0},{2,3},{3,2},{4,5},{5,4},{6,7},{7,6},{8,9},{9,8},{10,11... | collective-permute-start | bytes 3538952 | tf_op jit(solution)/shard_map/cond/branch_1_fun/ppermute | solution.py:396
  22.4 2.2 %collective-permute-start.11 = (bf16[3,288,256]{2,1,0:T(8,128)(2,1)S(1)}, bf16[3,288,256]{2,1,0:T(8,128)(2,1)S(1)}, u32[]{:S(2)}, u32[]{:S(2)}) collective-permute-start(bf16[3,288,256]{2,1,0:T(8,128)(2,1)S(1)} %constant_dynamic-update-slice_fusion), channel_id=1, source_target_pairs={{0,1},{1,0},{2,3},{3,2},{4,5},{5,4},{6,7},{7,6},{8,9},{9,8},{10,11... | collective-permute-start | bytes 1327112 | tf_op jit(solution)/shard_map/ppermute | solution.py:396
  22.8 12.2 %collective-permute-start.6 = (bf16[2,288,256]{2,1,0:T(8,128)(2,1)S(1)}, bf16[2,288,256]{2,1,0:T(8,128)(2,1)S(1)}, u32[]{:S(2)}, u32[]{:S(2)}) collective-permute-start(bf16[2,288,256]{2,1,0:T(8,128)(2,1)S(1)} %get-tuple-element.65), channel_id=1, source_target_pairs={{0,4},{1,9},{2,6},{3,11},{4,0},{5,13},{6,2},{7,15},{8,12},{9,1},{1... | collective-permute-start | bytes 884744 | tf_op jit(solution)/shard_map/ppermute | solution.py:475
  22.8 12.2 %collective-permute-start.8 = (bf16[1,288,256]{2,1,0:T(8,128)(2,1)S(1)}, bf16[1,288,256]{2,1,0:T(8,128)(2,1)S(1)}, u32[]{:S(2)}, u32[]{:S(2)}) collective-permute-start(bf16[1,288,256]{2,1,0:T(8,128)(2,1)S(1)} %get-tuple-element.69), channel_id=1, source_target_pairs={{0,12},{4,8},{8,4},{12,0},{1,13},{5,9},{9,5},{13,1},{2,14},{6,10},... | collective-permute-start | bytes 442376 | tf_op jit(solution)/shard_map/ppermute | solution.py:476
  28.8 2.1 %collective-permute-start = (f32[320,256]{1,0:T(8,128)S(1)}, f32[320,256]{1,0:T(8,128)S(1)}, u32[]{:S(2)}, u32[]{:S(2)}) collective-permute-start(f32[320,256]{1,0:T(8,128)S(1)} %get-tuple-element.41), channel_id=1, source_target_pairs={{0,1},{1,0},{2,3},{3,2},{4,5},{5,4},{6,7},{7,6},{8,9},{9,8},{10,11... | collective-permute-start | bytes 983048 | tf_op jit(solution)/shard_map/cond/branch_1_fun/ppermute | solution.py:396
  31.5 6.6 %collective-permute-start.13 = (bf16[320,256]{1,0:T(8,128)(2,1)S(1)}, bf16[320,256]{1,0:T(8,128)(2,1)S(1)}, u32[]{:S(2)}, u32[]{:S(2)}) collective-permute-start(bf16[320,256]{1,0:T(8,128)(2,1)S(1)} %get-tuple-element.77), channel_id=1, source_target_pairs={{0,2},{2,0},{1,3},{3,1},{4,6},{6,4},{5,7},{7,5},{8,10},{10,8},{9,1... | collective-permute-start | bytes 491528 | tf_op jit(solution)/shard_map/ppermute | solution.py:396
  32.8 7.5 %collective-permute-start.12 = (f32[2,256,256]{2,1,0:T(8,128)S(1)}, f32[2,256,256]{2,1,0:T(8,128)S(1)}, u32[]{:S(2)}, u32[]{:S(2)}) collective-permute-start(f32[2,256,256]{2,1,0:T(8,128)S(1)} %get-tuple-element.75.refs_6_), channel_id=1, source_target_pairs={{0,1},{1,0},{2,3},{3,2},{4,5},{5,4},{6,7},{7,6},{8,9},{9,8},{10,11... | collective-permute-start | bytes 1572872 | tf_op jit(solution)/shard_map/ppermute | solution.py:396
  35.0 3.7 %collective-permute-start.9 = (bf16[3,288,256]{2,1,0:T(8,128)(2,1)S(1)}, bf16[3,288,256]{2,1,0:T(8,128)(2,1)S(1)}, u32[]{:S(2)}, u32[]{:S(2)}) collective-permute-start(bf16[3,288,256]{2,1,0:T(8,128)(2,1)S(1)} %pad_maximum_fusion), channel_id=1, source_target_pairs={{0,1},{1,0},{2,3},{3,2},{4,5},{5,4},{6,7},{7,6},{8,9},{9,8},{10,11... | collective-permute-start | bytes 1327112 | tf_op jit(solution)/shard_map/ppermute | solution.py:396
  38.2 2.1 %collective-permute-start.14 = (f32[320,256]{1,0:T(8,128)S(1)}, f32[320,256]{1,0:T(8,128)S(1)}, u32[]{:S(2)}, u32[]{:S(2)}) collective-permute-start(f32[320,256]{1,0:T(8,128)S(1)} %convert_element_type.14), channel_id=1, source_target_pairs={{0,1},{1,0},{2,3},{3,2},{4,5},{5,4},{6,7},{7,6},{8,9},{9,8},{10,11... | collective-permute-start | bytes 983048 | tf_op jit(solution)/shard_map/ppermute | solution.py:396
  38.2 2.0 %collective-permute-start.10 = (f32[1,288,256]{2,1,0:T(8,128)S(1)}, f32[1,288,256]{2,1,0:T(8,128)S(1)}, u32[]{:S(2)}, u32[]{:S(2)}) collective-permute-start(f32[1,288,256]{2,1,0:T(8,128)S(1)} %get-tuple-element.70.refs_2_), channel_id=1, source_target_pairs={{0,1},{1,0},{2,3},{3,2},{4,5},{5,4},{6,7},{7,6},{8,9},{9,8},{10,11... | collective-permute-start | bytes 884744 | tf_op jit(solution)/shard_map/ppermute | solution.py:396

commit v5 on v4

--- a/solution.py
+++ b/solution.py
@@ -7,7 +7,6 @@
 from jax.experimental.pallas import tpu as pltpu
 from jax.sharding import PartitionSpec as P
 
-HIGHEST = lax.Precision.HIGHEST
 LAST = (((1,), (1,)), ((), ()))
 FIRST = (((0,), (0,)), ((), ()))
 VMEM = pl.BlockSpec(memory_space=pltpu.VMEM)
@@ -20,7 +19,29 @@
     return pltpu.with_memory_space_constraint(array, pltpu.HBM)
 
 
-PARTS = 3
+PARTS = 4
+
+
+class Scalars:
+    def __init__(self, sources, held, sems):
+        self.held = held
+        self.copies = [
+            pltpu.make_async_copy(source, target, sems.at[k])
+            for k, (source, target) in enumerate(zip(sources, held))
+        ]
+        for copy in self.copies:
+            copy.start()
+
+    def wait(self):
+        for copy in self.copies:
+            copy.wait()
+        return self.held
+
+
+def scalar_scratch(*arrays):
+    return [pltpu.SMEM(array.shape, jnp.int32) for array in arrays] + [
+        pltpu.SemaphoreType.DMA((len(arrays),))
+    ]
 
 
 def parts_of(block, held, sems):
@@ -35,24 +56,25 @@
     ]
 
 
-def load_kernel(slot_of, starts, index, coupling, block, held, matrix, couplings, table, sems, sem):
+def load_kernel(far_row, far_col, coupling, block, held, matrix, couplings, table, sems, sem, *scratch):
     parts = parts_of(block, held, sems)
+    for _, copy in parts:
+        copy.start()
     first = pltpu.make_async_copy(coupling, couplings, sem)
     first.start()
-    for _, copy in parts:
-        copy.start()
+    scalars = Scalars((far_row, far_col), scratch[:2], scratch[2])
     table[...] = jnp.zeros_like(table)
+    rows, columns = scalars.wait()
     first.wait()
-    sum_couplings(slot_of, starts, index, couplings, matrix, table)
+    sum_couplings(rows, columns, couplings, matrix, table)
     for _, copy in parts:
         copy.wait()
 
 
-def sum_couplings(slot_of, starts, index, coupling, matrix, table):
-    _, _, far_row, far_col = starts
+def sum_couplings(far_row, far_col, coupling, matrix, table):
     rank = coupling.shape[1]
     for f in range(coupling.shape[0]):
-        at = (index[far_row + f], slot_of(index[far_col + f], index[0], index[2]))
+        at = (far_row[f], far_col[f])
         table[at] = table[at] + coupling[f]
     for c in range(table.shape[0]):
         matrix[c * rank : (c + 1) * rank, :] = jnp.concatenate(
@@ -60,41 +82,25 @@
         )
 
 
-def load(slots, slot_of, index, starts, coupling, block):
+def load(slots, far_row, far_col, coupling, block):
     rank = coupling.shape[1]
     return pl.pallas_call(
-        functools.partial(load_kernel, slot_of, starts),
+        load_kernel,
         out_shape=(
             jax.ShapeDtypeStruct(block.shape, block.dtype),
             jax.ShapeDtypeStruct((2 * rank, slots * rank), jnp.float32),
         ),
-        in_specs=[SMEM, ANY, ANY],
+        in_specs=[ANY] * 4,
         out_specs=(VMEM, VMEM),
         scratch_shapes=[
             pltpu.VMEM(coupling.shape, coupling.dtype),
             pltpu.VMEM((2, slots, rank, rank), jnp.float32),
             pltpu.SemaphoreType.DMA((PARTS,)),
             pltpu.SemaphoreType.DMA,
+            *scalar_scratch(far_row, far_col),
         ],
         compiler_params=ROOM,
-    )(index, in_hbm(coupling), in_hbm(block))
-
-
-def matrix_kernel(slot_of, starts, index, coupling, matrix, table):
-    table[...] = jnp.zeros_like(table)
-    sum_couplings(slot_of, starts, index, coupling, matrix, table)
-
-
-def couplings_by(slots, slot_of, index, starts, coupling):
-    rank = coupling.shape[1]
-    return pl.pallas_call(
-        functools.partial(matrix_kernel, slot_of, starts),
-        out_shape=jax.ShapeDtypeStruct((2 * rank, slots * rank), jnp.float32),
-        in_specs=[SMEM, VMEM],
-        out_specs=VMEM,
-        scratch_shapes=[pltpu.VMEM((2, slots, rank, rank), jnp.float32)],
-        compiler_params=ROOM,
-    )(index, coupling)
+    )(in_hbm(far_row), in_hbm(far_col), in_hbm(coupling), in_hbm(block))
 
 
 def pack_kernel(index, panel, bases, packed, mine, held, sems):
@@ -134,27 +140,42 @@
     )(index, in_hbm(panel), in_hbm(bases))
 
 
+def parts_in_bfloat16(value, count):
+    out = []
+    for _ in range(count):
+        out.append(value.astype(jnp.bfloat16))
+        value = value - out[-1].astype(jnp.float32)
+    return out
+
+
+def product_in_parts(left, right, dims):
+    (inner_left,), (inner_right,) = dims[0]
+    left_high, left_low = parts_in_bfloat16(left, 2)
+    right_high, right_low = parts_in_bfloat16(right, 2)
+    return lax.dot_general(
+        jnp.concatenate([left_high, left_high, left_low], axis=inner_left),
+        jnp.concatenate([right_high, right_low, right_high], axis=inner_right),
+        dims,
+        preferred_element_type=jnp.float32,
+    )
+
+
 def each_pair(pairs, step):
-    unroll = 13 if pairs % 13 == 0 else 1
-
-    def several(n, carry):
-        for k in range(unroll):
-            step(n * unroll + k)
-        return carry
-
-    lax.fori_loop(0, pairs // unroll, several, 0)
-
-
-def back_kernel(plan, slot_of, starts, index, matrix, block, *refs):
+    for q in range(pairs):
+        step(q)
+
+
+def back_kernel(plan, slot_of, where, near_row, near_col, matrix, block, *refs):
     n = len(plan)
     pieces = refs[:n]
-    total, full = refs[n:]
-    near_row, near_col, _, _ = starts
+    total, full, *scratch = refs[n:]
+    scalars = Scalars((where, near_row, near_col), scratch[:3], scratch[3])
     panels = block.shape[2]
     clusters, rows = full.shape[:2]
     rank = matrix.shape[0] // clusters
     width = rows - rank
     total[:, :width, :] = jnp.zeros((total.shape[0], width, panels), jnp.float32)
+    index, near_row, near_col = scalars.wait()
     for piece, where in zip(pieces, plan):
         first, sub = where(index[0], index[1], index[2])
         for c in range(piece.shape[0]):
@@ -168,30 +189,25 @@
         ],
         axis=0,
     )
-    weights = lax.dot_general(
-        matrix[...],
-        projection,
-        FIRST,
-        precision=HIGHEST,
-        preferred_element_type=jnp.float32,
-    )
+    weights = product_in_parts(matrix[...], projection, FIRST)
     for t in range(total.shape[0]):
+        slot = slot_of(t, index[0], index[2])
         for i in range(width // panels):
-            total[t, width + i * rank : width + (i + 1) * rank, :] = weights[
+            total[slot, width + i * rank : width + (i + 1) * rank, :] = weights[
                 t * rank : (t + 1) * rank, i * panels : (i + 1) * panels
             ]
 
     def step(q):
         product = jnp.dot(
-            full[index[near_row + q], :width, :], block[q], preferred_element_type=jnp.float32
-        )
-        slot = slot_of(index[near_col + q], index[0], index[2])
+            full[near_row[q], :width, :], block[q], preferred_element_type=jnp.float32
+        )
+        slot = slot_of(near_col[q], index[0], index[2])
         total[slot, :width, :] += product.astype(jnp.bfloat16).astype(jnp.float32)
 
     each_pair(block.shape[0], step)
 
 
-def back_sums(slots, slot_of, pieces, index, starts, matrix, block):
+def back_sums(slots, slot_of, pieces, where, near_row, near_col, matrix, block):
     rows = pieces[0][0].shape[1]
     _, full_panels, panels = block.shape
     rank = matrix.shape[1] // slots
@@ -199,23 +215,25 @@
     tall = width + rank * (width // panels)
     plan = tuple(where for _, where in pieces)
     return pl.pallas_call(
-        functools.partial(back_kernel, plan, slot_of, starts),
+        functools.partial(back_kernel, plan, slot_of),
         out_shape=jax.ShapeDtypeStruct((slots, tall, panels), jnp.float32),
-        in_specs=[SMEM] + [VMEM] * (2 + len(pieces)),
+        in_specs=[ANY] * 3 + [VMEM] * (2 + len(pieces)),
         out_specs=VMEM,
-        scratch_shapes=[pltpu.VMEM((2, rows, full_panels), jnp.bfloat16)],
+        scratch_shapes=[
+            pltpu.VMEM((2, rows, full_panels), jnp.bfloat16),
+            *scalar_scratch(where, near_row, near_col),
+        ],
         compiler_params=ROOM,
-    )(index, matrix, block, *[p for p, _ in pieces])
-
-
-def forward_step(turns, index, starts, block, full, total):
-    near_row, near_col, _, _ = starts
+    )(where, in_hbm(near_row), in_hbm(near_col), matrix, block, *[p for p, _ in pieces])
+
+
+def forward_step(turns, index, near_row, near_col, block, full, total):
     rows, panels = total.shape[1] // len(turns), block.shape[2]
     subs = block.shape[1] // panels
 
     def step(q):
-        field = full[index[near_col + q], : total.shape[2], :]
-        row = index[near_row + q]
+        field = full[near_col[q], : total.shape[2], :]
+        row = near_row[q]
         for k, turn in enumerate(turns):
             at = lax.rem(index[1] + turn, subs)
             product = lax.dot_general(
@@ -229,16 +247,19 @@
     return step
 
 
-def forward_kernel(plan, turns, starts, index, matrix, block, *refs):
+def forward_kernel(plan, turns, where, near_row, near_col, matrix, block, *refs):
     n = len(plan)
     pieces = refs[:n]
-    keep, give, full, held, total, sems = refs[n:]
+    keep, give, full, held, total, sems, *scratch = refs[n:]
+    scalars = Scalars((where, near_row, near_col), scratch[:3], scratch[3])
     parts = parts_of(block, held, sems)
     for _, copy in parts:
         copy.start()
     slots, rows, _ = full.shape
     rank = matrix.shape[1] // slots
     width = rows - rank
+    total[...] = jnp.zeros_like(total)
+    index, near_row, near_col = scalars.wait()
     for piece, where in zip(pieces, plan):
         firsts = where(index[0], index[1], index[2])
         for c, first in enumerate(firsts):
@@ -252,11 +273,8 @@
         ],
         axis=0,
     )
-    weights = jnp.dot(
-        matrix[...], projection, precision=HIGHEST, preferred_element_type=jnp.float32
-    )
-    total[...] = jnp.zeros_like(total)
-    step = forward_step(turns, index, starts, held, full, total)
+    weights = product_in_parts(matrix[...], projection, (((1,), (0,)), ((), ())))
+    step = forward_step(turns, index, near_row, near_col, held, full, total)
     for pairs, copy in parts:
         copy.wait()
         for q in pairs:
@@ -268,7 +286,7 @@
     give[tall:, :] = weights
 
 
-def forward_far(slots, pieces, index, starts, matrix, block):
+def forward_far(slots, pieces, where, near_row, near_col, matrix, block):
     rows = pieces[0][0].shape[1]
     _, full_panels, panels = block.shape
     rank = matrix.shape[1] // slots
@@ -278,21 +296,22 @@
     tall = panels * len(turns)
     shape = jax.ShapeDtypeStruct((tall + 2 * rank, width), jnp.float32)
     return pl.pallas_call(
-        functools.partial(forward_kernel, plan, turns, starts),
+        functools.partial(forward_kernel, plan, turns),
         out_shape=(
             shape,
             shape,
             jax.ShapeDtypeStruct((slots, rows, panels), jnp.bfloat16),
             jax.ShapeDtypeStruct(block.shape, block.dtype),
         ),
-        in_specs=[SMEM, VMEM, ANY] + [VMEM] * len(pieces),
+        in_specs=[ANY] * 3 + [VMEM, ANY] + [VMEM] * len(pieces),
         out_specs=(VMEM,) * 4,
         scratch_shapes=[
             pltpu.VMEM((2, tall, width), jnp.float32),
             pltpu.SemaphoreType.DMA((PARTS,)),
+            *scalar_scratch(where, near_row, near_col),
         ],
         compiler_params=ROOM,
-    )(index, matrix, in_hbm(block), *[p for p, _ in pieces])
+    )(where, in_hbm(near_row), in_hbm(near_col), matrix, in_hbm(block), *[p for p, _ in pieces])
 
 
 def merge_kernel(index, keep, taken, payload, far):
@@ -324,19 +343,24 @@
     )(index, keep, taken)
 
 
-def own_kernel(starts, index, block, full, total):
+def own_kernel(where, near_row, near_col, block, full, total, *scratch):
+    scalars = Scalars((where, near_row, near_col), scratch[:3], scratch[3])
     total[...] = jnp.zeros_like(total)
-    each_pair(block.shape[0], forward_step((0,), index, starts, block, full, total))
-
-
-def forward_own(index, starts, block, full, width):
+    index, near_row, near_col = scalars.wait()
+    each_pair(
+        block.shape[0], forward_step((0,), index, near_row, near_col, block, full, total)
+    )
+
+
+def forward_own(where, near_row, near_col, block, full, width):
     return pl.pallas_call(
-        functools.partial(own_kernel, starts),
+        own_kernel,
         out_shape=jax.ShapeDtypeStruct((2, block.shape[2], width), jnp.float32),
-        in_specs=[SMEM, VMEM, VMEM],
+        in_specs=[ANY] * 3 + [VMEM, VMEM],
         out_specs=VMEM,
+        scratch_shapes=scalar_scratch(where, near_row, near_col),
         compiler_params=ROOM,
-    )(index, block, full)
+    )(where, in_hbm(near_row), in_hbm(near_col), block, full)
 
 
 def finish_kernel(counts, index, packed, *refs):
@@ -369,10 +393,9 @@
                 c, width + i * rank : width + (i + 1) * rank, :
             ]
         result[c] += back[c, :width, :].T + lax.dot_general(
-            packed[c, width:, :].astype(jnp.float32),
-            weight[c],
+            jnp.concatenate([packed[c, width:, :]] * 3, axis=0),
+            jnp.concatenate(parts_in_bfloat16(weight[c], 3), axis=0),
             FIRST,
-            precision=HIGHEST,
             preferred_element_type=jnp.float32,
         )
 
@@ -406,14 +429,6 @@
     )
 
 
-def index_table(where, *columns):
-    starts, at = [], where.shape[0]
-    for column in columns:
-        starts.append(at)
-        at += column.shape[0]
-    return jnp.concatenate([where, *columns]), starts
-
-
 def shards_small(panel_field, near_row, near_col, near_block, bases, far_row, far_col, coupling):
     owner, sub, core = lax.axis_index("clu"), lax.axis_index("sub"), lax.axis_index("rep")
     where = jnp.stack([owner, sub, core]).astype(jnp.int32)
@@ -439,15 +454,11 @@
         within = jnp.where(paired, local, jnp.where(turn == 3, 2, 3))
         return jnp.where(kept, within, 4 + within)
 
-    index, starts = index_table(where, near_row, near_col, far_row, far_col)
     apart = where[0] >= 0
 
-    def cluster_of(cluster, owner, core):
-        return cluster
-
-    def back_half(packed, across, coupling, block):
+    def back_half(packed, across, near_row, near_col, far_row, far_col, coupling, block):
         across_other = swap(across, "rep")
-        held, by_slot = load(8, slot_of, index, starts, coupling, block)
+        held, matrix = load(8, far_row, far_col, coupling, block)
         total = back_sums(
             8,
             slot_of,
@@ -456,19 +467,28 @@
                 (across, lambda o, s, r: (r, 1 - s)),
                 (across_other, lambda o, s, r: (1 - r, 1 - s)),
             ],
-            index,
-            starts,
-            by_slot,
+            where,
+            near_row,
+            near_col,
+            matrix,
             held,
         )
         taken = swap(total[4:], "rep")
         to_two = (total[:2] + taken[:2]).astype(jnp.bfloat16)
         to_one = (total[2:3] + taken[2:3]).astype(jnp.bfloat16)
-        by_cluster = couplings_by(8, cluster_of, index, starts, coupling)
-        return to_two, to_one, total[3:4] + taken[3:], by_cluster
-
-    to_two, to_one, own, by_cluster = stage(
-        apart, back_half, packed, across, coupling, near_block
+        return to_two, to_one, total[3:4] + taken[3:], matrix
+
+    to_two, to_one, own, matrix = stage(
+        apart,
+        back_half,
+        packed,
+        across,
+        near_row,
+        near_col,
+        far_row,
+        far_col,
+        coupling,
+        near_block,
     )
     to_two, *pair = lax.optimization_barrier((to_two, *incoming[:2]))
     to_one, *incoming = lax.optimization_barrier((to_one, *pair, incoming[2]))
@@ -477,7 +497,7 @@
     incoming = jnp.concatenate(incoming, axis=0)
     incoming_other = swap(incoming, "rep")
 
-    def forward_half(packed, incoming, incoming_other, matrix, block):
+    def forward_half(packed, incoming, incoming_other, matrix, near_row, near_col, block):
         ahead, behind, full, held = forward_far(
             8,
             [
@@ -488,26 +508,36 @@
                     lambda o, s, r: (2 * (o ^ (2 - r)),) * 2 + (2 * (o ^ 3) + 1 - r - 2,),
                 ),
             ],
-            index,
-            starts,
+            where,
+            near_row,
+            near_col,
             matrix,
             block,
         )
-        own_rows = forward_own(index, starts, held, full, width)
-        payload, far = to_other_sub(index, ahead, swap(behind, "rep"), panels)
+        own_rows = forward_own(where, near_row, near_col, held, full, width)
+        payload, far = to_other_sub(where, ahead, swap(behind, "rep"), panels)
         return payload, far, own_rows
 
     payload, far, own_rows = stage(
-        apart, forward_half, packed, incoming, incoming_other, by_cluster, near_block
+        apart,
+        forward_half,
+        packed,
+        incoming,
+        incoming_other,
+        matrix,
+        near_row,
+        near_col,
+        near_block,
     )
 
     from_sub = swap(payload, "sub")
     backs = jnp.concatenate([back_two, back_one], axis=0)
     backs_other = swap(backs, "rep")
     own_other, own_rows_other = swap(own, "rep"), swap(own_rows, "rep")
+    own_other, from_sub = lax.optimization_barrier((own_other, from_sub))
     from_sub_other = swap(from_sub.astype(jnp.float32), "rep")
     return finish(
-        index,
+        where,
         packed,
         (backs[:2], backs_other[:2]),
         ((own, backs[2:]), (own_other, backs_other[2:])),
@@ -526,26 +556,26 @@
     around = lax.all_gather(packed, "sub", axis=0)
     gathered = lax.all_gather(packed, "clu", axis=0, tiled=True)
     slots = owners * clusters
-    index, starts = index_table(where, near_row, near_col, far_row, far_col)
     def slot_of(cluster, owner, core):
         return cluster
 
-    held, matrix = load(slots, slot_of, index, starts, coupling, near_block)
+    held, matrix = load(slots, far_row, far_col, coupling, near_block)
     back = back_sums(
         slots,
         slot_of,
         [(around[k], lambda o, s, r, k=k: (0, k)) for k in range(subs)],
-        index,
-        starts,
+        where,
+        near_row,
+        near_col,
         matrix,
         held,
     )
     back = lax.psum(lax.psum_scatter(back, "clu", scatter_dimension=0, tiled=True), "rep")
     ahead, behind, full, held = forward_far(
-        slots, [(gathered, lambda o, s, r: (0,) * slots)], index, starts, matrix, near_block
+        slots, [(gathered, lambda o, s, r: (0,) * slots)], where, near_row, near_col, matrix, near_block
     )
     taken = swap(behind, "rep")
-    near = forward_own(index, starts, held, full, width)
+    near = forward_own(where, near_row, near_col, held, full, width)
     near = near + swap(near, "rep")
     far = lax.psum((ahead + taken)[(subs - 1) * panels :], "sub").reshape(clusters, -1, width)
     ahead = (ahead + taken)[: (subs - 1) * panels]
@@ -558,7 +588,7 @@
         near = near + jnp.where(core == 0, jnp.stack([got, swap(got, "rep")]), jnp.stack([swap(got, "rep"), got]))
     single = lax.dynamic_slice_in_dim(back, core, 1, axis=0)
     other = lax.dynamic_slice_in_dim(back, 1 - core, 1, axis=0)
-    return finish(index, packed, (), ((single,), (other,)), (near,), (far,), ())
+    return finish(where, packed, (), ((single,), (other,)), (near,), (far,), ())
 
 
 def shards(*arrays):

time: 42.5 us -> 41 us (0.965)
  Pallas kernels: 18.8 us -> 16.1 us
  waiting for transfers between devices: 6.35 us -> 8.13 us
  local copies, waits for them, and re-layouts: 1.26 us -> 0.18 us
  starting transfers between devices: 15.3 us -> 15.9 us
    pallas_call x5 -> x4, Pallas kernels: 14.6 us -> 12.1 us  [the longest x1 3.58 us: forward_far(): pl.pallas_call(functools.partial(forward_kernel, plan, turns), out_shape=...]
    ppermute x10, waiting for transfers between devices: 4.41 us -> 6 us  [swap(): return lax.ppermute(value, axis, [(0, 1), (1, 0)])]
    ppermute x1, starting transfers between devices: 1.71 us -> 3.08 us  [shards_small(): back_one = lax.ppermute(to_one, 'clu', opposite)]
    ppermute x10, starting transfers between devices: 7.94 us -> 6.79 us  [swap(): return lax.ppermute(value, axis, [(0, 1), (1, 0)])]
    concatenate x1 -> x0, local copies, waits for them, and re-layouts: 0.78 us -> none  [index_table(): return (jnp.concatenate([where, *columns]), starts)]
  transfers between devices with their start and end apart: 15 -> 15, of which waited for: 4 -> 4; matrix products, arithmetic and copies ran while one was open for 3% -> 1% of each run, Pallas kernels for 36% -> 31%
where the time goes in v5:
time: 41 us; the launch traced here: 40.8 us
  Pallas kernels  16.1 us (39%)
  starting transfers between devices  15.9 us (39%)
  waiting for transfers between devices  8.13 us (20%)
    ppermute x10, starting transfers between devices, swap(): return lax.ppermute(value, axis, [(0, 1), (1, 0)])  6.79 us
    ppermute x10, waiting for transfers between devices, swap(): return lax.ppermute(value, axis, [(0, 1), (1, 0)])  6 us
    ppermute x1, starting transfers between devices, shards_small(): incoming.append(lax.ppermute(mine, 'clu', opposite))  3.6 us
    pallas_call x1, Pallas kernels, forward_far(): pl.pallas_call(functools.partial(forward_kernel, plan, turns), out_shape=...  3.58 us
    pallas_call x1, Pallas kernels, load(): pl.pallas_call(load_kernel, out_shape=(jax.ShapeDtypeStruct(block.shape,...  3.39 us
    pallas_call x1, Pallas kernels, back_sums(): pl.pallas_call(functools.partial(back_kernel, plan, slot_of), out_shape=j...  3.26 us
    ppermute x1, starting transfers between devices, shards_small(): back_one = lax.ppermute(to_one, 'clu', opposite)  3.08 us
    ppermute x1, waiting for transfers between devices, shards_small(): back_one = lax.ppermute(to_one, 'clu', opposite)  2.13 us
  transfers between devices with their start and end apart: 15, of which 4 were waited for; matrix products, arithmetic and copies ran while one was open for 1% of the time, Pallas kernels for 31%

profile of v5, /device:TPU:0, one launch (start us, length us, event | category | flops | bytes accessed | tf_op | source)
XLA Modules:
  0.0 40.8 jit_solution(13159402156696140215)
XLA Ops:
  0.0 0.1 pad_add_fusion.index
  0.1 1.7 %shard_map.85 = (bf16[2,288,256]{2,1,0:T(8,128)(2,1)S(1)}, bf16[1,288,256]{2,1,0:T(8,128)(2,1)S(1)}) custom-call(s32[3]{0:T(128)S(1)} %pad_add_fusion.index, bf16[2,256,256]{2,1,0:T(8,128)(2,1)} %panel.1, bf16[2,32,256]{2,1,0:T(8,128)(2,1)} %bitcast.4), custom_call_target="tpu_custom_call" | custom-call | tf_op jit(solution)/shard_map/pallas_call | solution.py:127
  1.8 3.0 %collective-permute-start.3 = (bf16[1,288,256]{2,1,0:T(8,128)(2,1)S(1)}, bf16[1,288,256]{2,1,0:T(8,128)(2,1)S(1)}, u32[]{:S(2)}, u32[]{:S(2)}) collective-permute-start(bf16[1,288,256]{2,1,0:T(8,128)(2,1)S(1)} %get-tuple-element.83), channel_id=1, source_target_pairs={{0,2},{2,0},{1,3},{3,1},{4,6},{6,4},{5,7},{7,5},{8,10},{10,8},{9,1... | collective-permute-start | bytes 442376 | tf_op jit(solution)/shard_map/ppermute | solution.py:419
  4.8 1.6 %collective-permute-start.4 = (bf16[1,288,256]{2,1,0:T(8,128)(2,1)S(1)}, bf16[1,288,256]{2,1,0:T(8,128)(2,1)S(1)}, u32[]{:S(2)}, u32[]{:S(2)}) collective-permute-start(bf16[1,288,256]{2,1,0:T(8,128)(2,1)S(1)} %get-tuple-element.109), channel_id=1, source_target_pairs={{0,4},{1,9},{2,6},{3,11},{4,0},{5,13},{6,2},{7,15},{8,12},{9,1},{1... | collective-permute-start | bytes 442376 | tf_op jit(solution)/shard_map/ppermute | solution.py:445
  6.4 0.4 %collective-permute-start.5 = (bf16[1,288,256]{2,1,0:T(8,128)(2,1)S(1)}, bf16[1,288,256]{2,1,0:T(8,128)(2,1)S(1)}, u32[]{:S(2)}, u32[]{:S(2)}) collective-permute-start(bf16[1,288,256]{2,1,0:T(8,128)(2,1)S(1)} %get-tuple-element.108), channel_id=1, source_target_pairs={{0,4},{1,9},{2,6},{3,11},{4,0},{5,13},{6,2},{7,15},{8,12},{9,1},{1... | collective-permute-start | bytes 442376 | tf_op jit(solution)/shard_map/ppermute | solution.py:445
  6.9 3.6 %collective-permute-start.7 = (bf16[1,288,256]{2,1,0:T(8,128)(2,1)S(1)}, bf16[1,288,256]{2,1,0:T(8,128)(2,1)S(1)}, u32[]{:S(2)}, u32[]{:S(2)}) collective-permute-start(bf16[1,288,256]{2,1,0:T(8,128)(2,1)S(1)} %get-tuple-element.83), channel_id=1, source_target_pairs={{0,12},{4,8},{8,4},{12,0},{1,13},{5,9},{9,5},{13,1},{2,14},{6,10},... | collective-permute-start | bytes 442376 | tf_op jit(solution)/shard_map/ppermute | solution.py:446
  10.5 10.1 %conditional.2 = (bf16[2,288,256]{2,1,0:T(8,128)(2,1)S(1)}, bf16[1,288,256]{2,1,0:T(8,128)(2,1)S(1)}, f32[1,288,256]{2,1,0:T(8,128)S(1)}, f32[64,256]{1,0:T(8,128)S(1)}) conditional(s32[]{:T(128)} %convert_element_type.13, () %tuple.24, (s32[32]{0:T(128)}, s32[32]{0:T(128)}, f32[32,32,32]{2,1,0:T(8,128)}, bf16[26,512,256]{2,1,0:T(8,128)(2,1)}, ...), branch_computations={%region_0.0_spmd, %region_1.0_spmd} | conditional | flops 516096 | bytes 11288744 | solution.py:424
  10.5 0.0 collective-permute-start.1
  10.5 3.4 %branch_1_fun.5 = (bf16[26,512,256]{2,1,0:T(8,128)(2,1)S(1)}, f32[64,256]{1,0:T(8,128)S(1)}) custom-call(s32[32]{0:T(128)} %get-tuple-element.103.far_row, s32[32]{0:T(128)} %get-tuple-element.104.far_col, f32[32,32,32]{2,1,0:T(8,128)} %get-tuple-element.105.coupling, bf16[26,512,256]{2,1,0:T(8,128)(2,1)} %get-tuple-element.45.block), custom_call_target="tpu_custom_call" | custom-call | tf_op jit(solution)/shard_map/cond/branch_1_fun/pallas_call | solution.py:87
  13.9 0.0 copy-start
  13.9 3.3 %branch_1_fun.6 = f32[8,288,256]{2,1,0:T(8,128)S(1)} custom-call(s32[3]{0:T(128)S(1)} %get-tuple-element.39.where, s32[26]{0:T(128)} %get-tuple-element.40.near_row, s32[26]{0:T(128)} %get-tuple-element.41.near_col, f32[64,256]{1,0:T(8,128)S(1)} %get-tuple-element.117.matrix, bf16[26,512,256]{2,1,0:T(8,128)(2,1)S(1)} %get-tuple-element.47.block, ...), custom_call_target="tpu_custom_call" | custom-call | tf_op jit(solution)/shard_map/cond/branch_1_fun/pallas_call | solution.py:217
  17.2 0.1 slice.38
  17.3 0.0 copy-start.1
  17.3 0.6 %collective-permute-start.2 = (f32[4,288,256]{2,1,0:T(8,128)S(1)}, f32[4,288,256]{2,1,0:T(8,128)S(1)}, u32[]{:S(2)}, u32[]{:S(2)}) collective-permute-start(f32[4,288,256]{2,1,0:T(8,128)S(1)} %slice.38), channel_id=1, source_target_pairs={{0,1},{1,0},{2,3},{3,2},{4,5},{5,4},{6,7},{7,6},{8,9},{9,8},{10,11... | collective-permute-start | bytes 3538952 | tf_op jit(solution)/shard_map/cond/branch_1_fun/ppermute | solution.py:419
  17.9 2.5 %collective-permute-done.2 = f32[4,288,256]{2,1,0:T(8,128)S(1)} collective-permute-done((f32[4,288,256]{2,1,0:T(8,128)S(1)}, f32[4,288,256]{2,1,0:T(8,128)S(1)}, u32[]{:S(2)}, u32[]{:S(2)}) %collective-permute-start.2) | collective-permute-done | bytes 1179680 | tf_op jit(solution)/shard_map/cond/branch_1_fun/ppermute | solution.py:419
  20.4 0.1 slice_add_fusion.1
  20.5 0.1 fusion
  20.7 0.4 %collective-permute-start.11 = (bf16[3,288,256]{2,1,0:T(8,128)(2,1)S(1)}, bf16[3,288,256]{2,1,0:T(8,128)(2,1)S(1)}, u32[]{:S(2)}, u32[]{:S(2)}) collective-permute-start(bf16[3,288,256]{2,1,0:T(8,128)(2,1)S(1)} %constant_dynamic-update-slice_fusion), channel_id=1, source_target_pairs={{0,1},{1,0},{2,3},{3,2},{4,5},{5,4},{6,7},{7,6},{8,9},{9,8},{10,11... | collective-permute-start | bytes 1327112 | tf_op jit(solution)/shard_map/ppermute | solution.py:419
  21.1 0.3 collective-permute-start.6
  21.4 3.1 %collective-permute-start.8 = (bf16[1,288,256]{2,1,0:T(8,128)(2,1)S(1)}, bf16[1,288,256]{2,1,0:T(8,128)(2,1)S(1)}, u32[]{:S(2)}, u32[]{:S(2)}) collective-permute-start(bf16[1,288,256]{2,1,0:T(8,128)(2,1)S(1)} %get-tuple-element.89), channel_id=1, source_target_pairs={{0,12},{4,8},{8,4},{12,0},{1,13},{5,9},{9,5},{13,1},{2,14},{6,10},... | collective-permute-start | bytes 442376 | tf_op jit(solution)/shard_map/ppermute | solution.py:496
  24.5 6.7 %conditional.3 = (bf16[320,256]{1,0:T(8,128)(2,1)S(1)}, f32[2,32,256]{2,1,0:T(8,128)S(1)}, f32[2,256,256]{2,1,0:T(8,128)S(1)}) conditional(s32[]{:T(128)} %convert_element_type.13, () %tuple.28, (s32[3]{0:T(128)S(1)}, s32[26]{0:T(128)}, s32[26]{0:T(128)}, f32[64,256]{1,0:T(8,128)S(1)}, bf16[26,512,256]{2,1,0:T(8,128)(2,1)}, ...), branch_computations={%region_2.0_spmd, %region_3.0_spmd} | conditional | bytes 1310784 | solution.py:424
  24.5 3.6 %branch_1_fun.7 = (f32[320,256]{1,0:T(8,128)S(1)}, f32[320,256]{1,0:T(8,128)S(1)}, bf16[8,288,256]{2,1,0:T(8,128)(2,1)S(1)}, bf16[26,512,256]{2,1,0:T(8,128)(2,1)S(1)}) custom-call(s32[3]{0:T(128)S(1)} %get-tuple-element.50.where.index, s32[26]{0:T(128)} %get-tuple-element.51.near_row, s32[26]{0:T(128)} %get-tuple-element.52.near_col, ...), custom_call_target="tpu_custom_call" | custom-call | tf_op jit(solution)/shard_map/cond/branch_1_fun/pallas_call | solution.py:298
  28.1 0.6 %collective-permute-start = (f32[320,256]{1,0:T(8,128)S(1)}, f32[320,256]{1,0:T(8,128)S(1)}, u32[]{:S(2)}, u32[]{:S(2)}) collective-permute-start(f32[320,256]{1,0:T(8,128)S(1)} %get-tuple-element.59), channel_id=1, source_target_pairs={{0,1},{1,0},{2,3},{3,2},{4,5},{5,4},{6,7},{7,6},{8,9},{9,8},{10,11... | collective-permute-start | bytes 983048 | tf_op jit(solution)/shard_map/cond/branch_1_fun/ppermute | solution.py:419
  28.7 1.9 %branch_1_fun.9 = f32[2,256,256]{2,1,0:T(8,128)S(1)} custom-call(s32[3]{0:T(128)S(1)} %get-tuple-element.50.where.index, s32[26]{0:T(128)} %get-tuple-element.51.near_row, s32[26]{0:T(128)} %get-tuple-element.52.near_col, bf16[26,512,256]{2,1,0:T(8,128)(2,1)S(1)} %get-tuple-element.62.block, bf16[8,288,256]{2,1,0:T(8,128)(2,1)S(1)} %get-tuple-element.63.full), custom_call_target="tpu_custom_call" | custom-call | tf_op jit(solution)/shard_map/cond/branch_1_fun/pallas_call | solution.py:356
  30.6 0.6 %branch_1_fun.8 = (bf16[320,256]{1,0:T(8,128)(2,1)S(1)}, f32[2,32,256]{2,1,0:T(8,128)S(1)}) custom-call(s32[3]{0:T(128)S(1)} %get-tuple-element.50.where.index, f32[320,256]{1,0:T(8,128)S(1)} %get-tuple-element.58.keep, f32[320,256]{1,0:T(8,128)S(1)} %collective-permute-done.taken), custom_call_target="tpu_custom_call" | custom-call | tf_op jit(solution)/shard_map/cond/branch_1_fun/pallas_call | solution.py:334
  31.2 0.6 %collective-permute-start.12 = (bf16[320,256]{1,0:T(8,128)(2,1)S(1)}, bf16[320,256]{1,0:T(8,128)(2,1)S(1)}, u32[]{:S(2)}, u32[]{:S(2)}) collective-permute-start(bf16[320,256]{1,0:T(8,128)(2,1)S(1)} %get-tuple-element.95), channel_id=1, source_target_pairs={{0,2},{2,0},{1,3},{3,1},{4,6},{6,4},{5,7},{7,5},{8,10},{10,8},{9,1... | collective-permute-start | bytes 491528 | tf_op jit(solution)/shard_map/ppermute | solution.py:419
  31.8 2.1 %collective-permute-done.8.refs_3_ = bf16[1,288,256]{2,1,0:T(8,128)(2,1)S(1)} collective-permute-done((bf16[1,288,256]{2,1,0:T(8,128)(2,1)S(1)}, bf16[1,288,256]{2,1,0:T(8,128)(2,1)S(1)}, u32[]{:S(2)}, u32[]{:S(2)}) %collective-permute-start.8) | collective-permute-done | bytes 147488 | tf_op jit(solution)/shard_map/ppermute | solution.py:496
  34.0 1.5 %collective-permute-start.9 = (bf16[3,288,256]{2,1,0:T(8,128)(2,1)S(1)}, bf16[3,288,256]{2,1,0:T(8,128)(2,1)S(1)}, u32[]{:S(2)}, u32[]{:S(2)}) collective-permute-start(bf16[3,288,256]{2,1,0:T(8,128)(2,1)S(1)} %pad_maximum_fusion), channel_id=1, source_target_pairs={{0,1},{1,0},{2,3},{3,2},{4,5},{5,4},{6,7},{7,6},{8,9},{9,8},{10,11... | collective-permute-start | bytes 1327112 | tf_op jit(solution)/shard_map/ppermute | solution.py:419
  35.4 1.9 %collective-permute-done.12.refs_9_ = bf16[320,256]{1,0:T(8,128)(2,1)S(1)} collective-permute-done((bf16[320,256]{1,0:T(8,128)(2,1)S(1)}, bf16[320,256]{1,0:T(8,128)(2,1)S(1)}, u32[]{:S(2)}, u32[]{:S(2)}) %collective-permute-start.12) | collective-permute-done | bytes 163872 | tf_op jit(solution)/shard_map/ppermute | solution.py:419
  37.4 0.1 collective-permute-start.14
  37.6 1.6 %collective-permute-done.14.refs_10_ = f32[320,256]{1,0:T(8,128)S(1)} collective-permute-done((f32[320,256]{1,0:T(8,128)S(1)}, f32[320,256]{1,0:T(8,128)S(1)}, u32[]{:S(2)}, u32[]{:S(2)}) %collective-permute-start.14) | collective-permute-done | bytes 327712 | tf_op jit(solution)/shard_map/ppermute | solution.py:419
  39.1 1.7 %shard_map.86 = f32[2,256,256]{2,1,0:T(8,128)} custom-call(s32[3]{0:T(128)S(1)} %pad_add_fusion.index, bf16[2,288,256]{2,1,0:T(8,128)(2,1)S(1)} %get-tuple-element.82.packed, bf16[2,288,256]{2,1,0:T(8,128)(2,1)S(1)} %collective-permute-done.6.refs_0_, bf16[2,288,256]{2,1,0:T(8,128)(2,1)S(1)} %slice.44.refs_1_, f32[1,288,256]{2,1,0:T(8,128)S(1)} %get-tuple-element.90.refs_2_, ...), custom_call_target="tpu_custom_call" | custom-call | tf_op jit(solution)/shard_map/pallas_call | solution.py:405
  (23 shorter events, 0.2 us)
Async XLA Ops:
  1.8 8.7 %collective-permute-start.3 = (bf16[1,288,256]{2,1,0:T(8,128)(2,1)S(1)}, bf16[1,288,256]{2,1,0:T(8,128)(2,1)S(1)}, u32[]{:S(2)}, u32[]{:S(2)}) collective-permute-start(bf16[1,288,256]{2,1,0:T(8,128)(2,1)S(1)} %get-tuple-element.83), channel_id=1, source_target_pairs={{0,2},{2,0},{1,3},{3,1},{4,6},{6,4},{5,7},{7,5},{8,10},{10,8},{9,1... | collective-permute-start | bytes 442376 | tf_op jit(solution)/shard_map/ppermute | solution.py:419
  4.8 15.8 %collective-permute-start.4 = (bf16[1,288,256]{2,1,0:T(8,128)(2,1)S(1)}, bf16[1,288,256]{2,1,0:T(8,128)(2,1)S(1)}, u32[]{:S(2)}, u32[]{:S(2)}) collective-permute-start(bf16[1,288,256]{2,1,0:T(8,128)(2,1)S(1)} %get-tuple-element.109), channel_id=1, source_target_pairs={{0,4},{1,9},{2,6},{3,11},{4,0},{5,13},{6,2},{7,15},{8,12},{9,1},{1... | collective-permute-start | bytes 442376 | tf_op jit(solution)/shard_map/ppermute | solution.py:445
  6.4 14.2 %collective-permute-start.5 = (bf16[1,288,256]{2,1,0:T(8,128)(2,1)S(1)}, bf16[1,288,256]{2,1,0:T(8,128)(2,1)S(1)}, u32[]{:S(2)}, u32[]{:S(2)}) collective-permute-start(bf16[1,288,256]{2,1,0:T(8,128)(2,1)S(1)} %get-tuple-element.108), channel_id=1, source_target_pairs={{0,4},{1,9},{2,6},{3,11},{4,0},{5,13},{6,2},{7,15},{8,12},{9,1},{1... | collective-permute-start | bytes 442376 | tf_op jit(solution)/shard_map/ppermute | solution.py:445
  6.9 13.7 %collective-permute-start.7 = (bf16[1,288,256]{2,1,0:T(8,128)(2,1)S(1)}, bf16[1,288,256]{2,1,0:T(8,128)(2,1)S(1)}, u32[]{:S(2)}, u32[]{:S(2)}) collective-permute-start(bf16[1,288,256]{2,1,0:T(8,128)(2,1)S(1)} %get-tuple-element.83), channel_id=1, source_target_pairs={{0,12},{4,8},{8,4},{12,0},{1,13},{5,9},{9,5},{13,1},{2,14},{6,10},... | collective-permute-start | bytes 442376 | tf_op jit(solution)/shard_map/ppermute | solution.py:446
  10.5 3.4 %collective-permute-start.1 = (bf16[1,288,256]{2,1,0:T(8,128)(2,1)S(1)}, bf16[1,288,256]{2,1,0:T(8,128)(2,1)S(1)}, u32[]{:S(2)}, u32[]{:S(2)}) collective-permute-start(bf16[1,288,256]{2,1,0:T(8,128)(2,1)S(1)} %get-tuple-element.49.refs_1_), channel_id=1, source_target_pairs={{0,1},{1,0},{2,3},{3,2},{4,5},{5,4},{6,7},{7,6},{8,9},{9,8},{10,11... | collective-permute-start | bytes 442376 | tf_op jit(solution)/shard_map/cond/branch_1_fun/ppermute | solution.py:419
  13.9 3.3 %copy-start = (f32[64,256]{1,0:T(8,128)}, f32[64,256]{1,0:T(8,128)S(1)}, u32[]{:S(2)}) copy-start(f32[64,256]{1,0:T(8,128)S(1)} %get-tuple-element.117.matrix) | copy-start | bytes 196612 | tf_op jit(solution)/shard_map/cond
  17.3 3.3 %copy-start.1 = (f32[64,256]{1,0:T(8,128)S(1)}, f32[64,256]{1,0:T(8,128)}, u32[]{:S(2)}) copy-start(f32[64,256]{1,0:T(8,128)} %copy-done) | copy-start | bytes 196612 | tf_op jit(solution)/shard_map/cond
  17.3 3.1 %collective-permute-start.2 = (f32[4,288,256]{2,1,0:T(8,128)S(1)}, f32[4,288,256]{2,1,0:T(8,128)S(1)}, u32[]{:S(2)}, u32[]{:S(2)}) collective-permute-start(f32[4,288,256]{2,1,0:T(8,128)S(1)} %slice.38), channel_id=1, source_target_pairs={{0,1},{1,0},{2,3},{3,2},{4,5},{5,4},{6,7},{7,6},{8,9},{9,8},{10,11... | collective-permute-start | bytes 3538952 | tf_op jit(solution)/shard_map/cond/branch_1_fun/ppermute | solution.py:419
  20.7 3.9 %collective-permute-start.11 = (bf16[3,288,256]{2,1,0:T(8,128)(2,1)S(1)}, bf16[3,288,256]{2,1,0:T(8,128)(2,1)S(1)}, u32[]{:S(2)}, u32[]{:S(2)}) collective-permute-start(bf16[3,288,256]{2,1,0:T(8,128)(2,1)S(1)} %constant_dynamic-update-slice_fusion), channel_id=1, source_target_pairs={{0,1},{1,0},{2,3},{3,2},{4,5},{5,4},{6,7},{7,6},{8,9},{9,8},{10,11... | collective-permute-start | bytes 1327112 | tf_op jit(solution)/shard_map/ppermute | solution.py:419
  21.1 12.8 %collective-permute-start.6 = (bf16[2,288,256]{2,1,0:T(8,128)(2,1)S(1)}, bf16[2,288,256]{2,1,0:T(8,128)(2,1)S(1)}, u32[]{:S(2)}, u32[]{:S(2)}) collective-permute-start(bf16[2,288,256]{2,1,0:T(8,128)(2,1)S(1)} %get-tuple-element.85), channel_id=1, source_target_pairs={{0,4},{1,9},{2,6},{3,11},{4,0},{5,13},{6,2},{7,15},{8,12},{9,1},{1... | collective-permute-start | bytes 884744 | tf_op jit(solution)/shard_map/ppermute | solution.py:495
  21.4 12.5 %collective-permute-start.8 = (bf16[1,288,256]{2,1,0:T(8,128)(2,1)S(1)}, bf16[1,288,256]{2,1,0:T(8,128)(2,1)S(1)}, u32[]{:S(2)}, u32[]{:S(2)}) collective-permute-start(bf16[1,288,256]{2,1,0:T(8,128)(2,1)S(1)} %get-tuple-element.89), channel_id=1, source_target_pairs={{0,12},{4,8},{8,4},{12,0},{1,13},{5,9},{9,5},{13,1},{2,14},{6,10},... | collective-permute-start | bytes 442376 | tf_op jit(solution)/shard_map/ppermute | solution.py:496
  24.5 10.9 %collective-permute-start.10 = (f32[1,288,256]{2,1,0:T(8,128)S(1)}, f32[1,288,256]{2,1,0:T(8,128)S(1)}, u32[]{:S(2)}, u32[]{:S(2)}) collective-permute-start(f32[1,288,256]{2,1,0:T(8,128)S(1)} %get-tuple-element.90.refs_2_), channel_id=1, source_target_pairs={{0,1},{1,0},{2,3},{3,2},{4,5},{5,4},{6,7},{7,6},{8,9},{9,8},{10,11... | collective-permute-start | bytes 884744 | tf_op jit(solution)/shard_map/ppermute | solution.py:419
  28.1 2.5 %collective-permute-start = (f32[320,256]{1,0:T(8,128)S(1)}, f32[320,256]{1,0:T(8,128)S(1)}, u32[]{:S(2)}, u32[]{:S(2)}) collective-permute-start(f32[320,256]{1,0:T(8,128)S(1)} %get-tuple-element.59), channel_id=1, source_target_pairs={{0,1},{1,0},{2,3},{3,2},{4,5},{5,4},{6,7},{7,6},{8,9},{9,8},{10,11... | collective-permute-start | bytes 983048 | tf_op jit(solution)/shard_map/cond/branch_1_fun/ppermute | solution.py:419
  31.2 6.2 %collective-permute-start.12 = (bf16[320,256]{1,0:T(8,128)(2,1)S(1)}, bf16[320,256]{1,0:T(8,128)(2,1)S(1)}, u32[]{:S(2)}, u32[]{:S(2)}) collective-permute-start(bf16[320,256]{1,0:T(8,128)(2,1)S(1)} %get-tuple-element.95), channel_id=1, source_target_pairs={{0,2},{2,0},{1,3},{3,1},{4,6},{6,4},{5,7},{7,5},{8,10},{10,8},{9,1... | collective-permute-start | bytes 491528 | tf_op jit(solution)/shard_map/ppermute | solution.py:419
  31.8 7.3 %collective-permute-start.13 = (f32[2,256,256]{2,1,0:T(8,128)S(1)}, f32[2,256,256]{2,1,0:T(8,128)S(1)}, u32[]{:S(2)}, u32[]{:S(2)}) collective-permute-start(f32[2,256,256]{2,1,0:T(8,128)S(1)} %get-tuple-element.97.refs_6_), channel_id=1, source_target_pairs={{0,1},{1,0},{2,3},{3,2},{4,5},{5,4},{6,7},{7,6},{8,9},{9,8},{10,11... | collective-permute-start | bytes 1572872 | tf_op jit(solution)/shard_map/ppermute | solution.py:419
  34.0 3.5 %collective-permute-start.9 = (bf16[3,288,256]{2,1,0:T(8,128)(2,1)S(1)}, bf16[3,288,256]{2,1,0:T(8,128)(2,1)S(1)}, u32[]{:S(2)}, u32[]{:S(2)}) collective-permute-start(bf16[3,288,256]{2,1,0:T(8,128)(2,1)S(1)} %pad_maximum_fusion), channel_id=1, source_target_pairs={{0,1},{1,0},{2,3},{3,2},{4,5},{5,4},{6,7},{7,6},{8,9},{9,8},{10,11... | collective-permute-start | bytes 1327112 | tf_op jit(solution)/shard_map/ppermute | solution.py:419
  37.4 1.7 %collective-permute-start.14 = (f32[320,256]{1,0:T(8,128)S(1)}, f32[320,256]{1,0:T(8,128)S(1)}, u32[]{:S(2)}, u32[]{:S(2)}) collective-permute-start(f32[320,256]{1,0:T(8,128)S(1)} %convert_element_type.14), channel_id=1, source_target_pairs={{0,1},{1,0},{2,3},{3,2},{4,5},{5,4},{6,7},{7,6},{8,9},{9,8},{10,11... | collective-permute-start | bytes 983048 | tf_op jit(solution)/shard_map/ppermute | solution.py:419

commit v6 on v5

--- a/solution.py
+++ b/solution.py
@@ -10,7 +10,6 @@
 LAST = (((1,), (1,)), ((), ()))
 FIRST = (((0,), (0,)), ((), ()))
 VMEM = pl.BlockSpec(memory_space=pltpu.VMEM)
-SMEM = pl.BlockSpec(memory_space=pltpu.SMEM)
 ANY = pl.BlockSpec(memory_space=pl.ANY)
 ROOM = pltpu.CompilerParams(vmem_limit_bytes=32 * 1024 * 1024)
 
@@ -20,6 +19,10 @@
 
 
 PARTS = 4
+
+
+def place():
+    return lax.axis_index("clu"), lax.axis_index("sub"), lax.axis_index("rep")
 
 
 class Scalars:
@@ -103,7 +106,7 @@
     )(in_hbm(far_row), in_hbm(far_col), in_hbm(coupling), in_hbm(block))
 
 
-def pack_kernel(index, panel, bases, packed, mine, held, sems):
+def pack_kernel(panel, bases, packed, mine, held, sems):
     clusters, _, width = panel.shape
     moves = []
     for c in range(clusters):
@@ -118,10 +121,10 @@
         packed[c, :width, :] = held[c].T
     for c in range(clusters):
         moves[2 * c + 1].wait()
-    mine[0] = packed[index[2]]
-
-
-def pack(index, panel, bases):
+    mine[0] = packed[place()[2]]
+
+
+def pack(panel, bases):
     clusters, panels, width = panel.shape
     rows = width + bases.shape[1]
     return pl.pallas_call(
@@ -130,14 +133,14 @@
             jax.ShapeDtypeStruct((clusters, rows, panels), panel.dtype),
             jax.ShapeDtypeStruct((1, rows, panels), panel.dtype),
         ),
-        in_specs=[SMEM, ANY, ANY],
+        in_specs=[ANY, ANY],
         out_specs=(VMEM, VMEM),
         scratch_shapes=[
             pltpu.VMEM(panel.shape, panel.dtype),
             pltpu.SemaphoreType.DMA((2 * clusters,)),
         ],
         compiler_params=ROOM,
-    )(index, in_hbm(panel), in_hbm(bases))
+    )(in_hbm(panel), in_hbm(bases))
 
 
 def parts_in_bfloat16(value, count):
@@ -165,17 +168,18 @@
         step(q)
 
 
-def back_kernel(plan, slot_of, where, near_row, near_col, matrix, block, *refs):
+def back_kernel(plan, slot_of, near_row, near_col, matrix, block, *refs):
     n = len(plan)
     pieces = refs[:n]
     total, full, *scratch = refs[n:]
-    scalars = Scalars((where, near_row, near_col), scratch[:3], scratch[3])
+    scalars = Scalars((near_row, near_col), scratch[:2], scratch[2])
     panels = block.shape[2]
     clusters, rows = full.shape[:2]
     rank = matrix.shape[0] // clusters
     width = rows - rank
     total[:, :width, :] = jnp.zeros((total.shape[0], width, panels), jnp.float32)
-    index, near_row, near_col = scalars.wait()
+    index = place()
+    near_row, near_col = scalars.wait()
     for piece, where in zip(pieces, plan):
         first, sub = where(index[0], index[1], index[2])
         for c in range(piece.shape[0]):
@@ -207,7 +211,7 @@
     each_pair(block.shape[0], step)
 
 
-def back_sums(slots, slot_of, pieces, where, near_row, near_col, matrix, block):
+def back_sums(slots, slot_of, pieces, near_row, near_col, matrix, block):
     rows = pieces[0][0].shape[1]
     _, full_panels, panels = block.shape
     rank = matrix.shape[1] // slots
@@ -217,14 +221,14 @@
     return pl.pallas_call(
         functools.partial(back_kernel, plan, slot_of),
         out_shape=jax.ShapeDtypeStruct((slots, tall, panels), jnp.float32),
-        in_specs=[ANY] * 3 + [VMEM] * (2 + len(pieces)),
+        in_specs=[ANY] * 2 + [VMEM] * (2 + len(pieces)),
         out_specs=VMEM,
         scratch_shapes=[
             pltpu.VMEM((2, rows, full_panels), jnp.bfloat16),
-            *scalar_scratch(where, near_row, near_col),
+            *scalar_scratch(near_row, near_col),
         ],
         compiler_params=ROOM,
-    )(where, in_hbm(near_row), in_hbm(near_col), matrix, block, *[p for p, _ in pieces])
+    )(in_hbm(near_row), in_hbm(near_col), matrix, block, *[p for p, _ in pieces])
 
 
 def forward_step(turns, index, near_row, near_col, block, full, total):
@@ -247,11 +251,11 @@
     return step
 
 
-def forward_kernel(plan, turns, where, near_row, near_col, matrix, block, *refs):
+def forward_kernel(plan, turns, near_row, near_col, matrix, block, *refs):
     n = len(plan)
     pieces = refs[:n]
     keep, give, full, held, total, sems, *scratch = refs[n:]
-    scalars = Scalars((where, near_row, near_col), scratch[:3], scratch[3])
+    scalars = Scalars((near_row, near_col), scratch[:2], scratch[2])
     parts = parts_of(block, held, sems)
     for _, copy in parts:
         copy.start()
@@ -259,7 +263,8 @@
     rank = matrix.shape[1] // slots
     width = rows - rank
     total[...] = jnp.zeros_like(total)
-    index, near_row, near_col = scalars.wait()
+    index = place()
+    near_row, near_col = scalars.wait()
     for piece, where in zip(pieces, plan):
         firsts = where(index[0], index[1], index[2])
         for c, first in enumerate(firsts):
@@ -286,7 +291,7 @@
     give[tall:, :] = weights
 
 
-def forward_far(slots, pieces, where, near_row, near_col, matrix, block):
+def forward_far(slots, pieces, near_row, near_col, matrix, block):
     rows = pieces[0][0].shape[1]
     _, full_panels, panels = block.shape
     rank = matrix.shape[1] // slots
@@ -303,21 +308,21 @@
             jax.ShapeDtypeStruct((slots, rows, panels), jnp.bfloat16),
             jax.ShapeDtypeStruct(block.shape, block.dtype),
         ),
-        in_specs=[ANY] * 3 + [VMEM, ANY] + [VMEM] * len(pieces),
+        in_specs=[ANY] * 2 + [VMEM, ANY] + [VMEM] * len(pieces),
         out_specs=(VMEM,) * 4,
         scratch_shapes=[
             pltpu.VMEM((2, tall, width), jnp.float32),
             pltpu.SemaphoreType.DMA((PARTS,)),
-            *scalar_scratch(where, near_row, near_col),
+            *scalar_scratch(near_row, near_col),
         ],
         compiler_params=ROOM,
-    )(where, in_hbm(near_row), in_hbm(near_col), matrix, in_hbm(block), *[p for p, _ in pieces])
-
-
-def merge_kernel(index, keep, taken, payload, far):
+    )(in_hbm(near_row), in_hbm(near_col), matrix, in_hbm(block), *[p for p, _ in pieces])
+
+
+def merge_kernel(keep, taken, payload, far):
     rank = far.shape[1]
     panels = keep.shape[0] - 2 * rank
-    core = index[2]
+    core = place()[2]
     for c in range(2):
         rows = slice(panels + c * rank, panels + (c + 1) * rank)
         far[c] = keep[rows, :] + taken[rows, :]
@@ -328,7 +333,7 @@
     payload[panels + rank :, :] = (weights - high.astype(jnp.float32)).astype(payload.dtype)
 
 
-def to_other_sub(index, keep, taken, panels):
+def to_other_sub(keep, taken, panels):
     rows, width = keep.shape
     rank = (rows - panels) // 2
     return pl.pallas_call(
@@ -337,37 +342,38 @@
             jax.ShapeDtypeStruct((rows, width), jnp.bfloat16),
             jax.ShapeDtypeStruct((2, rank, width), jnp.float32),
         ),
-        in_specs=[SMEM, VMEM, VMEM],
+        in_specs=[VMEM, VMEM],
         out_specs=(VMEM, VMEM),
         compiler_params=ROOM,
-    )(index, keep, taken)
-
-
-def own_kernel(where, near_row, near_col, block, full, total, *scratch):
-    scalars = Scalars((where, near_row, near_col), scratch[:3], scratch[3])
+    )(keep, taken)
+
+
+def own_kernel(near_row, near_col, block, full, total, *scratch):
+    scalars = Scalars((near_row, near_col), scratch[:2], scratch[2])
     total[...] = jnp.zeros_like(total)
-    index, near_row, near_col = scalars.wait()
+    index = place()
+    near_row, near_col = scalars.wait()
     each_pair(
         block.shape[0], forward_step((0,), index, near_row, near_col, block, full, total)
     )
 
 
-def forward_own(where, near_row, near_col, block, full, width):
+def forward_own(near_row, near_col, block, full, width):
     return pl.pallas_call(
         own_kernel,
         out_shape=jax.ShapeDtypeStruct((2, block.shape[2], width), jnp.float32),
-        in_specs=[ANY] * 3 + [VMEM, VMEM],
+        in_specs=[ANY] * 2 + [VMEM, VMEM],
         out_specs=VMEM,
-        scratch_shapes=scalar_scratch(where, near_row, near_col),
+        scratch_shapes=scalar_scratch(near_row, near_col),
         compiler_params=ROOM,
-    )(where, in_hbm(near_row), in_hbm(near_col), block, full)
-
-
-def finish_kernel(counts, index, packed, *refs):
+    )(in_hbm(near_row), in_hbm(near_col), block, full)
+
+
+def finish_kernel(counts, packed, *refs):
     refs = list(refs)
     both, backs, nears, fars, subs = ([refs.pop(0) for _ in range(count)] for count in counts)
     result, back, weight = refs
-    core = index[2]
+    core = place()[2]
     clusters, rows, panels = packed.shape
     width = result.shape[2]
     rank = rows - width
@@ -400,19 +406,19 @@
         )
 
 
-def finish(index, packed, both, backs, nears, fars, subs):
+def finish(packed, both, backs, nears, fars, subs):
     groups = (both, backs[0] + backs[1], nears, fars, subs)
     return pl.pallas_call(
         functools.partial(finish_kernel, tuple(len(group) for group in groups)),
         out_shape=jax.ShapeDtypeStruct(nears[0].shape, jnp.float32),
-        in_specs=[SMEM] + [VMEM] * (1 + sum(len(group) for group in groups)),
+        in_specs=[VMEM] * (1 + sum(len(group) for group in groups)),
         out_specs=VMEM,
         scratch_shapes=[
             pltpu.VMEM((packed.shape[0],) + backs[0][0].shape[1:], jnp.float32),
             pltpu.VMEM(fars[0].shape, jnp.float32),
         ],
         compiler_params=ROOM,
-    )(index, packed, *[array for group in groups for array in group])
+    )(packed, *[array for group in groups for array in group])
 
 
 def swap(value, axis):
@@ -431,10 +437,9 @@
 
 def shards_small(panel_field, near_row, near_col, near_block, bases, far_row, far_col, coupling):
     owner, sub, core = lax.axis_index("clu"), lax.axis_index("sub"), lax.axis_index("rep")
-    where = jnp.stack([owner, sub, core]).astype(jnp.int32)
     _, panels, width = panel_field.shape
     rank = bases.shape[2]
-    packed, mine = pack(where, panel_field, jnp.swapaxes(bases, 1, 2))
+    packed, mine = pack(panel_field, jnp.swapaxes(bases, 1, 2))
 
     axes = ("clu", "sub", "rep")
     numbered = [(o, s, r) for o in range(4) for s in range(2) for r in range(2)]
@@ -454,7 +459,7 @@
         within = jnp.where(paired, local, jnp.where(turn == 3, 2, 3))
         return jnp.where(kept, within, 4 + within)
 
-    apart = where[0] >= 0
+    apart = owner >= 0
 
     def back_half(packed, across, near_row, near_col, far_row, far_col, coupling, block):
         across_other = swap(across, "rep")
@@ -467,7 +472,6 @@
                 (across, lambda o, s, r: (r, 1 - s)),
                 (across_other, lambda o, s, r: (1 - r, 1 - s)),
             ],
-            where,
             near_row,
             near_col,
             matrix,
@@ -490,8 +494,10 @@
         coupling,
         near_block,
     )
-    to_two, *pair = lax.optimization_barrier((to_two, *incoming[:2]))
-    to_one, *incoming = lax.optimization_barrier((to_one, *pair, incoming[2]))
+    first, second, third = incoming
+    to_one, third = lax.optimization_barrier((to_one, third))
+    to_two, first, third = lax.optimization_barrier((to_two, first, third))
+    to_two, *incoming = lax.optimization_barrier((to_two, first, second, third))
     back_two = lax.ppermute(to_two, axes, by_core)
     back_one = lax.ppermute(to_one, "clu", opposite)
     incoming = jnp.concatenate(incoming, axis=0)
@@ -508,14 +514,13 @@
                     lambda o, s, r: (2 * (o ^ (2 - r)),) * 2 + (2 * (o ^ 3) + 1 - r - 2,),
                 ),
             ],
-            where,
             near_row,
             near_col,
             matrix,
             block,
         )
-        own_rows = forward_own(where, near_row, near_col, held, full, width)
-        payload, far = to_other_sub(where, ahead, swap(behind, "rep"), panels)
+        own_rows = forward_own(near_row, near_col, held, full, width)
+        payload, far = to_other_sub(ahead, swap(behind, "rep"), panels)
         return payload, far, own_rows
 
     payload, far, own_rows = stage(
@@ -537,7 +542,6 @@
     own_other, from_sub = lax.optimization_barrier((own_other, from_sub))
     from_sub_other = swap(from_sub.astype(jnp.float32), "rep")
     return finish(
-        where,
         packed,
         (backs[:2], backs_other[:2]),
         ((own, backs[2:]), (own_other, backs_other[2:])),
@@ -550,9 +554,8 @@
 def shards_any(panel_field, near_row, near_col, near_block, bases, far_row, far_col, coupling):
     owner, sub, core = lax.axis_index("clu"), lax.axis_index("sub"), lax.axis_index("rep")
     owners, subs = lax.axis_size("clu"), lax.axis_size("sub")
-    where = jnp.stack([owner, sub, core]).astype(jnp.int32)
     clusters, panels, width = panel_field.shape
-    packed, _ = pack(where, panel_field, jnp.swapaxes(bases, 1, 2))
+    packed, _ = pack(panel_field, jnp.swapaxes(bases, 1, 2))
     around = lax.all_gather(packed, "sub", axis=0)
     gathered = lax.all_gather(packed, "clu", axis=0, tiled=True)
     slots = owners * clusters
@@ -564,7 +567,6 @@
         slots,
         slot_of,
         [(around[k], lambda o, s, r, k=k: (0, k)) for k in range(subs)],
-        where,
         near_row,
         near_col,
         matrix,
@@ -572,10 +574,10 @@
     )
     back = lax.psum(lax.psum_scatter(back, "clu", scatter_dimension=0, tiled=True), "rep")
     ahead, behind, full, held = forward_far(
-        slots, [(gathered, lambda o, s, r: (0,) * slots)], where, near_row, near_col, matrix, near_block
+        slots, [(gathered, lambda o, s, r: (0,) * slots)], near_row, near_col, matrix, near_block
     )
     taken = swap(behind, "rep")
-    near = forward_own(where, near_row, near_col, held, full, width)
+    near = forward_own(near_row, near_col, held, full, width)
     near = near + swap(near, "rep")
     far = lax.psum((ahead + taken)[(subs - 1) * panels :], "sub").reshape(clusters, -1, width)
     ahead = (ahead + taken)[: (subs - 1) * panels]
@@ -588,7 +590,7 @@
         near = near + jnp.where(core == 0, jnp.stack([got, swap(got, "rep")]), jnp.stack([swap(got, "rep"), got]))
     single = lax.dynamic_slice_in_dim(back, core, 1, axis=0)
     other = lax.dynamic_slice_in_dim(back, 1 - core, 1, axis=0)
-    return finish(where, packed, (), ((single,), (other,)), (near,), (far,), ())
+    return finish(packed, (), ((single,), (other,)), (near,), (far,), ())
 
 
 def shards(*arrays):

time: 41 us -> 38.4 us (0.937)
  Pallas kernels: 16.1 us -> 14.6 us
  waiting for transfers between devices: 8.13 us -> 7.19 us
    ppermute x10, waiting for transfers between devices: 6 us -> 4.64 us  [swap(): return lax.ppermute(value, axis, [(0, 1), (1, 0)])]
    ppermute x10, starting transfers between devices: 6.79 us -> 7.68 us  [swap(): return lax.ppermute(value, axis, [(0, 1), (1, 0)])]
    ppermute x1, starting transfers between devices: 3.08 us -> 2.34 us  [shards_small(): back_one = lax.ppermute(to_one, 'clu', opposite)]
    pallas_call x1, Pallas kernels: 1.67 us -> 1.13 us  [pack(): pl.pallas_call(pack_kernel, out_shape=(jax.ShapeDtypeStruct((clusters, ro...]
    pallas_call x1, Pallas kernels: 0.58 us -> 0.04 us  [to_other_sub(): pl.pallas_call(merge_kernel, out_shape=(jax.ShapeDtypeStruct((rows, width...]
  transfers between devices with their start and end apart: 15 -> 15, of which waited for: 4 -> 5; matrix products, arithmetic and copies ran while one was open for 1% -> 1% of each run, Pallas kernels for 31% -> 32%
where the time goes in v6:
time: 38.4 us; the launch traced here: 38.2 us
  starting transfers between devices  15.8 us (41%)
  Pallas kernels  14.6 us (38%)
  waiting for transfers between devices  7.19 us (19%)
    ppermute x10, starting transfers between devices, swap(): return lax.ppermute(value, axis, [(0, 1), (1, 0)])  7.68 us
    ppermute x10, waiting for transfers between devices, swap(): return lax.ppermute(value, axis, [(0, 1), (1, 0)])  4.64 us
    ppermute x1, starting transfers between devices, shards_small(): incoming.append(lax.ppermute(mine, 'clu', opposite))  3.6 us
    pallas_call x1, Pallas kernels, forward_far(): pl.pallas_call(functools.partial(forward_kernel, plan, turns), out_shape=...  3.57 us
    pallas_call x1, Pallas kernels, load(): pl.pallas_call(load_kernel, out_shape=(jax.ShapeDtypeStruct(block.shape,...  3.4 us
    pallas_call x1, Pallas kernels, back_sums(): pl.pallas_call(functools.partial(back_kernel, plan, slot_of), out_shape=j...  3.23 us
    ppermute x1, waiting for transfers between devices, shards_small(): back_one = lax.ppermute(to_one, 'clu', opposite)  2.54 us
    ppermute x1, starting transfers between devices, shards_small(): back_one = lax.ppermute(to_one, 'clu', opposite)  2.34 us
  transfers between devices with their start and end apart: 15, of which 5 were waited for; matrix products, arithmetic and copies ran while one was open for 1% of the time, Pallas kernels for 32%

profile of v6, /device:TPU:0, one launch (start us, length us, event | category | flops | bytes accessed | tf_op | source)
XLA Modules:
  0.0 38.2 jit_solution(17657353304126019858)
XLA Ops:
  0.0 1.1 %shard_map.85 = (bf16[2,288,256]{2,1,0:T(8,128)(2,1)S(1)}, bf16[1,288,256]{2,1,0:T(8,128)(2,1)S(1)}) custom-call(bf16[2,256,256]{2,1,0:T(8,128)(2,1)} %panel.1, bf16[2,32,256]{2,1,0:T(8,128)(2,1)} %bitcast.1), custom_call_target="tpu_custom_call" | custom-call | tf_op jit(solution)/shard_map/pallas_call | solution.py:130
  1.1 3.0 %collective-permute-start.3 = (bf16[1,288,256]{2,1,0:T(8,128)(2,1)S(1)}, bf16[1,288,256]{2,1,0:T(8,128)(2,1)S(1)}, u32[]{:S(2)}, u32[]{:S(2)}) collective-permute-start(bf16[1,288,256]{2,1,0:T(8,128)(2,1)S(1)} %get-tuple-element.79), channel_id=1, source_target_pairs={{0,2},{2,0},{1,3},{3,1},{4,6},{6,4},{5,7},{7,5},{8,10},{10,8},{9,1... | collective-permute-start | bytes 442376 | tf_op jit(solution)/shard_map/ppermute | solution.py:425
  4.1 3.6 %collective-permute-start.5 = (bf16[1,288,256]{2,1,0:T(8,128)(2,1)S(1)}, bf16[1,288,256]{2,1,0:T(8,128)(2,1)S(1)}, u32[]{:S(2)}, u32[]{:S(2)}) collective-permute-start(bf16[1,288,256]{2,1,0:T(8,128)(2,1)S(1)} %get-tuple-element.79), channel_id=1, source_target_pairs={{0,12},{4,8},{8,4},{12,0},{1,13},{5,9},{9,5},{13,1},{2,14},{6,10},... | collective-permute-start | bytes 442376 | tf_op jit(solution)/shard_map/ppermute | solution.py:451
  7.8 0.1 collective-permute-start.4
  7.8 2.0 %collective-permute-start.6 = (bf16[1,288,256]{2,1,0:T(8,128)(2,1)S(1)}, bf16[1,288,256]{2,1,0:T(8,128)(2,1)S(1)}, u32[]{:S(2)}, u32[]{:S(2)}) collective-permute-start(bf16[1,288,256]{2,1,0:T(8,128)(2,1)S(1)} %get-tuple-element.106), channel_id=1, source_target_pairs={{0,4},{1,9},{2,6},{3,11},{4,0},{5,13},{6,2},{7,15},{8,12},{9,1},{1... | collective-permute-start | bytes 442376 | tf_op jit(solution)/shard_map/ppermute | solution.py:450
  9.9 10.0 %conditional.2 = (bf16[2,288,256]{2,1,0:T(8,128)(2,1)S(1)}, bf16[1,288,256]{2,1,0:T(8,128)(2,1)S(1)}, f32[1,288,256]{2,1,0:T(8,128)S(1)}, f32[64,256]{1,0:T(8,128)S(1)}) conditional(s32[]{:T(128)} %convert_element_type.13, () %tuple.25, (s32[32]{0:T(128)}, s32[32]{0:T(128)}, f32[32,32,32]{2,1,0:T(8,128)}, bf16[26,512,256]{2,1,0:T(8,128)(2,1)}, ...), branch_computations={%region_0.0_spmd, %region_1.0_spmd} | conditional | flops 516096 | bytes 11288744 | solution.py:430
  9.9 0.0 collective-permute-start.1
  9.9 3.4 %branch_1_fun.5 = (bf16[26,512,256]{2,1,0:T(8,128)(2,1)S(1)}, f32[64,256]{1,0:T(8,128)S(1)}) custom-call(s32[32]{0:T(128)} %get-tuple-element.101.far_row, s32[32]{0:T(128)} %get-tuple-element.102.far_col, f32[32,32,32]{2,1,0:T(8,128)} %get-tuple-element.103.coupling, bf16[26,512,256]{2,1,0:T(8,128)(2,1)} %get-tuple-element.40.block), custom_call_target="tpu_custom_call" | custom-call | tf_op jit(solution)/shard_map/cond/branch_1_fun/pallas_call | solution.py:90
  13.3 0.0 copy-start
  13.3 0.0 collective-permute-done.1.refs_2_
  13.3 3.2 %branch_1_fun.6 = f32[8,288,256]{2,1,0:T(8,128)S(1)} custom-call(s32[26]{0:T(128)} %get-tuple-element.35.near_row, s32[26]{0:T(128)} %get-tuple-element.36.near_col, f32[64,256]{1,0:T(8,128)S(1)} %get-tuple-element.115.matrix, bf16[26,512,256]{2,1,0:T(8,128)(2,1)S(1)} %get-tuple-element.42.block, bf16[2,288,256]{2,1,0:T(8,128)(2,1)S(1)} %get-tuple-element.43.refs_0_, ...), custom_call_target="tpu_custom_call" | custom-call | tf_op jit(solution)/shard_map/cond/branch_1_fun/pallas_call | solution.py:221
  16.5 0.1 slice.38
  16.6 0.0 copy-start.1
  16.6 0.6 %collective-permute-start.2 = (f32[4,288,256]{2,1,0:T(8,128)S(1)}, f32[4,288,256]{2,1,0:T(8,128)S(1)}, u32[]{:S(2)}, u32[]{:S(2)}) collective-permute-start(f32[4,288,256]{2,1,0:T(8,128)S(1)} %slice.38), channel_id=1, source_target_pairs={{0,1},{1,0},{2,3},{3,2},{4,5},{5,4},{6,7},{7,6},{8,9},{9,8},{10,11... | collective-permute-start | bytes 3538952 | tf_op jit(solution)/shard_map/cond/branch_1_fun/ppermute | solution.py:425
  17.2 2.5 %collective-permute-done.2 = f32[4,288,256]{2,1,0:T(8,128)S(1)} collective-permute-done((f32[4,288,256]{2,1,0:T(8,128)S(1)}, f32[4,288,256]{2,1,0:T(8,128)S(1)}, u32[]{:S(2)}, u32[]{:S(2)}) %collective-permute-start.2) | collective-permute-done | bytes 1179680 | tf_op jit(solution)/shard_map/cond/branch_1_fun/ppermute | solution.py:425
  19.7 0.1 slice_add_fusion.1
  19.8 0.1 fusion
  20.0 0.4 %collective-permute-start.11 = (bf16[3,288,256]{2,1,0:T(8,128)(2,1)S(1)}, bf16[3,288,256]{2,1,0:T(8,128)(2,1)S(1)}, u32[]{:S(2)}, u32[]{:S(2)}) collective-permute-start(bf16[3,288,256]{2,1,0:T(8,128)(2,1)S(1)} %constant_dynamic-update-slice_fusion), channel_id=1, source_target_pairs={{0,1},{1,0},{2,3},{3,2},{4,5},{5,4},{6,7},{7,6},{8,9},{9,8},{10,11... | collective-permute-start | bytes 1327112 | tf_op jit(solution)/shard_map/ppermute | solution.py:425
  20.4 0.1 collective-permute-start.7
  20.5 2.3 %collective-permute-start.8 = (bf16[1,288,256]{2,1,0:T(8,128)(2,1)S(1)}, bf16[1,288,256]{2,1,0:T(8,128)(2,1)S(1)}, u32[]{:S(2)}, u32[]{:S(2)}) collective-permute-start(bf16[1,288,256]{2,1,0:T(8,128)(2,1)S(1)} %get-tuple-element.87), channel_id=1, source_target_pairs={{0,12},{4,8},{8,4},{12,0},{1,13},{5,9},{9,5},{13,1},{2,14},{6,10},... | collective-permute-start | bytes 442376 | tf_op jit(solution)/shard_map/ppermute | solution.py:502
  22.9 6.1 %conditional.3 = (bf16[320,256]{1,0:T(8,128)(2,1)S(1)}, f32[2,32,256]{2,1,0:T(8,128)S(1)}, f32[2,256,256]{2,1,0:T(8,128)S(1)}) conditional(s32[]{:T(128)} %convert_element_type.13, () %tuple.30, (s32[26]{0:T(128)}, s32[26]{0:T(128)}, f32[64,256]{1,0:T(8,128)S(1)}, bf16[26,512,256]{2,1,0:T(8,128)(2,1)}, bf16[2,288,256]{2,1,0:T(8,128)(2,1)S(1)}, ...), branch_computations={%region_2.0_spmd, %region_3.0_spmd} | conditional | bytes 1310784 | solution.py:430
  22.9 3.6 %branch_1_fun.7 = (f32[320,256]{1,0:T(8,128)S(1)}, f32[320,256]{1,0:T(8,128)S(1)}, bf16[8,288,256]{2,1,0:T(8,128)(2,1)S(1)}, bf16[26,512,256]{2,1,0:T(8,128)(2,1)S(1)}) custom-call(s32[26]{0:T(128)} %get-tuple-element.45.near_row, s32[26]{0:T(128)} %get-tuple-element.46.near_col, f32[64,256]{1,0:T(8,128)S(1)} %get-tuple-element.47.matrix, ...), custom_call_target="tpu_custom_call" | custom-call | tf_op jit(solution)/shard_map/cond/branch_1_fun/pallas_call | solution.py:303
  26.5 0.6 %collective-permute-start = (f32[320,256]{1,0:T(8,128)S(1)}, f32[320,256]{1,0:T(8,128)S(1)}, u32[]{:S(2)}, u32[]{:S(2)}) collective-permute-start(f32[320,256]{1,0:T(8,128)S(1)} %get-tuple-element.53), channel_id=1, source_target_pairs={{0,1},{1,0},{2,3},{3,2},{4,5},{5,4},{6,7},{7,6},{8,9},{9,8},{10,11... | collective-permute-start | bytes 983048 | tf_op jit(solution)/shard_map/cond/branch_1_fun/ppermute | solution.py:425
  27.0 1.9 %branch_1_fun.9 = f32[2,256,256]{2,1,0:T(8,128)S(1)} custom-call(s32[26]{0:T(128)} %get-tuple-element.45.near_row, s32[26]{0:T(128)} %get-tuple-element.46.near_col, bf16[26,512,256]{2,1,0:T(8,128)(2,1)S(1)} %get-tuple-element.56.block, bf16[8,288,256]{2,1,0:T(8,128)(2,1)S(1)} %get-tuple-element.57.full), custom_call_target="tpu_custom_call" | custom-call | tf_op jit(solution)/shard_map/cond/branch_1_fun/pallas_call | solution.py:362
  29.0 1.6 %collective-permute-start.12 = (bf16[320,256]{1,0:T(8,128)(2,1)S(1)}, bf16[320,256]{1,0:T(8,128)(2,1)S(1)}, u32[]{:S(2)}, u32[]{:S(2)}) collective-permute-start(bf16[320,256]{1,0:T(8,128)(2,1)S(1)} %get-tuple-element.93), channel_id=1, source_target_pairs={{0,2},{2,0},{1,3},{3,1},{4,6},{6,4},{5,7},{7,5},{8,10},{10,8},{9,1... | collective-permute-start | bytes 491528 | tf_op jit(solution)/shard_map/ppermute | solution.py:425
  30.5 2.5 %collective-permute-done.8.refs_3_ = bf16[1,288,256]{2,1,0:T(8,128)(2,1)S(1)} collective-permute-done((bf16[1,288,256]{2,1,0:T(8,128)(2,1)S(1)}, bf16[1,288,256]{2,1,0:T(8,128)(2,1)S(1)}, u32[]{:S(2)}, u32[]{:S(2)}) %collective-permute-start.8) | collective-permute-done | bytes 147488 | tf_op jit(solution)/shard_map/ppermute | solution.py:502
  33.1 1.5 %collective-permute-start.9 = (bf16[3,288,256]{2,1,0:T(8,128)(2,1)S(1)}, bf16[3,288,256]{2,1,0:T(8,128)(2,1)S(1)}, u32[]{:S(2)}, u32[]{:S(2)}) collective-permute-start(bf16[3,288,256]{2,1,0:T(8,128)(2,1)S(1)} %pad_maximum_fusion), channel_id=1, source_target_pairs={{0,1},{1,0},{2,3},{3,2},{4,5},{5,4},{6,7},{7,6},{8,9},{9,8},{10,11... | collective-permute-start | bytes 1327112 | tf_op jit(solution)/shard_map/ppermute | solution.py:425
  34.6 0.6 %collective-permute-done.12.refs_9_ = bf16[320,256]{1,0:T(8,128)(2,1)S(1)} collective-permute-done((bf16[320,256]{1,0:T(8,128)(2,1)S(1)}, bf16[320,256]{1,0:T(8,128)(2,1)S(1)}, u32[]{:S(2)}, u32[]{:S(2)}) %collective-permute-start.12) | collective-permute-done | bytes 163872 | tf_op jit(solution)/shard_map/ppermute | solution.py:425
  35.2 0.1 collective-permute-start.14
  35.3 0.7 %collective-permute-done.9 = bf16[3,288,256]{2,1,0:T(8,128)(2,1)S(1)} collective-permute-done((bf16[3,288,256]{2,1,0:T(8,128)(2,1)S(1)}, bf16[3,288,256]{2,1,0:T(8,128)(2,1)S(1)}, u32[]{:S(2)}, u32[]{:S(2)}) %collective-permute-start.9) | collective-permute-done | bytes 442400 | tf_op jit(solution)/shard_map/ppermute | solution.py:425
  36.1 0.8 %collective-permute-done.14.refs_10_ = f32[320,256]{1,0:T(8,128)S(1)} collective-permute-done((f32[320,256]{1,0:T(8,128)S(1)}, f32[320,256]{1,0:T(8,128)S(1)}, u32[]{:S(2)}, u32[]{:S(2)}) %collective-permute-start.14) | collective-permute-done | bytes 327712 | tf_op jit(solution)/shard_map/ppermute | solution.py:425
  36.9 1.3 %shard_map.86 = f32[2,256,256]{2,1,0:T(8,128)} custom-call(bf16[2,288,256]{2,1,0:T(8,128)(2,1)S(1)} %get-tuple-element.78.packed, bf16[2,288,256]{2,1,0:T(8,128)(2,1)S(1)} %collective-permute-done.7.refs_0_, bf16[2,288,256]{2,1,0:T(8,128)(2,1)S(1)} %slice.44.refs_1_, f32[1,288,256]{2,1,0:T(8,128)S(1)} %get-tuple-element.88.refs_2_, ...), custom_call_target="tpu_custom_call" | custom-call | tf_op jit(solution)/shard_map/pallas_call | solution.py:411
  (22 shorter events, 0.2 us)
Async XLA Ops:
  1.1 8.7 %collective-permute-start.3 = (bf16[1,288,256]{2,1,0:T(8,128)(2,1)S(1)}, bf16[1,288,256]{2,1,0:T(8,128)(2,1)S(1)}, u32[]{:S(2)}, u32[]{:S(2)}) collective-permute-start(bf16[1,288,256]{2,1,0:T(8,128)(2,1)S(1)} %get-tuple-element.79), channel_id=1, source_target_pairs={{0,2},{2,0},{1,3},{3,1},{4,6},{6,4},{5,7},{7,5},{8,10},{10,8},{9,1... | collective-permute-start | bytes 442376 | tf_op jit(solution)/shard_map/ppermute | solution.py:425
  4.1 15.7 %collective-permute-start.5 = (bf16[1,288,256]{2,1,0:T(8,128)(2,1)S(1)}, bf16[1,288,256]{2,1,0:T(8,128)(2,1)S(1)}, u32[]{:S(2)}, u32[]{:S(2)}) collective-permute-start(bf16[1,288,256]{2,1,0:T(8,128)(2,1)S(1)} %get-tuple-element.79), channel_id=1, source_target_pairs={{0,12},{4,8},{8,4},{12,0},{1,13},{5,9},{9,5},{13,1},{2,14},{6,10},... | collective-permute-start | bytes 442376 | tf_op jit(solution)/shard_map/ppermute | solution.py:451
  7.8 12.1 %collective-permute-start.4 = (bf16[1,288,256]{2,1,0:T(8,128)(2,1)S(1)}, bf16[1,288,256]{2,1,0:T(8,128)(2,1)S(1)}, u32[]{:S(2)}, u32[]{:S(2)}) collective-permute-start(bf16[1,288,256]{2,1,0:T(8,128)(2,1)S(1)} %get-tuple-element.107), channel_id=1, source_target_pairs={{0,4},{1,9},{2,6},{3,11},{4,0},{5,13},{6,2},{7,15},{8,12},{9,1},{1... | collective-permute-start | bytes 442376 | tf_op jit(solution)/shard_map/ppermute | solution.py:450
  7.8 12.1 %collective-permute-start.6 = (bf16[1,288,256]{2,1,0:T(8,128)(2,1)S(1)}, bf16[1,288,256]{2,1,0:T(8,128)(2,1)S(1)}, u32[]{:S(2)}, u32[]{:S(2)}) collective-permute-start(bf16[1,288,256]{2,1,0:T(8,128)(2,1)S(1)} %get-tuple-element.106), channel_id=1, source_target_pairs={{0,4},{1,9},{2,6},{3,11},{4,0},{5,13},{6,2},{7,15},{8,12},{9,1},{1... | collective-permute-start | bytes 442376 | tf_op jit(solution)/shard_map/ppermute | solution.py:450
  9.9 3.4 %collective-permute-start.1 = (bf16[1,288,256]{2,1,0:T(8,128)(2,1)S(1)}, bf16[1,288,256]{2,1,0:T(8,128)(2,1)S(1)}, u32[]{:S(2)}, u32[]{:S(2)}) collective-permute-start(bf16[1,288,256]{2,1,0:T(8,128)(2,1)S(1)} %get-tuple-element.44.refs_1_), channel_id=1, source_target_pairs={{0,1},{1,0},{2,3},{3,2},{4,5},{5,4},{6,7},{7,6},{8,9},{9,8},{10,11... | collective-permute-start | bytes 442376 | tf_op jit(solution)/shard_map/cond/branch_1_fun/ppermute | solution.py:425
  13.3 3.3 %copy-start = (f32[64,256]{1,0:T(8,128)}, f32[64,256]{1,0:T(8,128)S(1)}, u32[]{:S(2)}) copy-start(f32[64,256]{1,0:T(8,128)S(1)} %get-tuple-element.115.matrix) | copy-start | bytes 196612 | tf_op jit(solution)/shard_map/cond
  16.6 3.2 %copy-start.1 = (f32[64,256]{1,0:T(8,128)S(1)}, f32[64,256]{1,0:T(8,128)}, u32[]{:S(2)}) copy-start(f32[64,256]{1,0:T(8,128)} %copy-done) | copy-start | bytes 196612 | tf_op jit(solution)/shard_map/cond
  16.6 3.1 %collective-permute-start.2 = (f32[4,288,256]{2,1,0:T(8,128)S(1)}, f32[4,288,256]{2,1,0:T(8,128)S(1)}, u32[]{:S(2)}, u32[]{:S(2)}) collective-permute-start(f32[4,288,256]{2,1,0:T(8,128)S(1)} %slice.38), channel_id=1, source_target_pairs={{0,1},{1,0},{2,3},{3,2},{4,5},{5,4},{6,7},{7,6},{8,9},{9,8},{10,11... | collective-permute-start | bytes 3538952 | tf_op jit(solution)/shard_map/cond/branch_1_fun/ppermute | solution.py:425
  20.0 2.9 %collective-permute-start.11 = (bf16[3,288,256]{2,1,0:T(8,128)(2,1)S(1)}, bf16[3,288,256]{2,1,0:T(8,128)(2,1)S(1)}, u32[]{:S(2)}, u32[]{:S(2)}) collective-permute-start(bf16[3,288,256]{2,1,0:T(8,128)(2,1)S(1)} %constant_dynamic-update-slice_fusion), channel_id=1, source_target_pairs={{0,1},{1,0},{2,3},{3,2},{4,5},{5,4},{6,7},{7,6},{8,9},{9,8},{10,11... | collective-permute-start | bytes 1327112 | tf_op jit(solution)/shard_map/ppermute | solution.py:425
  20.4 12.7 %collective-permute-start.7 = (bf16[2,288,256]{2,1,0:T(8,128)(2,1)S(1)}, bf16[2,288,256]{2,1,0:T(8,128)(2,1)S(1)}, u32[]{:S(2)}, u32[]{:S(2)}) collective-permute-start(bf16[2,288,256]{2,1,0:T(8,128)(2,1)S(1)} %get-tuple-element.86), channel_id=1, source_target_pairs={{0,4},{1,9},{2,6},{3,11},{4,0},{5,13},{6,2},{7,15},{8,12},{9,1},{1... | collective-permute-start | bytes 884744 | tf_op jit(solution)/shard_map/ppermute | solution.py:501
  20.5 12.5 %collective-permute-start.8 = (bf16[1,288,256]{2,1,0:T(8,128)(2,1)S(1)}, bf16[1,288,256]{2,1,0:T(8,128)(2,1)S(1)}, u32[]{:S(2)}, u32[]{:S(2)}) collective-permute-start(bf16[1,288,256]{2,1,0:T(8,128)(2,1)S(1)} %get-tuple-element.87), channel_id=1, source_target_pairs={{0,12},{4,8},{8,4},{12,0},{1,13},{5,9},{9,5},{13,1},{2,14},{6,10},... | collective-permute-start | bytes 442376 | tf_op jit(solution)/shard_map/ppermute | solution.py:502
  22.9 11.7 %collective-permute-start.10 = (f32[1,288,256]{2,1,0:T(8,128)S(1)}, f32[1,288,256]{2,1,0:T(8,128)S(1)}, u32[]{:S(2)}, u32[]{:S(2)}) collective-permute-start(f32[1,288,256]{2,1,0:T(8,128)S(1)} %get-tuple-element.88.refs_2_), channel_id=1, source_target_pairs={{0,1},{1,0},{2,3},{3,2},{4,5},{5,4},{6,7},{7,6},{8,9},{9,8},{10,11... | collective-permute-start | bytes 884744 | tf_op jit(solution)/shard_map/ppermute | solution.py:425
  26.5 2.5 %collective-permute-start = (f32[320,256]{1,0:T(8,128)S(1)}, f32[320,256]{1,0:T(8,128)S(1)}, u32[]{:S(2)}, u32[]{:S(2)}) collective-permute-start(f32[320,256]{1,0:T(8,128)S(1)} %get-tuple-element.53), channel_id=1, source_target_pairs={{0,1},{1,0},{2,3},{3,2},{4,5},{5,4},{6,7},{7,6},{8,9},{9,8},{10,11... | collective-permute-start | bytes 983048 | tf_op jit(solution)/shard_map/cond/branch_1_fun/ppermute | solution.py:425
  29.0 6.2 %collective-permute-start.12 = (bf16[320,256]{1,0:T(8,128)(2,1)S(1)}, bf16[320,256]{1,0:T(8,128)(2,1)S(1)}, u32[]{:S(2)}, u32[]{:S(2)}) collective-permute-start(bf16[320,256]{1,0:T(8,128)(2,1)S(1)} %get-tuple-element.93), channel_id=1, source_target_pairs={{0,2},{2,0},{1,3},{3,1},{4,6},{6,4},{5,7},{7,5},{8,10},{10,8},{9,1... | collective-permute-start | bytes 491528 | tf_op jit(solution)/shard_map/ppermute | solution.py:425
  30.5 6.4 %collective-permute-start.13 = (f32[2,256,256]{2,1,0:T(8,128)S(1)}, f32[2,256,256]{2,1,0:T(8,128)S(1)}, u32[]{:S(2)}, u32[]{:S(2)}) collective-permute-start(f32[2,256,256]{2,1,0:T(8,128)S(1)} %get-tuple-element.95.refs_6_), channel_id=1, source_target_pairs={{0,1},{1,0},{2,3},{3,2},{4,5},{5,4},{6,7},{7,6},{8,9},{9,8},{10,11... | collective-permute-start | bytes 1572872 | tf_op jit(solution)/shard_map/ppermute | solution.py:425
  33.1 2.9 %collective-permute-start.9 = (bf16[3,288,256]{2,1,0:T(8,128)(2,1)S(1)}, bf16[3,288,256]{2,1,0:T(8,128)(2,1)S(1)}, u32[]{:S(2)}, u32[]{:S(2)}) collective-permute-start(bf16[3,288,256]{2,1,0:T(8,128)(2,1)S(1)} %pad_maximum_fusion), channel_id=1, source_target_pairs={{0,1},{1,0},{2,3},{3,2},{4,5},{5,4},{6,7},{7,6},{8,9},{9,8},{10,11... | collective-permute-start | bytes 1327112 | tf_op jit(solution)/shard_map/ppermute | solution.py:425
  35.2 1.7 %collective-permute-start.14 = (f32[320,256]{1,0:T(8,128)S(1)}, f32[320,256]{1,0:T(8,128)S(1)}, u32[]{:S(2)}, u32[]{:S(2)}) collective-permute-start(f32[320,256]{1,0:T(8,128)S(1)} %convert_element_type.14), channel_id=1, source_target_pairs={{0,1},{1,0},{2,3},{3,2},{4,5},{5,4},{6,7},{7,6},{8,9},{9,8},{10,11... | collective-permute-start | bytes 983048 | tf_op jit(solution)/shard_map/ppermute | solution.py:425

commit v7 on v6

--- a/solution.py
+++ b/solution.py
@@ -59,17 +59,22 @@
     ]
 
 
-def load_kernel(far_row, far_col, coupling, block, held, matrix, couplings, table, sems, sem, *scratch):
+def load_kernel(
+    near_row, near_col, far_row, far_col, coupling, block,
+    held, matrix, row_held, col_held, couplings, table, sems, sem, *scratch
+):
+    scalars = Scalars((far_row, far_col), scratch[:2], scratch[2])
+    small = Scalars((near_row, near_col), (row_held, col_held), scratch[3])
+    first = pltpu.make_async_copy(coupling, couplings, sem)
+    first.start()
     parts = parts_of(block, held, sems)
     for _, copy in parts:
         copy.start()
-    first = pltpu.make_async_copy(coupling, couplings, sem)
-    first.start()
-    scalars = Scalars((far_row, far_col), scratch[:2], scratch[2])
     table[...] = jnp.zeros_like(table)
     rows, columns = scalars.wait()
     first.wait()
     sum_couplings(rows, columns, couplings, matrix, table)
+    small.wait()
     for _, copy in parts:
         copy.wait()
 
@@ -85,25 +90,28 @@
         )
 
 
-def load(slots, far_row, far_col, coupling, block):
+def load(slots, near_row, near_col, far_row, far_col, coupling, block):
     rank = coupling.shape[1]
     return pl.pallas_call(
         load_kernel,
         out_shape=(
             jax.ShapeDtypeStruct(block.shape, block.dtype),
             jax.ShapeDtypeStruct((2 * rank, slots * rank), jnp.float32),
+            jax.ShapeDtypeStruct(near_row.shape, jnp.int32),
+            jax.ShapeDtypeStruct(near_col.shape, jnp.int32),
         ),
-        in_specs=[ANY] * 4,
-        out_specs=(VMEM, VMEM),
+        in_specs=[ANY] * 6,
+        out_specs=(VMEM,) * 4,
         scratch_shapes=[
             pltpu.VMEM(coupling.shape, coupling.dtype),
             pltpu.VMEM((2, slots, rank, rank), jnp.float32),
             pltpu.SemaphoreType.DMA((PARTS,)),
             pltpu.SemaphoreType.DMA,
             *scalar_scratch(far_row, far_col),
+            pltpu.SemaphoreType.DMA((2,)),
         ],
         compiler_params=ROOM,
-    )(in_hbm(far_row), in_hbm(far_col), in_hbm(coupling), in_hbm(block))
+    )(*[in_hbm(array) for array in (near_row, near_col, far_row, far_col, coupling, block)])
 
 
 def pack_kernel(panel, bases, packed, mine, held, sems):
@@ -228,7 +236,7 @@
             *scalar_scratch(near_row, near_col),
         ],
         compiler_params=ROOM,
-    )(in_hbm(near_row), in_hbm(near_col), matrix, block, *[p for p, _ in pieces])
+    )(near_row, near_col, matrix, block, *[p for p, _ in pieces])
 
 
 def forward_step(turns, index, near_row, near_col, block, full, total):
@@ -236,14 +244,13 @@
     subs = block.shape[1] // panels
 
     def step(q):
-        field = full[near_col[q], : total.shape[2], :]
+        field = full[near_col[q]]
         row = near_row[q]
         for k, turn in enumerate(turns):
             at = lax.rem(index[1] + turn, subs)
-            product = lax.dot_general(
+            product = jnp.dot(
                 block[q, pl.ds(pl.multiple_of(at * panels, panels), panels), :],
                 field,
-                LAST,
                 preferred_element_type=jnp.float32,
             )
             total[row, k * rows : (k + 1) * rows, :] += product
@@ -254,31 +261,25 @@
 def forward_kernel(plan, turns, near_row, near_col, matrix, block, *refs):
     n = len(plan)
     pieces = refs[:n]
-    keep, give, full, held, total, sems, *scratch = refs[n:]
+    keep, give, full, held, total, projection, sems, *scratch = refs[n:]
     scalars = Scalars((near_row, near_col), scratch[:2], scratch[2])
     parts = parts_of(block, held, sems)
     for _, copy in parts:
         copy.start()
-    slots, rows, _ = full.shape
+    slots, _, width = full.shape
     rank = matrix.shape[1] // slots
-    width = rows - rank
     total[...] = jnp.zeros_like(total)
     index = place()
     near_row, near_col = scalars.wait()
     for piece, where in zip(pieces, plan):
         firsts = where(index[0], index[1], index[2])
         for c, first in enumerate(firsts):
-            full[first + c] = piece[c]
-    projection = jnp.concatenate(
-        [
-            lax.dot_general(
-                full[t, width:, :], full[t, :width, :], LAST, preferred_element_type=jnp.float32
+            panel = piece[c, :width, :].T
+            full[first + c] = panel
+            projection[pl.ds(pl.multiple_of((first + c) * rank, rank), rank), :] = jnp.dot(
+                piece[c, width:, :], panel, preferred_element_type=jnp.float32
             )
-            for t in range(slots)
-        ],
-        axis=0,
-    )
-    weights = product_in_parts(matrix[...], projection, (((1,), (0,)), ((), ())))
+    weights = product_in_parts(matrix[...], projection[...], (((1,), (0,)), ((), ())))
     step = forward_step(turns, index, near_row, near_col, held, full, total)
     for pairs, copy in parts:
         copy.wait()
@@ -305,13 +306,14 @@
         out_shape=(
             shape,
             shape,
-            jax.ShapeDtypeStruct((slots, rows, panels), jnp.bfloat16),
+            jax.ShapeDtypeStruct((slots, panels, width), jnp.bfloat16),
             jax.ShapeDtypeStruct(block.shape, block.dtype),
         ),
         in_specs=[ANY] * 2 + [VMEM, ANY] + [VMEM] * len(pieces),
         out_specs=(VMEM,) * 4,
         scratch_shapes=[
             pltpu.VMEM((2, tall, width), jnp.float32),
+            pltpu.VMEM((slots * rank, width), jnp.float32),
             pltpu.SemaphoreType.DMA((PARTS,)),
             *scalar_scratch(near_row, near_col),
         ],
@@ -366,7 +368,7 @@
         out_specs=VMEM,
         scratch_shapes=scalar_scratch(near_row, near_col),
         compiler_params=ROOM,
-    )(in_hbm(near_row), in_hbm(near_col), block, full)
+    )(near_row, near_col, block, full)
 
 
 def finish_kernel(counts, packed, *refs):
@@ -463,7 +465,9 @@
 
     def back_half(packed, across, near_row, near_col, far_row, far_col, coupling, block):
         across_other = swap(across, "rep")
-        held, matrix = load(8, far_row, far_col, coupling, block)
+        held, matrix, near_row, near_col = load(
+            8, near_row, near_col, far_row, far_col, coupling, block
+        )
         total = back_sums(
             8,
             slot_of,
@@ -480,9 +484,9 @@
         taken = swap(total[4:], "rep")
         to_two = (total[:2] + taken[:2]).astype(jnp.bfloat16)
         to_one = (total[2:3] + taken[2:3]).astype(jnp.bfloat16)
-        return to_two, to_one, total[3:4] + taken[3:], matrix
-
-    to_two, to_one, own, matrix = stage(
+        return to_two, to_one, total[3:4] + taken[3:], matrix, near_row, near_col
+
+    to_two, to_one, own, matrix, row_held, col_held = stage(
         apart,
         back_half,
         packed,
@@ -503,7 +507,9 @@
     incoming = jnp.concatenate(incoming, axis=0)
     incoming_other = swap(incoming, "rep")
 
-    def forward_half(packed, incoming, incoming_other, matrix, near_row, near_col, block):
+    def forward_half(
+        packed, incoming, incoming_other, matrix, near_row, near_col, row_held, col_held, block
+    ):
         ahead, behind, full, held = forward_far(
             8,
             [
@@ -519,7 +525,7 @@
             matrix,
             block,
         )
-        own_rows = forward_own(near_row, near_col, held, full, width)
+        own_rows = forward_own(row_held, col_held, held, full, width)
         payload, far = to_other_sub(ahead, swap(behind, "rep"), panels)
         return payload, far, own_rows
 
@@ -532,6 +538,8 @@
         matrix,
         near_row,
         near_col,
+        row_held,
+        col_held,
         near_block,
     )
 
@@ -562,7 +570,9 @@
     def slot_of(cluster, owner, core):
         return cluster
 
-    held, matrix = load(slots, far_row, far_col, coupling, near_block)
+    held, matrix, _, _ = load(
+        slots, near_row, near_col, far_row, far_col, coupling, near_block
+    )
     back = back_sums(
         slots,
         slot_of,

time: 38.4 us -> 38 us (0.990)
  Pallas kernels: 14.6 us -> 14.2 us
  transfers between devices with their start and end apart: 15 -> 15, of which waited for: 5 -> 5; matrix products, arithmetic and copies ran while one was open for 1% -> 1% of each run, Pallas kernels for 32% -> 31%
where the time goes in v7:
time: 38 us; the launch traced here: 37.8 us
  starting transfers between devices  15.8 us (42%)
  Pallas kernels  14.2 us (37%)
  waiting for transfers between devices  7.18 us (19%)
    ppermute x10, starting transfers between devices, swap(): return lax.ppermute(value, axis, [(0, 1), (1, 0)])  7.69 us
    ppermute x10, waiting for transfers between devices, swap(): return lax.ppermute(value, axis, [(0, 1), (1, 0)])  4.43 us
    ppermute x1, starting transfers between devices, shards_small(): incoming.append(lax.ppermute(mine, 'clu', opposite))  3.6 us
    pallas_call x1, Pallas kernels, forward_far(): pl.pallas_call(functools.partial(forward_kernel, plan, turns), out_shape=...  3.54 us
    pallas_call x1, Pallas kernels, load(): pl.pallas_call(load_kernel, out_shape=(jax.ShapeDtypeStruct(block.shape,...  3.27 us
    pallas_call x1, Pallas kernels, back_sums(): pl.pallas_call(functools.partial(back_kernel, plan, slot_of), out_shape=j...  3.19 us
    ppermute x1, waiting for transfers between devices, shards_small(): back_one = lax.ppermute(to_one, 'clu', opposite)  2.75 us
    ppermute x1, starting transfers between devices, shards_small(): back_one = lax.ppermute(to_one, 'clu', opposite)  2.34 us
  transfers between devices with their start and end apart: 15, of which 5 were waited for; matrix products, arithmetic and copies ran while one was open for 1% of the time, Pallas kernels for 31%

profile of v7, /device:TPU:0, one launch (start us, length us, event | category | flops | bytes accessed | tf_op | source)
XLA Modules:
  0.0 37.8 jit_solution(4419052998353023008)
XLA Ops:
  0.0 1.1 %shard_map.85 = (bf16[2,288,256]{2,1,0:T(8,128)(2,1)S(1)}, bf16[1,288,256]{2,1,0:T(8,128)(2,1)S(1)}) custom-call(bf16[2,256,256]{2,1,0:T(8,128)(2,1)} %panel.1, bf16[2,32,256]{2,1,0:T(8,128)(2,1)} %bitcast.1), custom_call_target="tpu_custom_call" | custom-call | tf_op jit(solution)/shard_map/pallas_call | solution.py:138
  1.1 3.0 %collective-permute-start.3 = (bf16[1,288,256]{2,1,0:T(8,128)(2,1)S(1)}, bf16[1,288,256]{2,1,0:T(8,128)(2,1)S(1)}, u32[]{:S(2)}, u32[]{:S(2)}) collective-permute-start(bf16[1,288,256]{2,1,0:T(8,128)(2,1)S(1)} %get-tuple-element.89), channel_id=1, source_target_pairs={{0,2},{2,0},{1,3},{3,1},{4,6},{6,4},{5,7},{7,5},{8,10},{10,8},{9,1... | collective-permute-start | bytes 442376 | tf_op jit(solution)/shard_map/ppermute | solution.py:427
  4.1 3.6 %collective-permute-start.5 = (bf16[1,288,256]{2,1,0:T(8,128)(2,1)S(1)}, bf16[1,288,256]{2,1,0:T(8,128)(2,1)S(1)}, u32[]{:S(2)}, u32[]{:S(2)}) collective-permute-start(bf16[1,288,256]{2,1,0:T(8,128)(2,1)S(1)} %get-tuple-element.89), channel_id=1, source_target_pairs={{0,12},{4,8},{8,4},{12,0},{1,13},{5,9},{9,5},{13,1},{2,14},{6,10},... | collective-permute-start | bytes 442376 | tf_op jit(solution)/shard_map/ppermute | solution.py:453
  7.8 0.1 collective-permute-start.4
  7.8 2.0 %collective-permute-start.6 = (bf16[1,288,256]{2,1,0:T(8,128)(2,1)S(1)}, bf16[1,288,256]{2,1,0:T(8,128)(2,1)S(1)}, u32[]{:S(2)}, u32[]{:S(2)}) collective-permute-start(bf16[1,288,256]{2,1,0:T(8,128)(2,1)S(1)} %get-tuple-element.118), channel_id=1, source_target_pairs={{0,4},{1,9},{2,6},{3,11},{4,0},{5,13},{6,2},{7,15},{8,12},{9,1},{1... | collective-permute-start | bytes 442376 | tf_op jit(solution)/shard_map/ppermute | solution.py:452
  9.9 0.0 collective-permute-done.3
  9.9 9.9 %conditional.2 = (bf16[2,288,256]{2,1,0:T(8,128)(2,1)S(1)}, bf16[1,288,256]{2,1,0:T(8,128)(2,1)S(1)}, f32[1,288,256]{2,1,0:T(8,128)S(1)}, f32[64,256]{1,0:T(8,128)S(1)}, s32[26]{0:T(128)S(1)}, /*index=5*/s32[26]{0:T(128)S(1)}) conditional(s32[]{:T(128)} %convert_element_type.13, () %tuple.25, (s32[26]{0:T(128)}, s32[26]{0:T(128)}, s32[32]{0:T(128)}, ...), branch_computations={%region_0.0_spmd, %region_1.0_spmd} | conditional | flops 516096 | bytes 11290536 | solution.py:432
  9.9 0.0 collective-permute-start.1
  9.9 3.3 %branch_1_fun.5 = (bf16[26,512,256]{2,1,0:T(8,128)(2,1)S(1)}, f32[64,256]{1,0:T(8,128)S(1)}, s32[26]{0:T(128)S(1)}, s32[26]{0:T(128)S(1)}) custom-call(s32[26]{0:T(128)} %get-tuple-element.39.near_row, s32[26]{0:T(128)} %get-tuple-element.40.near_col, s32[32]{0:T(128)} %get-tuple-element.113.far_row, s32[32]{0:T(128)} %get-tuple-element.114.far_col, ...), custom_call_target="tpu_custom_call" | custom-call | tf_op jit(solution)/shard_map/cond/branch_1_fun/pallas_call | solution.py:95
  13.1 0.0 copy-start
  13.2 3.2 %branch_1_fun.6 = f32[8,288,256]{2,1,0:T(8,128)S(1)} custom-call(s32[26]{0:T(128)S(1)} %get-tuple-element.130.near_row, s32[26]{0:T(128)S(1)} %get-tuple-element.131.near_col, f32[64,256]{1,0:T(8,128)S(1)} %get-tuple-element.129.matrix, bf16[26,512,256]{2,1,0:T(8,128)(2,1)S(1)} %get-tuple-element.48.block, ...), custom_call_target="tpu_custom_call" | custom-call | tf_op jit(solution)/shard_map/cond/branch_1_fun/pallas_call | solution.py:229
  16.4 0.1 slice.38
  16.5 0.0 copy-start.1
  16.5 0.6 %collective-permute-start.2 = (f32[4,288,256]{2,1,0:T(8,128)S(1)}, f32[4,288,256]{2,1,0:T(8,128)S(1)}, u32[]{:S(2)}, u32[]{:S(2)}) collective-permute-start(f32[4,288,256]{2,1,0:T(8,128)S(1)} %slice.38), channel_id=1, source_target_pairs={{0,1},{1,0},{2,3},{3,2},{4,5},{5,4},{6,7},{7,6},{8,9},{9,8},{10,11... | collective-permute-start | bytes 3538952 | tf_op jit(solution)/shard_map/cond/branch_1_fun/ppermute | solution.py:427
  17.1 2.5 %collective-permute-done.2 = f32[4,288,256]{2,1,0:T(8,128)S(1)} collective-permute-done((f32[4,288,256]{2,1,0:T(8,128)S(1)}, f32[4,288,256]{2,1,0:T(8,128)S(1)}, u32[]{:S(2)}, u32[]{:S(2)}) %collective-permute-start.2) | collective-permute-done | bytes 1179680 | tf_op jit(solution)/shard_map/cond/branch_1_fun/ppermute | solution.py:427
  19.6 0.1 slice_add_fusion.1
  19.7 0.1 fusion
  19.9 0.4 %collective-permute-start.11 = (bf16[3,288,256]{2,1,0:T(8,128)(2,1)S(1)}, bf16[3,288,256]{2,1,0:T(8,128)(2,1)S(1)}, u32[]{:S(2)}, u32[]{:S(2)}) collective-permute-start(bf16[3,288,256]{2,1,0:T(8,128)(2,1)S(1)} %constant_dynamic-update-slice_fusion), channel_id=1, source_target_pairs={{0,1},{1,0},{2,3},{3,2},{4,5},{5,4},{6,7},{7,6},{8,9},{9,8},{10,11... | collective-permute-start | bytes 1327112 | tf_op jit(solution)/shard_map/ppermute | solution.py:427
  20.3 0.0 collective-permute-start.7
  20.4 2.3 %collective-permute-start.8 = (bf16[1,288,256]{2,1,0:T(8,128)(2,1)S(1)}, bf16[1,288,256]{2,1,0:T(8,128)(2,1)S(1)}, u32[]{:S(2)}, u32[]{:S(2)}) collective-permute-start(bf16[1,288,256]{2,1,0:T(8,128)(2,1)S(1)} %get-tuple-element.97), channel_id=1, source_target_pairs={{0,12},{4,8},{8,4},{12,0},{1,13},{5,9},{9,5},{13,1},{2,14},{6,10},... | collective-permute-start | bytes 442376 | tf_op jit(solution)/shard_map/ppermute | solution.py:506
  22.7 5.9 %conditional.3 = (bf16[320,256]{1,0:T(8,128)(2,1)S(1)}, f32[2,32,256]{2,1,0:T(8,128)S(1)}, f32[2,256,256]{2,1,0:T(8,128)S(1)}) conditional(s32[]{:T(128)} %convert_element_type.13, () %tuple.30, (s32[26]{0:T(128)}, s32[26]{0:T(128)}, f32[64,256]{1,0:T(8,128)S(1)}, bf16[26,512,256]{2,1,0:T(8,128)(2,1)}, bf16[2,288,256]{2,1,0:T(8,128)(2,1)S(1)}, ...), branch_computations={%region_2.0_spmd, %region_3.0_spmd} | conditional | bytes 1310784 | solution.py:432
  22.7 3.5 %branch_1_fun.7 = (f32[320,256]{1,0:T(8,128)S(1)}, f32[320,256]{1,0:T(8,128)S(1)}, bf16[8,256,256]{2,1,0:T(8,128)(2,1)S(1)}, bf16[26,512,256]{2,1,0:T(8,128)(2,1)S(1)}) custom-call(s32[26]{0:T(128)} %get-tuple-element.51.near_row, s32[26]{0:T(128)} %get-tuple-element.52.near_col, f32[64,256]{1,0:T(8,128)S(1)} %get-tuple-element.53.matrix, ...), custom_call_target="tpu_custom_call" | custom-call | tf_op jit(solution)/shard_map/cond/branch_1_fun/pallas_call | solution.py:304
  26.3 0.6 %collective-permute-start = (f32[320,256]{1,0:T(8,128)S(1)}, f32[320,256]{1,0:T(8,128)S(1)}, u32[]{:S(2)}, u32[]{:S(2)}) collective-permute-start(f32[320,256]{1,0:T(8,128)S(1)} %get-tuple-element.59), channel_id=1, source_target_pairs={{0,1},{1,0},{2,3},{3,2},{4,5},{5,4},{6,7},{7,6},{8,9},{9,8},{10,11... | collective-permute-start | bytes 983048 | tf_op jit(solution)/shard_map/cond/branch_1_fun/ppermute | solution.py:427
  26.8 1.7 %branch_1_fun.9 = f32[2,256,256]{2,1,0:T(8,128)S(1)} custom-call(s32[26]{0:T(128)S(1)} %get-tuple-element.62.near_row, s32[26]{0:T(128)S(1)} %get-tuple-element.63.near_col, bf16[26,512,256]{2,1,0:T(8,128)(2,1)S(1)} %get-tuple-element.64.block, bf16[8,256,256]{2,1,0:T(8,128)(2,1)S(1)} %get-tuple-element.65.full), custom_call_target="tpu_custom_call" | custom-call | tf_op jit(solution)/shard_map/cond/branch_1_fun/pallas_call | solution.py:364
  28.6 1.6 %collective-permute-start.12 = (bf16[320,256]{1,0:T(8,128)(2,1)S(1)}, bf16[320,256]{1,0:T(8,128)(2,1)S(1)}, u32[]{:S(2)}, u32[]{:S(2)}) collective-permute-start(bf16[320,256]{1,0:T(8,128)(2,1)S(1)} %get-tuple-element.105), channel_id=1, source_target_pairs={{0,2},{2,0},{1,3},{3,1},{4,6},{6,4},{5,7},{7,5},{8,10},{10,8},{9,1... | collective-permute-start | bytes 491528 | tf_op jit(solution)/shard_map/ppermute | solution.py:427
  30.2 2.7 %collective-permute-done.8.refs_3_ = bf16[1,288,256]{2,1,0:T(8,128)(2,1)S(1)} collective-permute-done((bf16[1,288,256]{2,1,0:T(8,128)(2,1)S(1)}, bf16[1,288,256]{2,1,0:T(8,128)(2,1)S(1)}, u32[]{:S(2)}, u32[]{:S(2)}) %collective-permute-start.8) | collective-permute-done | bytes 147488 | tf_op jit(solution)/shard_map/ppermute | solution.py:506
  33.0 1.5 %collective-permute-start.9 = (bf16[3,288,256]{2,1,0:T(8,128)(2,1)S(1)}, bf16[3,288,256]{2,1,0:T(8,128)(2,1)S(1)}, u32[]{:S(2)}, u32[]{:S(2)}) collective-permute-start(bf16[3,288,256]{2,1,0:T(8,128)(2,1)S(1)} %pad_maximum_fusion), channel_id=1, source_target_pairs={{0,1},{1,0},{2,3},{3,2},{4,5},{5,4},{6,7},{7,6},{8,9},{9,8},{10,11... | collective-permute-start | bytes 1327112 | tf_op jit(solution)/shard_map/ppermute | solution.py:427
  34.4 0.4 collective-permute-done.12.refs_9_
  34.8 0.1 collective-permute-start.14
  34.9 0.9 %collective-permute-done.9 = bf16[3,288,256]{2,1,0:T(8,128)(2,1)S(1)} collective-permute-done((bf16[3,288,256]{2,1,0:T(8,128)(2,1)S(1)}, bf16[3,288,256]{2,1,0:T(8,128)(2,1)S(1)}, u32[]{:S(2)}, u32[]{:S(2)}) %collective-permute-start.9) | collective-permute-done | bytes 442400 | tf_op jit(solution)/shard_map/ppermute | solution.py:427
  35.9 0.6 %collective-permute-done.14.refs_10_ = f32[320,256]{1,0:T(8,128)S(1)} collective-permute-done((f32[320,256]{1,0:T(8,128)S(1)}, f32[320,256]{1,0:T(8,128)S(1)}, u32[]{:S(2)}, u32[]{:S(2)}) %collective-permute-start.14) | collective-permute-done | bytes 327712 | tf_op jit(solution)/shard_map/ppermute | solution.py:427
  36.5 1.3 %shard_map.86 = f32[2,256,256]{2,1,0:T(8,128)} custom-call(bf16[2,288,256]{2,1,0:T(8,128)(2,1)S(1)} %get-tuple-element.88.packed, bf16[2,288,256]{2,1,0:T(8,128)(2,1)S(1)} %collective-permute-done.7.refs_0_, bf16[2,288,256]{2,1,0:T(8,128)(2,1)S(1)} %slice.44.refs_1_, f32[1,288,256]{2,1,0:T(8,128)S(1)} %get-tuple-element.98.refs_2_, ...), custom_call_target="tpu_custom_call" | custom-call | tf_op jit(solution)/shard_map/pallas_call | solution.py:413
  (30 shorter events, 0.2 us)
Async XLA Ops:
  1.1 8.7 %collective-permute-start.3 = (bf16[1,288,256]{2,1,0:T(8,128)(2,1)S(1)}, bf16[1,288,256]{2,1,0:T(8,128)(2,1)S(1)}, u32[]{:S(2)}, u32[]{:S(2)}) collective-permute-start(bf16[1,288,256]{2,1,0:T(8,128)(2,1)S(1)} %get-tuple-element.89), channel_id=1, source_target_pairs={{0,2},{2,0},{1,3},{3,1},{4,6},{6,4},{5,7},{7,5},{8,10},{10,8},{9,1... | collective-permute-start | bytes 442376 | tf_op jit(solution)/shard_map/ppermute | solution.py:427
  4.1 15.6 %collective-permute-start.5 = (bf16[1,288,256]{2,1,0:T(8,128)(2,1)S(1)}, bf16[1,288,256]{2,1,0:T(8,128)(2,1)S(1)}, u32[]{:S(2)}, u32[]{:S(2)}) collective-permute-start(bf16[1,288,256]{2,1,0:T(8,128)(2,1)S(1)} %get-tuple-element.89), channel_id=1, source_target_pairs={{0,12},{4,8},{8,4},{12,0},{1,13},{5,9},{9,5},{13,1},{2,14},{6,10},... | collective-permute-start | bytes 442376 | tf_op jit(solution)/shard_map/ppermute | solution.py:453
  7.8 12.0 %collective-permute-start.4 = (bf16[1,288,256]{2,1,0:T(8,128)(2,1)S(1)}, bf16[1,288,256]{2,1,0:T(8,128)(2,1)S(1)}, u32[]{:S(2)}, u32[]{:S(2)}) collective-permute-start(bf16[1,288,256]{2,1,0:T(8,128)(2,1)S(1)} %get-tuple-element.119), channel_id=1, source_target_pairs={{0,4},{1,9},{2,6},{3,11},{4,0},{5,13},{6,2},{7,15},{8,12},{9,1},{1... | collective-permute-start | bytes 442376 | tf_op jit(solution)/shard_map/ppermute | solution.py:452
  7.8 12.0 %collective-permute-start.6 = (bf16[1,288,256]{2,1,0:T(8,128)(2,1)S(1)}, bf16[1,288,256]{2,1,0:T(8,128)(2,1)S(1)}, u32[]{:S(2)}, u32[]{:S(2)}) collective-permute-start(bf16[1,288,256]{2,1,0:T(8,128)(2,1)S(1)} %get-tuple-element.118), channel_id=1, source_target_pairs={{0,4},{1,9},{2,6},{3,11},{4,0},{5,13},{6,2},{7,15},{8,12},{9,1},{1... | collective-permute-start | bytes 442376 | tf_op jit(solution)/shard_map/ppermute | solution.py:452
  9.9 3.3 %collective-permute-start.1 = (bf16[1,288,256]{2,1,0:T(8,128)(2,1)S(1)}, bf16[1,288,256]{2,1,0:T(8,128)(2,1)S(1)}, u32[]{:S(2)}, u32[]{:S(2)}) collective-permute-start(bf16[1,288,256]{2,1,0:T(8,128)(2,1)S(1)} %get-tuple-element.50.refs_1_), channel_id=1, source_target_pairs={{0,1},{1,0},{2,3},{3,2},{4,5},{5,4},{6,7},{7,6},{8,9},{9,8},{10,11... | collective-permute-start | bytes 442376 | tf_op jit(solution)/shard_map/cond/branch_1_fun/ppermute | solution.py:427
  13.1 3.2 %copy-start = (f32[64,256]{1,0:T(8,128)}, f32[64,256]{1,0:T(8,128)S(1)}, u32[]{:S(2)}) copy-start(f32[64,256]{1,0:T(8,128)S(1)} %get-tuple-element.129.matrix) | copy-start | bytes 196612 | tf_op jit(solution)/shard_map/cond
  13.2 3.2 %copy-start.2 = (s32[26]{0:T(128)}, s32[26]{0:T(128)S(1)}, u32[]{:S(2)}) copy-start(s32[26]{0:T(128)S(1)} %get-tuple-element.130.near_row) | copy-start | bytes 316 | tf_op jit(solution)/shard_map/cond
  13.2 3.2 %copy-start.4 = (s32[26]{0:T(128)}, s32[26]{0:T(128)S(1)}, u32[]{:S(2)}) copy-start(s32[26]{0:T(128)S(1)} %get-tuple-element.131.near_col) | copy-start | bytes 316 | tf_op jit(solution)/shard_map/cond
  16.5 3.3 %copy-start.1 = (f32[64,256]{1,0:T(8,128)S(1)}, f32[64,256]{1,0:T(8,128)}, u32[]{:S(2)}) copy-start(f32[64,256]{1,0:T(8,128)} %copy-done) | copy-start | bytes 196612 | tf_op jit(solution)/shard_map/cond
  16.5 3.3 %copy-start.3 = (s32[26]{0:T(128)S(1)}, s32[26]{0:T(128)}, u32[]{:S(2)}) copy-start(s32[26]{0:T(128)} %copy-done.2) | copy-start | bytes 316 | tf_op jit(solution)/shard_map/cond
  16.5 3.3 %copy-start.5 = (s32[26]{0:T(128)S(1)}, s32[26]{0:T(128)}, u32[]{:S(2)}) copy-start(s32[26]{0:T(128)} %copy-done.4) | copy-start | bytes 316 | tf_op jit(solution)/shard_map/cond
  16.5 3.0 %collective-permute-start.2 = (f32[4,288,256]{2,1,0:T(8,128)S(1)}, f32[4,288,256]{2,1,0:T(8,128)S(1)}, u32[]{:S(2)}, u32[]{:S(2)}) collective-permute-start(f32[4,288,256]{2,1,0:T(8,128)S(1)} %slice.38), channel_id=1, source_target_pairs={{0,1},{1,0},{2,3},{3,2},{4,5},{5,4},{6,7},{7,6},{8,9},{9,8},{10,11... | collective-permute-start | bytes 3538952 | tf_op jit(solution)/shard_map/cond/branch_1_fun/ppermute | solution.py:427
  19.9 2.8 %collective-permute-start.11 = (bf16[3,288,256]{2,1,0:T(8,128)(2,1)S(1)}, bf16[3,288,256]{2,1,0:T(8,128)(2,1)S(1)}, u32[]{:S(2)}, u32[]{:S(2)}) collective-permute-start(bf16[3,288,256]{2,1,0:T(8,128)(2,1)S(1)} %constant_dynamic-update-slice_fusion), channel_id=1, source_target_pairs={{0,1},{1,0},{2,3},{3,2},{4,5},{5,4},{6,7},{7,6},{8,9},{9,8},{10,11... | collective-permute-start | bytes 1327112 | tf_op jit(solution)/shard_map/ppermute | solution.py:427
  20.3 12.6 %collective-permute-start.7 = (bf16[2,288,256]{2,1,0:T(8,128)(2,1)S(1)}, bf16[2,288,256]{2,1,0:T(8,128)(2,1)S(1)}, u32[]{:S(2)}, u32[]{:S(2)}) collective-permute-start(bf16[2,288,256]{2,1,0:T(8,128)(2,1)S(1)} %get-tuple-element.96), channel_id=1, source_target_pairs={{0,4},{1,9},{2,6},{3,11},{4,0},{5,13},{6,2},{7,15},{8,12},{9,1},{1... | collective-permute-start | bytes 884744 | tf_op jit(solution)/shard_map/ppermute | solution.py:505
  20.4 12.5 %collective-permute-start.8 = (bf16[1,288,256]{2,1,0:T(8,128)(2,1)S(1)}, bf16[1,288,256]{2,1,0:T(8,128)(2,1)S(1)}, u32[]{:S(2)}, u32[]{:S(2)}) collective-permute-start(bf16[1,288,256]{2,1,0:T(8,128)(2,1)S(1)} %get-tuple-element.97), channel_id=1, source_target_pairs={{0,12},{4,8},{8,4},{12,0},{1,13},{5,9},{9,5},{13,1},{2,14},{6,10},... | collective-permute-start | bytes 442376 | tf_op jit(solution)/shard_map/ppermute | solution.py:506
  22.7 11.7 %collective-permute-start.10 = (f32[1,288,256]{2,1,0:T(8,128)S(1)}, f32[1,288,256]{2,1,0:T(8,128)S(1)}, u32[]{:S(2)}, u32[]{:S(2)}) collective-permute-start(f32[1,288,256]{2,1,0:T(8,128)S(1)} %get-tuple-element.98.refs_2_), channel_id=1, source_target_pairs={{0,1},{1,0},{2,3},{3,2},{4,5},{5,4},{6,7},{7,6},{8,9},{9,8},{10,11... | collective-permute-start | bytes 884744 | tf_op jit(solution)/shard_map/ppermute | solution.py:427
  26.3 2.3 %collective-permute-start = (f32[320,256]{1,0:T(8,128)S(1)}, f32[320,256]{1,0:T(8,128)S(1)}, u32[]{:S(2)}, u32[]{:S(2)}) collective-permute-start(f32[320,256]{1,0:T(8,128)S(1)} %get-tuple-element.59), channel_id=1, source_target_pairs={{0,1},{1,0},{2,3},{3,2},{4,5},{5,4},{6,7},{7,6},{8,9},{9,8},{10,11... | collective-permute-start | bytes 983048 | tf_op jit(solution)/shard_map/cond/branch_1_fun/ppermute | solution.py:427
  28.6 6.2 %collective-permute-start.12 = (bf16[320,256]{1,0:T(8,128)(2,1)S(1)}, bf16[320,256]{1,0:T(8,128)(2,1)S(1)}, u32[]{:S(2)}, u32[]{:S(2)}) collective-permute-start(bf16[320,256]{1,0:T(8,128)(2,1)S(1)} %get-tuple-element.105), channel_id=1, source_target_pairs={{0,2},{2,0},{1,3},{3,1},{4,6},{6,4},{5,7},{7,5},{8,10},{10,8},{9,1... | collective-permute-start | bytes 491528 | tf_op jit(solution)/shard_map/ppermute | solution.py:427
  30.2 6.4 %collective-permute-start.13 = (f32[2,256,256]{2,1,0:T(8,128)S(1)}, f32[2,256,256]{2,1,0:T(8,128)S(1)}, u32[]{:S(2)}, u32[]{:S(2)}) collective-permute-start(f32[2,256,256]{2,1,0:T(8,128)S(1)} %get-tuple-element.107.refs_6_), channel_id=1, source_target_pairs={{0,1},{1,0},{2,3},{3,2},{4,5},{5,4},{6,7},{7,6},{8,9},{9,8},{10,11... | collective-permute-start | bytes 1572872 | tf_op jit(solution)/shard_map/ppermute | solution.py:427
  33.0 2.9 %collective-permute-start.9 = (bf16[3,288,256]{2,1,0:T(8,128)(2,1)S(1)}, bf16[3,288,256]{2,1,0:T(8,128)(2,1)S(1)}, u32[]{:S(2)}, u32[]{:S(2)}) collective-permute-start(bf16[3,288,256]{2,1,0:T(8,128)(2,1)S(1)} %pad_maximum_fusion), channel_id=1, source_target_pairs={{0,1},{1,0},{2,3},{3,2},{4,5},{5,4},{6,7},{7,6},{8,9},{9,8},{10,11... | collective-permute-start | bytes 1327112 | tf_op jit(solution)/shard_map/ppermute | solution.py:427
  34.8 1.7 %collective-permute-start.14 = (f32[320,256]{1,0:T(8,128)S(1)}, f32[320,256]{1,0:T(8,128)S(1)}, u32[]{:S(2)}, u32[]{:S(2)}) collective-permute-start(f32[320,256]{1,0:T(8,128)S(1)} %convert_element_type.14), channel_id=1, source_target_pairs={{0,1},{1,0},{2,3},{3,2},{4,5},{5,4},{6,7},{7,6},{8,9},{9,8},{10,11... | collective-permute-start | bytes 983048 | tf_op jit(solution)/shard_map/ppermute | solution.py:427
